TPU v7x, 512 devices: a whole 4x8x8 slice. The times are simulated.
512 devices in a mesh: img: 32 (over x, y), ref: 16 (over z, core).
Axes of the slice: x: 4, y: 8, z: 8, core: 2. Of those that a mesh axis runs over, the one named last changes fastest.
Arguments:
- images: bfloat16 [32768, 2048], P('img'), may hold values from -8 to 8
- references: bfloat16 [8192, 2048], P('ref'), may hold values from -1 to 1
- initial_contrast: float32 [32768], P('img'), may hold values from 0.25 to 1.75
Outputs:
- new_references: bfloat16 [8192, 2048], P('ref')
- contrast: float32 [32768], P('img')
- loglik: float32 [32768], P('img')
All inputs are finite; a program needn't handle non-finite values.
Results may differ from a plain program's by a relative error of at most 0.0041.
Values may be sent and summed in bfloat16 or wider, within the bound.
No kernel may reach another device: no remote copies, remote signals or barrier semaphores. Data moves between devices by JAX's collectives and lax.ppermute only.
A program may use at most 64 MiB of HBM per device.

v0:
```python
import math

import jax
import jax.numpy as jnp
from jax import lax
from jax.sharding import PartitionSpec as P

ITERS = 3


sharpness = 2.0
prior_weight = 1.0
epsilon = 1e-06


def sent_to_all(value, axis):
    devices = lax.axis_size(axis)
    return lax.all_to_all(
        jnp.broadcast_to(value[None], (devices, *value.shape)), axis, 0, 0, tiled=True
    )


def over_copies(value, axis):
    everything = sent_to_all(value, axis)
    return jnp.max(everything, axis=0)


def taken_together(value, axis):
    everything = sent_to_all(value, axis)
    return jnp.sum(everything, axis=0)


def together(arrays, axis):
    vector, at, finished = (jnp.concatenate([a.reshape(-1) for a in arrays]), 0, [])
    so_far = taken_together(vector, axis)
    for a in arrays:
        finished.append(so_far[at : at + a.size].reshape(a.shape))
        at += a.size
    return tuple(finished)


def scores_of(cross_terms, ref_norms, contrast):
    contrast_col = contrast[:, None]
    return sharpness * (
        contrast_col * cross_terms - 0.5 * (contrast_col * contrast_col) * ref_norms[None, :]
    )


def statistics(cross_terms, ref_norms, contrast):
    scored = scores_of(cross_terms, ref_norms, contrast)
    highest = over_copies(jnp.max(scored, axis=1), "ref")
    exponent = jnp.exp(scored - highest[:, None])
    summed, weighted_cross, weighted_norm = together(
        (
            jnp.sum(exponent, axis=1),
            jnp.sum(exponent * cross_terms, axis=1),
            jnp.sum(exponent * ref_norms[None, :], axis=1),
        ),
        "ref",
    )
    return (highest, summed, weighted_cross, weighted_norm, exponent)


def normalize(sums):
    meansq = jnp.mean(sums * sums, axis=1)
    return (sums * lax.rsqrt(meansq + epsilon)[:, None]).astype(jnp.bfloat16)


def per_device(images, references, initial_contrast):
    ref_norms = jnp.sum(jnp.square(references.astype(jnp.float32)), axis=1)
    cross_terms = lax.dot_general(
        images, references, (((1,), (1,)), ((), ())), preferred_element_type=jnp.float32
    )
    contrast = initial_contrast
    for iteration in range(ITERS + 1):
        highest, summed, weighted_cross, weighted_norm, exponent = statistics(
            cross_terms, ref_norms, contrast
        )
        if iteration < ITERS:
            contrast = (weighted_cross / summed + prior_weight * initial_contrast) / (
                weighted_norm / summed + prior_weight
            )
    posterior = exponent / summed[:, None]
    weights = (posterior * contrast[:, None]).astype(jnp.bfloat16)
    img_partial = lax.dot_general(
        weights, images, (((0,), (0,)), ((), ())), preferred_element_type=jnp.float32
    )
    gathered = normalize(lax.psum(img_partial, "img"))
    width = images.shape[1]
    new_norms = jnp.sum(jnp.square(gathered.astype(jnp.float32)), axis=1) / width
    new_cross = lax.dot_general(
        images, gathered, (((1,), (1,)), ((), ())), preferred_element_type=jnp.float32
    ) * width ** (-0.5)
    final_high, final_sum, final_cross, final_norm, final_exp = statistics(
        new_cross, new_norms, contrast
    )
    loglik = final_high + jnp.log(final_sum) - math.log(gathered.shape[0] * lax.axis_size("ref"))
    return (gathered, contrast, loglik)


def solution(mesh):
    placed = (P("img", None), P("ref", None), P("img"))
    return jax.shard_map(
        per_device,
        mesh=mesh,
        in_specs=placed,
        out_specs=(P("ref", None), P("img"), P("img")),
        check_vma=False,
    )
```

profile of v0, /device:TPU:1, one launch (start us, length us, event | category | flops | bytes accessed | tf_op | source)
XLA Modules:
  0.0 348.5 jit_solution(8609487402731776584)
XLA Ops:
  7.2 2.2 multiply_reduce_fusion.2
  9.5 4.7 %fusion.2 = (f32[1024]{0:T(1024)S(1)}, f32[1024,512]{0,1:T(8,128)S(1)}) fusion(f32[512]{0:T(512)S(1)} %multiply_reduce_fusion.2, f32[1024]{0:T(1024)S(1)} %multiply_multiply_fusion.3, f32[1024]{0:T(1024)S(1)} %copy-done.3, bf16[1024,2048]{1,0:T(8,128)(2,1)} %param.3, bf16[512,2048]{1,0:T(8,128)(2,1)S(1)} %copy-done.1), kind=kOutput, calls=%fused_computation.27 | convolution fusion | flops 2150104064 | bytes 8402944 | tf_op jit(solution)/shard_map/dot_general | solution.py:71
  14.2 19.4 %all_to_all.60 = f32[16,1,1024]{2,1,0:T(1,128)S(1)} all-to-all(f32[16,1,1024]{2,1,0:T(1,128)S(1)} %broadcast_in_dim.20), channel_id=1, replica_groups=mesh['img'=32,'ref'=16] {'ref'}, dimensions={0} | all-to-all | bytes 131072 | tf_op jit(solution)/shard_map/all_to_all | solution.py:18
  33.7 1.0 fusion.3
  34.8 13.0 %all_to_all.61 = f32[16,1,3072]{2,1,0:T(1,128)S(1)} all-to-all(f32[16,1,3072]{2,1,0:T(1,128)S(1)} %broadcast_in_dim.21), channel_id=1, replica_groups=mesh['img'=32,'ref'=16] {'ref'}, dimensions={0} | all-to-all | bytes 393216 | tf_op jit(solution)/shard_map/all_to_all | solution.py:18
  48.4 10.5 %all_to_all.62 = f32[16,1,1024]{2,1,0:T(1,128)S(1)} all-to-all(f32[16,1,1024]{2,1,0:T(1,128)S(1)} %broadcast_in_dim.22), channel_id=1, replica_groups=mesh['img'=32,'ref'=16] {'ref'}, dimensions={0} | all-to-all | bytes 131072 | tf_op jit(solution)/shard_map/all_to_all | solution.py:18
  58.9 1.0 fusion.5
  60.0 13.0 %all_to_all.63 = f32[16,1,3072]{2,1,0:T(1,128)S(1)} all-to-all(f32[16,1,3072]{2,1,0:T(1,128)S(1)} %broadcast_in_dim.23), channel_id=1, replica_groups=mesh['img'=32,'ref'=16] {'ref'}, dimensions={0} | all-to-all | bytes 393216 | tf_op jit(solution)/shard_map/all_to_all | solution.py:18
  73.5 10.5 %all_to_all.64 = f32[16,1,1024]{2,1,0:T(1,128)S(1)} all-to-all(f32[16,1,1024]{2,1,0:T(1,128)S(1)} %broadcast_in_dim.24), channel_id=1, replica_groups=mesh['img'=32,'ref'=16] {'ref'}, dimensions={0} | all-to-all | bytes 131072 | tf_op jit(solution)/shard_map/all_to_all | solution.py:18
  84.0 1.0 fusion.7
  85.1 13.0 %all_to_all.65 = f32[16,1,3072]{2,1,0:T(1,128)S(1)} all-to-all(f32[16,1,3072]{2,1,0:T(1,128)S(1)} %broadcast_in_dim.25), channel_id=1, replica_groups=mesh['img'=32,'ref'=16] {'ref'}, dimensions={0} | all-to-all | bytes 393216 | tf_op jit(solution)/shard_map/all_to_all | solution.py:18
  98.7 10.5 %all_to_all.66 = f32[16,1,1024]{2,1,0:T(1,128)S(1)} all-to-all(f32[16,1,1024]{2,1,0:T(1,128)S(1)} %broadcast_in_dim.26), channel_id=1, replica_groups=mesh['img'=32,'ref'=16] {'ref'}, dimensions={0} | all-to-all | bytes 131072 | tf_op jit(solution)/shard_map/all_to_all | solution.py:18
  109.2 1.0 fusion.25
  110.3 12.9 %all_to_all.67 = f32[16,1,3072]{2,1,0:T(1,128)S(1)} all-to-all(f32[16,1,3072]{2,1,0:T(1,128)S(1)} %broadcast_in_dim.27), channel_id=1, replica_groups=mesh['img'=32,'ref'=16] {'ref'}, dimensions={0} | all-to-all | bytes 393216 | tf_op jit(solution)/shard_map/all_to_all | solution.py:18
  123.4 6.8 %fusion.11 = f32[512,2048]{1,0:T(8,128)} fusion(bf16[1024,2048]{1,0:T(8,128)(2,1)} %param.3, f32[1024]{0:T(1024)S(1)} %slice.53, f32[1024]{0:T(1024)S(1)} %get-tuple-element.19, f32[1024,512]{0,1:T(8,128)S(1)} %get-tuple-element.27, f32[1024]{0:T(1024)S(1)} %reduce_max.97, f32[1024]{0:T(1024)S(1)} %multiply_multiply_fusion, f32[512]{0:T(512)S(1)} %multiply_reduce_fusion.2), kind=kOutput, calls=%fused_computation.36 | convolution fusion | flops 2151677952 | bytes 10504192 | tf_op jit(solution)/shard_map/dot_general | solution.py:85
  130.2 169.0 %all-reduce.2.cloned.1.call-done = f32[512,2048]{1,0:T(8,128)} async-done(((f32[512,2048]{1,0:T(8,128)}), f32[512,2048]{1,0:T(8,128)}) %all-reduce.2.cloned.1.call-update) | async-done | bytes 4194320 | tf_op jit(solution)/shard_map/psum | solution.py:88
  299.2 2.7 multiply_reduce_fusion.1
  301.9 0.8 copy-done
  302.6 0.6 multiply_reduce_fusion
  303.3 2.3 copy-done.5
  305.6 2.5 fusion.10
  308.1 18.6 %all_to_all.68 = f32[16,1,1024]{2,1,0:T(1,128)S(1)} all-to-all(f32[16,1,1024]{2,1,0:T(1,128)S(1)} %broadcast_in_dim.28), channel_id=1, replica_groups=mesh['img'=32,'ref'=16] {'ref'}, dimensions={0} | all-to-all | bytes 131072 | tf_op jit(solution)/shard_map/all_to_all | solution.py:18
  326.8 1.0 fusion.9
  327.9 13.0 %all_to_all.69 = f32[16,1,3072]{2,1,0:T(1,128)S(1)} all-to-all(f32[16,1,3072]{2,1,0:T(1,128)S(1)} %broadcast_in_dim.29), channel_id=1, replica_groups=mesh['img'=32,'ref'=16] {'ref'}, dimensions={0} | all-to-all | bytes 393216 | tf_op jit(solution)/shard_map/all_to_all | solution.py:18
  (49 shorter events, 3.6 us)
Async XLA Ops:
  7.2 2.3 copy-start.3
  7.2 292.0 %all-reduce.2.cloned.1.call-start = ((), (), s32[]{:S(2)}) async-start(), calls=%async_computation.10 | async-start | bytes 8388608 | tf_op jit(solution)/shard_map/psum | solution.py:88
  7.2 2.3 copy-start.1
  98.2 25.2 %copy-start.4 = (f32[1024]{0:T(1024)}, f32[1024]{0:T(1024)S(1)}, u32[]{:S(2)}) copy-start(f32[1024]{0:T(1024)S(1)} %get-tuple-element.19) | copy-start | bytes 12292
  299.2 3.4 copy-start
  302.6 2.9 copy-start.5
  303.2 4.8 %copy-start.2 = (bf16[512,2048]{1,0:T(8,128)(2,1)}, bf16[512,2048]{1,0:T(8,128)(2,1)S(1)}, u32[]{:S(2)}) copy-start(bf16[512,2048]{1,0:T(8,128)(2,1)S(1)} %get-tuple-element.21) | copy-start | bytes 6291460
Sparse Core Ops, SparseCore 0:
  130.3 168.7 all-reduce.1
where the time goes:
time: 349 us; the launch traced here: 348 us
  waiting for transfers between devices  169 us (48%)
  blocking collectives  134 us (38%)
  between operations  14.4 us (4%)
  matrix products  14 us (4%)
  other arithmetic  13.2 us (4%)
  local copies, waits for them, and re-layouts  3.77 us (1%)
    psum x1, waiting for transfers between devices, per_device(): gathered = normalize(lax.psum(img_partial, 'img'))  169 us
    all_to_all x10, blocking collectives, sent_to_all(): lax.all_to_all(jnp.broadcast_to(value[None], (devices, *value.shape)), ax...  134 us
  transfers between devices with their start and end apart: 1, of which 1 were waited for; matrix products, arithmetic and copies ran while one was open for 0% of the time, Pallas kernels for 0%

commit v1 on v0

v1 whole, which is shorter than its diff:
```python
import math

import jax
import jax.numpy as jnp
from jax import lax
from jax.sharding import PartitionSpec as P

ITERS = 3


sharpness = 2.0
prior_weight = 1.0
epsilon = 1e-06


def sent_to_all(value, axis):
    devices = lax.axis_size(axis)
    return lax.all_to_all(
        jnp.broadcast_to(value[None], (devices, *value.shape)), axis, 0, 0, tiled=True
    )


def scores_of(cross_terms, ref_norms, contrast):
    contrast_col = contrast[:, None]
    return sharpness * (
        contrast_col * cross_terms - 0.5 * (contrast_col * contrast_col) * ref_norms[None, :]
    )


def statistics(cross_terms, ref_norms, contrast, weighted=True):
    scored = scores_of(cross_terms, ref_norms, contrast)
    own_high = jnp.max(scored, axis=1)
    exponent = jnp.exp(scored - own_high[:, None])
    rows = [own_high, jnp.sum(exponent, axis=1)]
    if weighted:
        rows.append(jnp.sum(exponent * cross_terms, axis=1))
        rows.append(jnp.sum(exponent * ref_norms[None, :], axis=1))
    everything = sent_to_all(jnp.stack(rows), "ref")
    highest = jnp.max(everything[:, 0], axis=0)
    scale = jnp.exp(everything[:, 0] - highest[None])
    sums = jnp.sum(everything[:, 1:] * scale[:, None], axis=0)
    return highest, sums, exponent, jnp.exp(own_high - highest)


def normalize(sums):
    meansq = jnp.mean(sums * sums, axis=1)
    return (sums * lax.rsqrt(meansq + epsilon)[:, None]).astype(jnp.bfloat16)


def per_device(images, references, initial_contrast):
    ref_norms = jnp.sum(jnp.square(references.astype(jnp.float32)), axis=1)
    cross_terms = lax.dot_general(
        images, references, (((1,), (1,)), ((), ())), preferred_element_type=jnp.float32
    )
    contrast = initial_contrast
    for _ in range(ITERS):
        _, (summed, along, weight), _, _ = statistics(cross_terms, ref_norms, contrast)
        contrast = (along / summed + prior_weight * initial_contrast) / (
            weight / summed + prior_weight
        )
    _, (summed,), exponent, scale = statistics(cross_terms, ref_norms, contrast, False)
    weights = (exponent * (scale / summed * contrast)[:, None]).astype(jnp.bfloat16)
    img_partial = lax.dot_general(
        weights, images, (((0,), (0,)), ((), ())), preferred_element_type=jnp.float32
    )
    size = lax.axis_size("img")
    refs, width = img_partial.shape
    pieces = img_partial.astype(jnp.bfloat16).reshape(size, refs // size, width)
    pieces = lax.all_to_all(pieces, "img", 0, 0, tiled=True)
    mine = normalize(jnp.sum(pieces.astype(jnp.float32), axis=0))
    gathered = sent_to_all(mine, "img").reshape(refs, width)
    new_norms = jnp.sum(jnp.square(gathered.astype(jnp.float32)), axis=1) / width
    new_cross = lax.dot_general(
        images, gathered, (((1,), (1,)), ((), ())), preferred_element_type=jnp.float32
    ) * width ** (-0.5)
    final_high, (final_sum,), _, _ = statistics(new_cross, new_norms, contrast, False)
    loglik = final_high + jnp.log(final_sum) - math.log(refs * lax.axis_size("ref"))
    return (gathered, contrast, loglik)


def solution(mesh):
    placed = (P("img", None), P("ref", None), P("img"))
    return jax.shard_map(
        per_device,
        mesh=mesh,
        in_specs=placed,
        out_specs=(P("ref", None), P("img"), P("img")),
        check_vma=False,
    )
```

time: 349 us -> 220 us (0.63)
  waiting for transfers between devices: 169 us -> 0 us
  blocking collectives: 134 us -> 193 us
  between operations: 14.4 us -> 0.95 us
    psum x1 -> x0, waiting for transfers between devices: 169 us -> none  [per_device(): gathered = normalize(lax.psum(img_partial, 'img'))]
    all_to_all x0 -> x1, blocking collectives: none -> 59.4 us  [per_device(): pieces = lax.all_to_all(pieces, 'img', 0, 0, tiled=True)]
    dot_general x1, matrix products: 6.79 us -> 2.63 us  [per_device(): lax.dot_general(weights, images, (((0,), (0,)), ((), ())), preferred_elem...]
    all_to_all x10 -> x6, blocking collectives: 134 us -> 134 us  [sent_to_all(): lax.all_to_all(jnp.broadcast_to(value[None], (devices, *value.shape)), ax...]
  transfers between devices with their start and end apart: 1 -> 0, of which waited for: 1 -> 0; matrix products, arithmetic and copies ran while one was open for 0% -> 0% of each run, Pallas kernels for 0% -> 0%
where the time goes in v1:
time: 220 us; the launch traced here: 219 us
  blocking collectives  193 us (88%)
  matrix products  12 us (5%)
  other arithmetic  10.9 us (5%)
    all_to_all x6, blocking collectives, sent_to_all(): lax.all_to_all(jnp.broadcast_to(value[None], (devices, *value.shape)), ax...  134 us
    all_to_all x1, blocking collectives, per_device(): pieces = lax.all_to_all(pieces, 'img', 0, 0, tiled=True)  59.4 us
    dot_general x1, matrix products, per_device(): lax.dot_general(images, references, (((1,), (1,)), ((), ())), preferred_e...  4.69 us
    dot_general x1, matrix products, per_device(): lax.dot_general(images, gathered, (((1,), (1,)), ((), ())), preferred_ele...  4.67 us

profile of v1, /device:TPU:1, one launch (start us, length us, event | category | flops | bytes accessed | tf_op | source)
XLA Modules:
  0.0 219.2 jit_solution(17102809376016276069)
XLA Ops:
  0.7 2.2 %multiply_reduce_fusion.1 = f32[512]{0:T(512)S(1)} fusion(bf16[512,2048]{1,0:T(8,128)(2,1)} %param.4), kind=kLoop, calls=%fused_computation.2 | loop fusion | flops 3145216 | bytes 2099200 | tf_op jit(solution)/shard_map/reduce_sum | solution.py:51
  2.9 0.7 multiply_multiply_fusion.3
  3.6 4.7 %fusion.2 = (f32[1024]{0:T(1024)S(1)}, f32[1024,512]{0,1:T(8,128)S(1)}) fusion(f32[512]{0:T(512)S(1)} %multiply_reduce_fusion.1, f32[1024]{0:T(1024)S(1)} %multiply_multiply_fusion.3, f32[1024]{0:T(1024)S(1)} %copy-done.2, bf16[1024,2048]{1,0:T(8,128)(2,1)} %param.3, bf16[512,2048]{1,0:T(8,128)(2,1)S(1)} %copy-done), kind=kOutput, calls=%fused_computation.23 | convolution fusion | flops 2150104064 | bytes 8402944 | tf_op jit(solution)/shard_map/dot_general | solution.py:52
  8.3 1.0 fusion.3
  9.3 23.3 %all_to_all.35 = f32[16,4,1024]{2,1,0:T(4,128)S(1)} all-to-all(f32[16,4,1024]{2,1,0:T(4,128)S(1)} %broadcast_in_dim.12), channel_id=1, replica_groups=mesh['img'=32,'ref'=16] {'ref'}, dimensions={0} | all-to-all | bytes 524288 | tf_op jit(solution)/shard_map/all_to_all | solution.py:18
  33.0 0.4 fusion.4
  33.4 1.0 fusion.5
  34.5 14.4 %all_to_all.36 = f32[16,4,1024]{2,1,0:T(4,128)S(1)} all-to-all(f32[16,4,1024]{2,1,0:T(4,128)S(1)} %broadcast_in_dim.13), channel_id=1, replica_groups=mesh['img'=32,'ref'=16] {'ref'}, dimensions={0} | all-to-all | bytes 524288 | tf_op jit(solution)/shard_map/all_to_all | solution.py:18
  49.2 0.4 fusion.6
  49.6 1.0 fusion.7
  50.7 14.4 %all_to_all.37 = f32[16,4,1024]{2,1,0:T(4,128)S(1)} all-to-all(f32[16,4,1024]{2,1,0:T(4,128)S(1)} %broadcast_in_dim.14), channel_id=1, replica_groups=mesh['img'=32,'ref'=16] {'ref'}, dimensions={0} | all-to-all | bytes 524288 | tf_op jit(solution)/shard_map/all_to_all | solution.py:18
  65.4 0.4 fusion.8
  65.8 0.6 fusion.1
  66.5 12.0 %all_to_all.38 = f32[16,2,1024]{2,1,0:T(2,128)S(1)} all-to-all(f32[16,2,1024]{2,1,0:T(2,128)S(1)} %broadcast_in_dim.15), channel_id=1, replica_groups=mesh['img'=32,'ref'=16] {'ref'}, dimensions={0} | all-to-all | bytes 262144 | tf_op jit(solution)/shard_map/all_to_all | solution.py:18
  78.7 2.6 %convolution_convert_fusion = bf16[512,2048]{1,0:T(8,128)(2,1)S(1)} fusion(bf16[1024,2048]{1,0:T(8,128)(2,1)S(1)} %copy-done.3, f32[1024,512]{0,1:T(8,128)S(1)} %get-tuple-element.31, f32[1024]{0:T(1024)S(1)} %divide_multiply_fusion, f32[1024]{0:T(1024)S(1)} %fusion.8, f32[1024]{0:T(1024)S(1)} %multiply_multiply_fusion, f32[1024]{0:T(1024)S(1)} %get-tuple-element.38, ...), kind=kOutput, calls=%fused_computation.3 | convolution fusion | flops 2152202240 | bytes 8407040 | tf_op jit(solution)/shard_map/dot_general | solution.py:63
  81.3 59.4 %all_to_all.39 = bf16[32,16,2048]{2,1,0:T(8,128)(2,1)S(1)} all-to-all(bf16[32,16,2048]{2,1,0:T(8,128)(2,1)S(1)} %bitcast.44), channel_id=1, replica_groups=mesh['img'=32,'ref'=16] {'img'}, dimensions={0} | all-to-all | bytes 4194304 | tf_op jit(solution)/shard_map/all_to_all | solution.py:69
  140.8 0.3 convert_reduce_fusion
  141.6 53.7 %all_to_all.40 = bf16[32,16,2048]{2,1,0:T(8,128)(2,1)S(1)} all-to-all(bf16[32,16,2048]{2,1,0:T(8,128)(2,1)S(1)} %broadcast_in_dim.16), channel_id=1, replica_groups=mesh['img'=32,'ref'=16] {'img'}, dimensions={0} | all-to-all | bytes 4194304 | tf_op jit(solution)/shard_map/all_to_all | solution.py:18
  195.3 0.5 multiply_reduce_fusion
  195.9 4.7 %fusion.27 = (f32[1024]{0:T(1024)S(1)}, f32[1024,512]{0,1:T(8,128)S(1)}) fusion(f32[512]{0:T(512)S(1)} %div.69, f32[1024]{0:T(1024)S(1)} %multiply_multiply_fusion, f32[1024]{0:T(1024)S(1)} %get-tuple-element.12, bf16[512,2048]{1,0:T(8,128)(2,1)S(1)} %bitcast.42, bf16[1024,2048]{1,0:T(8,128)(2,1)} %param.3), kind=kOutput, calls=%fused_computation.91 | convolution fusion | flops 2150104064 | bytes 8402944 | tf_op jit(solution)/shard_map/dot_general | solution.py:73
  200.5 0.3 exponential_reduce_fusion
  200.9 16.1 %all_to_all.41 = f32[16,2,1024]{2,1,0:T(2,128)S(1)} all-to-all(f32[16,2,1024]{2,1,0:T(2,128)S(1)} %broadcast_in_dim.17), channel_id=1, replica_groups=mesh['img'=32,'ref'=16] {'ref'}, dimensions={0} | all-to-all | bytes 262144 | tf_op jit(solution)/shard_map/all_to_all | solution.py:18
  217.2 0.6 add_add_fusion
  217.8 1.3 copy.73
  (48 shorter events, 2.1 us)
Async XLA Ops:
  0.6 2.9 %copy-start = (bf16[512,2048]{1,0:T(8,128)(2,1)S(1)}, bf16[512,2048]{1,0:T(8,128)(2,1)}, u32[]{:S(2)}) copy-start(bf16[512,2048]{1,0:T(8,128)(2,1)} %param.4) | copy-start | bytes 6291460
  0.6 2.9 %copy-start.2 = (f32[1024]{0:T(1024)S(1)}, f32[1024]{0:T(1024)}, u32[]{:S(2)}) copy-start(f32[1024]{0:T(1024)} %param.5) | copy-start | bytes 12292
  65.4 13.3 %copy-start.1 = (f32[1024]{0:T(1024)}, f32[1024]{0:T(1024)S(1)}, u32[]{:S(2)}) copy-start(f32[1024]{0:T(1024)S(1)} %get-tuple-element.38) | copy-start | bytes 12292
  65.4 13.3 %copy-start.3 = (bf16[1024,2048]{1,0:T(8,128)(2,1)S(1)}, bf16[1024,2048]{1,0:T(8,128)(2,1)}, u32[]{:S(2)}) copy-start(bf16[1024,2048]{1,0:T(8,128)(2,1)} %param.3) | copy-start | bytes 12582916

commit v2 on v1

v2 whole, which is shorter than its diff:
```python
import math

import jax
import jax.numpy as jnp
from jax import lax
from jax.sharding import PartitionSpec as P

ITERS = 3


sharpness = 2.0
prior_weight = 1.0
epsilon = 1e-06


X, Y = 4, 8
NEAR = [[x * Y + 2 * pair + side for x in range(X) for side in range(2)] for pair in range(Y // 2)]
FAR = [[x * Y + 2 * pair + side for pair in range(Y // 2)] for x in range(X) for side in range(2)]


def exchanged(pieces, axis, groups=None):
    return lax.all_to_all(pieces, axis, 0, 0, tiled=True, axis_index_groups=groups)


def sent_to_all(value, axis, groups=None):
    devices = len(groups[0]) if groups else lax.axis_size(axis)
    return exchanged(jnp.broadcast_to(value[None], (devices, *value.shape)), axis, groups)


def summed_share(partial):
    rows, width = partial.shape
    for groups in (NEAR, FAR):
        rows //= len(groups[0])
        pieces = partial.astype(jnp.bfloat16).reshape(len(groups[0]), rows, width)
        partial = jnp.sum(exchanged(pieces, "img", groups).astype(jnp.float32), axis=0)
    return partial


def gathered_rows(share):
    for groups in (FAR, NEAR):
        share = sent_to_all(share, "img", groups).reshape(-1, share.shape[-1])
    return share


def scores_of(cross_terms, ref_norms, contrast):
    contrast_col = contrast[:, None]
    return sharpness * (
        contrast_col * cross_terms - 0.5 * (contrast_col * contrast_col) * ref_norms[None, :]
    )


def statistics(cross_terms, ref_norms, contrast, weighted=True):
    scored = scores_of(cross_terms, ref_norms, contrast)
    own_high = jnp.max(scored, axis=1)
    exponent = jnp.exp(scored - own_high[:, None])
    own_sum = jnp.sum(exponent, axis=1)
    own_log = own_high + jnp.log(own_sum)
    if not weighted:
        logs = sent_to_all(own_log[None], "ref")[:, 0]
        highest = jnp.max(logs, axis=0)
        log_total = highest + jnp.log(jnp.sum(jnp.exp(logs - highest[None]), axis=0))
        return log_total, exponent, own_high
    own = jnp.concatenate(
        [
            own_log,
            jnp.sum(exponent * cross_terms, axis=1) / own_sum,
            jnp.sum(exponent * ref_norms[None, :], axis=1) / own_sum,
        ]
    )
    logs, along, weight = jnp.split(sent_to_all(own[None], "ref")[:, 0], 3, axis=1)
    share = jnp.exp(logs - jnp.max(logs, axis=0)[None])
    total = jnp.sum(share, axis=0)
    return jnp.sum(share * along, axis=0) / total, jnp.sum(share * weight, axis=0) / total


def normalize(sums):
    meansq = jnp.mean(sums * sums, axis=1)
    return (sums * lax.rsqrt(meansq + epsilon)[:, None]).astype(jnp.bfloat16)


def per_device(images, references, initial_contrast):
    ref_norms = jnp.sum(jnp.square(references.astype(jnp.float32)), axis=1)
    cross_terms = lax.dot_general(
        images, references, (((1,), (1,)), ((), ())), preferred_element_type=jnp.float32
    )
    contrast = initial_contrast
    for _ in range(ITERS):
        along, weight = statistics(cross_terms, ref_norms, contrast)
        contrast = (along + prior_weight * initial_contrast) / (weight + prior_weight)
    log_total, exponent, own_high = statistics(cross_terms, ref_norms, contrast, False)
    factor = jnp.exp(own_high - log_total) * contrast
    weights = (exponent * factor[:, None]).astype(jnp.bfloat16)
    img_partial = lax.dot_general(
        weights, images, (((0,), (0,)), ((), ())), preferred_element_type=jnp.float32
    )
    gathered = gathered_rows(normalize(summed_share(img_partial)))
    refs, width = gathered.shape
    new_norms = jnp.sum(jnp.square(gathered.astype(jnp.float32)), axis=1) / width
    new_cross = lax.dot_general(
        images, gathered, (((1,), (1,)), ((), ())), preferred_element_type=jnp.float32
    ) * width ** (-0.5)
    log_total, _, _ = statistics(new_cross, new_norms, contrast, False)
    loglik = log_total - math.log(refs * lax.axis_size("ref"))
    return (gathered, contrast, loglik)


def solution(mesh):
    placed = (P("img", None), P("ref", None), P("img"))
    return jax.shard_map(
        per_device,
        mesh=mesh,
        in_specs=placed,
        out_specs=(P("ref", None), P("img"), P("img")),
        check_vma=False,
    )
```

time: 220 us -> 185 us (0.84)
  blocking collectives: 193 us -> 157 us
    all_to_all x7 -> x9, blocking collectives: 193 us -> 157 us  [exchanged(): lax.all_to_all(pieces, axis, 0, 0, tiled=True, axis_index_groups=groups)]
    reduce_sum x11 -> x12, other arithmetic: 4.63 us -> 4.41 us  [the longest x3 2.86 us: statistics(): jnp.sum(exponent * cross_terms, axis=1) / own_sum]
where the time goes in v2:
time: 185 us
  blocking collectives  157 us (85%)
  matrix products  14.1 us (8%)
  other arithmetic  10.1 us (5%)
  local copies, waits for them, and re-layouts  2.18 us (1%)
    all_to_all x9, blocking collectives, exchanged(): lax.all_to_all(pieces, axis, 0, 0, tiled=True, axis_index_groups=groups)  157 us
    dot_general x1, matrix products, per_device(): lax.dot_general(weights, images, (((0,), (0,)), ((), ())), preferred_elem...  4.78 us
    dot_general x1, matrix products, per_device(): lax.dot_general(images, references, (((1,), (1,)), ((), ())), preferred_e...  4.69 us
    dot_general x1, matrix products, per_device(): lax.dot_general(images, gathered, (((1,), (1,)), ((), ())), preferred_ele...  4.67 us

profile of v2, /device:TPU:1, one launch (start us, length us, event | category | flops | bytes accessed | tf_op | source)
XLA Modules:
  0.0 184.6 jit_solution(12762701932585647234)
XLA Ops:
  0.7 2.2 %multiply_reduce_fusion.1 = f32[512]{0:T(512)S(1)} fusion(bf16[512,2048]{1,0:T(8,128)(2,1)} %param.4), kind=kLoop, calls=%fused_computation.1 | loop fusion | flops 3145216 | bytes 2099200 | tf_op jit(solution)/shard_map/reduce_sum | solution.py:82
  2.9 0.7 multiply_multiply_fusion.3
  3.6 4.7 %fusion.2 = (f32[1024]{0:T(1024)S(1)}, f32[1024,512]{0,1:T(8,128)S(1)}) fusion(f32[512]{0:T(512)S(1)} %multiply_reduce_fusion.1, f32[1024]{0:T(1024)S(1)} %multiply_multiply_fusion.3, f32[1024]{0:T(1024)S(1)} %copy-done.2, bf16[1024,2048]{1,0:T(8,128)(2,1)} %param.3, bf16[512,2048]{1,0:T(8,128)(2,1)S(1)} %copy-done), kind=kOutput, calls=%fused_computation.22 | convolution fusion | flops 2150104064 | bytes 8402944 | tf_op jit(solution)/shard_map/dot_general | solution.py:83
  8.3 1.0 multiply_reduce_fusion.7
  9.4 22.0 %all_to_all.45 = f32[16,1,3072]{2,1,0:T(1,128)S(1)} all-to-all(f32[16,1,3072]{2,1,0:T(1,128)S(1)} %broadcast_in_dim.16), channel_id=1, replica_groups=mesh['img'=32,'ref'=16] {'ref'}, dimensions={0} | all-to-all | bytes 393216 | tf_op jit(solution)/shard_map/all_to_all | solution.py:22
  31.4 0.4 fusion.4
  31.9 1.0 multiply_reduce_fusion.5
  33.0 13.0 %all_to_all.46 = f32[16,1,3072]{2,1,0:T(1,128)S(1)} all-to-all(f32[16,1,3072]{2,1,0:T(1,128)S(1)} %broadcast_in_dim.17), channel_id=1, replica_groups=mesh['img'=32,'ref'=16] {'ref'}, dimensions={0} | all-to-all | bytes 393216 | tf_op jit(solution)/shard_map/all_to_all | solution.py:22
  46.1 0.4 fusion.6
  46.5 1.0 multiply_reduce_fusion.3
  47.6 13.0 %all_to_all.47 = f32[16,1,3072]{2,1,0:T(1,128)S(1)} all-to-all(f32[16,1,3072]{2,1,0:T(1,128)S(1)} %broadcast_in_dim.18), channel_id=1, replica_groups=mesh['img'=32,'ref'=16] {'ref'}, dimensions={0} | all-to-all | bytes 393216 | tf_op jit(solution)/shard_map/all_to_all | solution.py:22
  60.8 0.4 fusion.8
  61.2 0.6 fusion.1
  61.9 10.5 %all_to_all.48 = f32[16,1,1024]{2,1,0:T(1,128)S(1)} all-to-all(f32[16,1,1024]{2,1,0:T(1,128)S(1)} %broadcast_in_dim.19), channel_id=1, replica_groups=mesh['img'=32,'ref'=16] {'ref'}, dimensions={0} | all-to-all | bytes 131072 | tf_op jit(solution)/shard_map/all_to_all | solution.py:22
  72.5 4.8 %convolution_convert_fusion = bf16[512,2048]{1,0:T(8,128)(2,1)S(1)} fusion(bf16[1024,2048]{1,0:T(8,128)(2,1)} %param.3, f32[1024,512]{0,1:T(8,128)S(1)} %get-tuple-element.37, f32[1024]{0:T(1024)S(1)} %exponential_multiply_fusion, f32[1024]{0:T(1024)S(1)} %fusion.8, f32[1024]{0:T(1024)S(1)} %multiply_multiply_fusion, f32[1024]{0:T(1024)S(1)} %get-tuple-element.44, ...), kind=kOutput, calls=%fused_computation.2 | convolution fusion | flops 2152202240 | bytes 8407040 | tf_op jit(solution)/shard_map/dot_general | solution.py:93
  77.2 31.4 %all_to_all.49 = bf16[8,64,2048]{2,1,0:T(8,128)(2,1)S(1)} all-to-all(bf16[8,64,2048]{2,1,0:T(8,128)(2,1)S(1)} %bitcast.36), channel_id=1, replica_groups={{0,16,128,144,256,272,384,400},{32,48,160,176,288,304,416,432},{64,80,1..., dimensions={0} | all-to-all | bytes 4194304 | tf_op jit(solution)/shard_map/all_to_all | solution.py:22
  109.1 13.8 %all_to_all.50 = bf16[4,16,2048]{2,1,0:T(8,128)(2,1)S(1)} all-to-all(bf16[4,16,2048]{2,1,0:T(8,128)(2,1)S(1)} %bitcast.43), channel_id=1, replica_groups={{0,32,64,96},{16,48,80,112},{128,160,192,224},{144,176,208,240},{256,28..., dimensions={0} | all-to-all | bytes 524288 | tf_op jit(solution)/shard_map/all_to_all | solution.py:22
  123.2 12.8 %all_to_all.51 = bf16[4,16,2048]{2,1,0:T(8,128)(2,1)S(1)} all-to-all(bf16[4,16,2048]{2,1,0:T(8,128)(2,1)S(1)} %broadcast_in_dim.20), channel_id=1, replica_groups={{0,32,64,96},{16,48,80,112},{128,160,192,224},{144,176,208,240},{256,28..., dimensions={0} | all-to-all | bytes 524288 | tf_op jit(solution)/shard_map/all_to_all | solution.py:22
  136.2 25.4 %all_to_all.52 = bf16[8,64,2048]{2,1,0:T(8,128)(2,1)S(1)} all-to-all(bf16[8,64,2048]{2,1,0:T(8,128)(2,1)S(1)} %broadcast_in_dim.22), channel_id=1, replica_groups={{0,16,128,144,256,272,384,400},{32,48,160,176,288,304,416,432},{64,80,1..., dimensions={0} | all-to-all | bytes 4194304 | tf_op jit(solution)/shard_map/all_to_all | solution.py:22
  161.6 0.5 multiply_reduce_fusion
  162.2 4.7 %fusion.29 = (f32[1024]{0:T(1024)S(1)}, f32[1024,512]{0,1:T(8,128)S(1)}) fusion(f32[512]{0:T(512)S(1)} %div.74, f32[1024]{0:T(1024)S(1)} %multiply_multiply_fusion, f32[1024]{0:T(1024)S(1)} %get-tuple-element.21, bf16[512,2048]{1,0:T(8,128)(2,1)S(1)} %bitcast.34, bf16[1024,2048]{1,0:T(8,128)(2,1)} %param.3), kind=kOutput, calls=%fused_computation.89 | convolution fusion | flops 2150104064 | bytes 8402944 | tf_op jit(solution)/shard_map/dot_general | solution.py:99
  167.3 15.3 %all_to_all.53 = f32[16,1,1024]{2,1,0:T(1,128)S(1)} all-to-all(f32[16,1,1024]{2,1,0:T(1,128)S(1)} %broadcast_in_dim.23), channel_id=1, replica_groups=mesh['img'=32,'ref'=16] {'ref'}, dimensions={0} | all-to-all | bytes 131072 | tf_op jit(solution)/shard_map/all_to_all | solution.py:22
  182.7 0.6 add_add_fusion
  183.3 1.3 copy.24
  (47 shorter events, 2.3 us)
Async XLA Ops:
  0.6 2.9 %copy-start = (bf16[512,2048]{1,0:T(8,128)(2,1)S(1)}, bf16[512,2048]{1,0:T(8,128)(2,1)}, u32[]{:S(2)}) copy-start(bf16[512,2048]{1,0:T(8,128)(2,1)} %param.4) | copy-start | bytes 6291460
  0.6 2.9 %copy-start.2 = (f32[1024]{0:T(1024)S(1)}, f32[1024]{0:T(1024)}, u32[]{:S(2)}) copy-start(f32[1024]{0:T(1024)} %param.5) | copy-start | bytes 12292
  60.7 11.7 %copy-start.1 = (f32[1024]{0:T(1024)}, f32[1024]{0:T(1024)S(1)}, u32[]{:S(2)}) copy-start(f32[1024]{0:T(1024)S(1)} %get-tuple-element.44) | copy-start | bytes 12292

commit v3 on v1

v3 whole, which is shorter than its diff:
```python
import math

import jax
import jax.numpy as jnp
from jax import lax
from jax.sharding import PartitionSpec as P

ITERS = 3


sharpness = 2.0
prior_weight = 1.0
epsilon = 1e-06


X, Y = 4, 8
DISTANCES = (2, 1, 3)
COLUMNS = [[x * Y + y for y in range(Y)] for x in range(X)]


def exchanged(pieces, axis, groups=None):
    return lax.all_to_all(pieces, axis, 0, 0, tiled=True, axis_index_groups=groups)


def sent_to_all(value, axis, groups=None):
    devices = len(groups[0]) if groups else lax.axis_size(axis)
    return exchanged(jnp.broadcast_to(value[None], (devices, *value.shape)), axis, groups)


def along_x(value, distance):
    return lax.ppermute(value, "img", [(i, (i + distance * Y) % (X * Y)) for i in range(X * Y)])


def scores_of(cross_terms, ref_norms, contrast):
    contrast_col = contrast[:, None]
    return sharpness * (
        contrast_col * cross_terms - 0.5 * (contrast_col * contrast_col) * ref_norms[None, :]
    )


def relative(cross_terms, ref_norms, contrast):
    scored = scores_of(cross_terms, ref_norms, contrast)
    own_high = jnp.max(scored, axis=1)
    return jnp.exp(scored - own_high[:, None]), own_high


def refitted(cross_terms, ref_norms, contrast, prior):
    exponent, own_high = relative(cross_terms, ref_norms, contrast)
    upper = jnp.sum(exponent * (cross_terms + prior_weight * prior[:, None]), axis=1)
    lower = jnp.sum(exponent * (ref_norms + prior_weight)[None, :], axis=1)
    own = jnp.concatenate([own_high + jnp.log(lower), upper / lower])
    logs, quotients = jnp.split(sent_to_all(own[None], "ref")[:, 0], 2, axis=1)
    share = jnp.exp(logs - jnp.max(logs, axis=0)[None])
    return jnp.sum(share * quotients, axis=0) / jnp.sum(share, axis=0)


def log_total(own_log):
    logs = sent_to_all(own_log[None], "ref")[:, 0]
    highest = jnp.max(logs, axis=0)
    return highest + jnp.log(jnp.sum(jnp.exp(logs - highest[None]), axis=0))


def normalize(sums):
    meansq = jnp.mean(sums * sums, axis=1)
    return (sums * lax.rsqrt(meansq + epsilon)[:, None]).astype(jnp.bfloat16)


def per_device(images, references, initial_contrast):
    ref_norms = jnp.sum(jnp.square(references.astype(jnp.float32)), axis=1)
    cross_terms = lax.dot_general(
        images, references, (((1,), (1,)), ((), ())), preferred_element_type=jnp.float32
    )
    contrast = initial_contrast
    for _ in range(ITERS):
        contrast = refitted(cross_terms, ref_norms, contrast, initial_contrast)
    exponent, own_high = relative(cross_terms, ref_norms, contrast)
    total = log_total(own_high + jnp.log(jnp.sum(exponent, axis=1)))
    factor = jnp.exp(own_high - total) * contrast
    weights = (exponent * factor[:, None]).astype(jnp.bfloat16)

    refs, width = references.shape
    rows = refs // X
    x = lax.div(lax.axis_index("img"), Y)

    def partial_of(x):
        chosen = lax.dynamic_slice_in_dim(weights, x * rows, rows, 1)
        return lax.dot_general(
            chosen, images, (((0,), (0,)), ((), ())), preferred_element_type=jnp.float32
        )

    arrived = [
        along_x(partial_of(lax.rem(x + d, X)).astype(jnp.bfloat16), d) for d in DISTANCES
    ]
    partial = partial_of(x)
    for piece in arrived:
        partial = partial + piece.astype(jnp.float32)
    pieces = partial.astype(jnp.bfloat16).reshape(Y, rows // Y, width)
    sums = jnp.sum(exchanged(pieces, "img", COLUMNS).astype(jnp.float32), axis=0)

    own = sent_to_all(normalize(sums), "img", COLUMNS).reshape(rows, width)
    held = [(x, own)] + [(lax.rem(x + X - d, X), along_x(own, d)) for d in DISTANCES]
    gathered = jnp.zeros((refs, width), jnp.bfloat16)
    own_logs = []
    for at, piece in held:
        gathered = lax.dynamic_update_slice_in_dim(gathered, piece, at * rows, 0)
        new_norms = jnp.sum(jnp.square(piece.astype(jnp.float32)), axis=1) / width
        new_cross = lax.dot_general(
            images, piece, (((1,), (1,)), ((), ())), preferred_element_type=jnp.float32
        ) * width ** (-0.5)
        exponent, own_high = relative(new_cross, new_norms, contrast)
        own_logs.append(own_high + jnp.log(jnp.sum(exponent, axis=1)))
    own_logs = jnp.stack(own_logs)
    highest = jnp.max(own_logs, axis=0)
    own_log = highest + jnp.log(jnp.sum(jnp.exp(own_logs - highest[None]), axis=0))
    loglik = log_total(own_log) - math.log(refs * lax.axis_size("ref"))
    return (gathered, contrast, loglik)


def solution(mesh):
    placed = (P("img", None), P("ref", None), P("img"))
    return jax.shard_map(
        per_device,
        mesh=mesh,
        in_specs=placed,
        out_specs=(P("ref", None), P("img"), P("img")),
        check_vma=False,
    )
```

time: 220 us -> 198 us (0.900)
  blocking collectives: 193 us -> 83.6 us
  waiting for transfers between devices: 0 us -> 42.1 us
  starting transfers between devices: 0 us -> 34.4 us
  matrix products: 12 us -> 21 us
  local copies, waits for them, and re-layouts: 1.93 us -> 5.02 us
    all_to_all x7 -> x5, blocking collectives: 193 us -> 83.6 us  [exchanged(): lax.all_to_all(pieces, axis, 0, 0, tiled=True, axis_index_groups=groups)]
    ppermute x0 -> x6, waiting for transfers between devices: none -> 29.5 us  [along_x(): lax.ppermute(value, 'img', [(i, (i + distance * Y) % (X * Y)) for i in ra...]
    ppermute x0 -> x6, starting transfers between devices: none -> 21.6 us  [along_x(): lax.ppermute(value, 'img', [(i, (i + distance * Y) % (X * Y)) for i in ra...]
    all_to_all x0 -> x2, starting transfers between devices: none -> 12.8 us  [exchanged(): lax.all_to_all(pieces, axis, 0, 0, tiled=True, axis_index_groups=groups)]
    all_to_all x0 -> x2, waiting for transfers between devices: none -> 12.6 us  [exchanged(): lax.all_to_all(pieces, axis, 0, 0, tiled=True, axis_index_groups=groups)]
    dot_general x2 -> x8, matrix products: 7.31 us -> 16.3 us  [the longest x4 8.38 us: per_device(): lax.dot_general(images, piece, (((1,), (1,)), ((), ())), preferred_elemen...]
    dynamic_update_slice x0 -> x4, local copies, waits for them, and re-layouts: none -> 2.57 us  [per_device(): gathered = lax.dynamic_update_slice_in_dim(gathered, piece, at * rows, 0)]
    reduce_sum x12 -> x19, other arithmetic: 5.09 us -> 4.83 us  [the longest x3 2.84 us: refitted(): lower = jnp.sum(exponent * (ref_norms + prior_weight)[None, :], axis=1)]
  transfers between devices with their start and end apart: 0 -> 8, of which waited for: 0 -> 6; matrix products, arithmetic and copies ran while one was open for 0% -> 4% of each run, Pallas kernels for 0% -> 0%
where the time goes in v3:
time: 198 us; the launch traced here: 197 us
  blocking collectives  83.6 us (42%)
  waiting for transfers between devices  42.1 us (21%)
  starting transfers between devices  34.4 us (17%)
  matrix products  21 us (11%)
  other arithmetic  10 us (5%)
  local copies, waits for them, and re-layouts  5.02 us (3%)
    all_to_all x5, blocking collectives, exchanged(): lax.all_to_all(pieces, axis, 0, 0, tiled=True, axis_index_groups=groups)  83.6 us
    ppermute x6, waiting for transfers between devices, along_x(): lax.ppermute(value, 'img', [(i, (i + distance * Y) % (X * Y)) for i in ra...  29.5 us
    ppermute x6, starting transfers between devices, along_x(): lax.ppermute(value, 'img', [(i, (i + distance * Y) % (X * Y)) for i in ra...  21.6 us
    all_to_all x2, starting transfers between devices, exchanged(): lax.all_to_all(pieces, axis, 0, 0, tiled=True, axis_index_groups=groups)  12.8 us
    all_to_all x2, waiting for transfers between devices, exchanged(): lax.all_to_all(pieces, axis, 0, 0, tiled=True, axis_index_groups=groups)  12.6 us
    dot_general x4, matrix products, per_device(): lax.dot_general(images, piece, (((1,), (1,)), ((), ())), preferred_elemen...  8.38 us
    dot_general x4, matrix products, partial_of(): lax.dot_general(chosen, images, (((0,), (0,)), ((), ())), preferred_eleme...  7.93 us
    dot_general x1, matrix products, per_device(): lax.dot_general(images, references, (((1,), (1,)), ((), ())), preferred_e...  4.69 us
  transfers between devices with their start and end apart: 8, of which 6 were waited for; matrix products, arithmetic and copies ran while one was open for 4% of the time, Pallas kernels for 0%

profile of v3, /device:TPU:1, one launch (start us, length us, event | category | flops | bytes accessed | tf_op | source)
XLA Modules:
  0.0 197.4 jit_solution(84224247419277107)
XLA Ops:
  0.7 2.2 %multiply_reduce_fusion = f32[512]{0:T(512)S(1)} fusion(bf16[512,2048]{1,0:T(8,128)(2,1)} %param.4), kind=kLoop, calls=%fused_computation | loop fusion | flops 3145216 | bytes 2099200 | tf_op jit(solution)/shard_map/reduce_sum | solution.py:69
  2.9 4.7 %fusion.13 = (f32[1024]{0:T(1024)S(1)}, f32[1024,512]{0,1:T(8,128)S(1)}) fusion(f32[512]{0:T(512)S(1)} %multiply_reduce_fusion, f32[1024]{0:T(1024)S(1)} %multiply_multiply_fusion.3, f32[1024]{0:T(1024)S(1)} %copy-done.5, bf16[1024,2048]{1,0:T(8,128)(2,1)} %param.3, bf16[512,2048]{1,0:T(8,128)(2,1)S(1)} %copy-done.2), kind=kOutput, calls=%fused_computation.36 | convolution fusion | flops 2150104064 | bytes 8402944 | tf_op jit(solution)/shard_map/dot_general | solution.py:70
  8.7 20.8 %all_to_all.35 = f32[16,1,2048]{2,1,0:T(1,128)S(1)} all-to-all(f32[16,1,2048]{2,1,0:T(1,128)S(1)} %broadcast_in_dim.15), channel_id=1, replica_groups=mesh['img'=32,'ref'=16] {'ref'}, dimensions={0} | all-to-all | bytes 262144 | tf_op jit(solution)/shard_map/all_to_all | solution.py:22
  31.1 11.6 %all_to_all.36 = f32[16,1,2048]{2,1,0:T(1,128)S(1)} all-to-all(f32[16,1,2048]{2,1,0:T(1,128)S(1)} %broadcast_in_dim.16), channel_id=1, replica_groups=mesh['img'=32,'ref'=16] {'ref'}, dimensions={0} | all-to-all | bytes 262144 | tf_op jit(solution)/shard_map/all_to_all | solution.py:22
  44.2 11.6 %all_to_all.37 = f32[16,1,2048]{2,1,0:T(1,128)S(1)} all-to-all(f32[16,1,2048]{2,1,0:T(1,128)S(1)} %broadcast_in_dim.17), channel_id=1, replica_groups=mesh['img'=32,'ref'=16] {'ref'}, dimensions={0} | all-to-all | bytes 262144 | tf_op jit(solution)/shard_map/all_to_all | solution.py:22
  57.7 3.4 %all-to-all-start.3 = ((f32[16,1,1024]{2,1,0:T(1,128)}), f32[16,1,1024]{2,1,0:T(1,128)S(1)}, u32[]{:S(2)}, u32[]{:S(2)}) async-start(f32[16,1,1024]{2,1,0:T(1,128)} %broadcast_in_dim.18), calls=%async_computation.3 | async-start | bytes 131072 | tf_op jit(solution)/shard_map/all_to_all | solution.py:22
  61.1 7.2 %all-to-all-done.3 = f32[16,1,1024]{2,1,0:T(1,128)S(1)} async-done(((f32[16,1,1024]{2,1,0:T(1,128)}), f32[16,1,1024]{2,1,0:T(1,128)S(1)}, u32[]{:S(2)}, u32[]{:S(2)}) %all-to-all-start.3) | async-done | bytes 65568 | tf_op jit(solution)/shard_map/all_to_all | solution.py:22
  69.2 3.1 %convolution_convert_fusion = bf16[128,2048]{1,0:T(8,128)(2,1)S(1)} fusion(bf16[1024,2048]{1,0:T(8,128)(2,1)} %param.3, bf16[1024,512]{0,1:T(8,128)(2,1)S(1)} %multiply_convert_fusion, s32[]{:T(128)S(6)} %select_n.19), kind=kOutput, calls=%fused_computation.1 | convolution fusion | flops 537133056 | bytes 4980740 | tf_op jit(solution)/shard_map/dot_general | solution.py:87
  74.1 4.6 %collective-permute-start = (bf16[128,2048]{1,0:T(8,128)(2,1)S(1)}, bf16[128,2048]{1,0:T(8,128)(2,1)S(1)}, u32[]{:S(2)}, u32[]{:S(2)}) collective-permute-start(bf16[128,2048]{1,0:T(8,128)(2,1)S(1)} %convolution_convert_fusion.2), channel_id=1, source_target_pairs={{0,256},{16,272},{32,288},{48,304},{64,320},{80,336},{96,352},{112... | collective-permute-start | bytes 1572872 | tf_op jit(solution)/shard_map/ppermute | solution.py:31
  78.7 2.2 %collective-permute-start.1 = (bf16[128,2048]{1,0:T(8,128)(2,1)S(1)}, bf16[128,2048]{1,0:T(8,128)(2,1)}, u32[]{:S(2)}, u32[]{:S(2)}) collective-permute-start(bf16[128,2048]{1,0:T(8,128)(2,1)S(1)} %convolution_convert_fusion.1), channel_id=1, source_target_pairs={{0,128},{16,144},{32,160},{48,176},{64,192},{80,208},{96,224},{112... | collective-permute-start | bytes 1572872 | tf_op jit(solution)/shard_map/ppermute | solution.py:31
  81.0 4.4 %collective-permute-start.2 = (bf16[128,2048]{1,0:T(8,128)(2,1)S(1)}, bf16[128,2048]{1,0:T(8,128)(2,1)}, u32[]{:S(2)}, u32[]{:S(2)}) collective-permute-start(bf16[128,2048]{1,0:T(8,128)(2,1)S(1)} %convolution_convert_fusion), channel_id=1, source_target_pairs={{0,384},{16,400},{32,416},{48,432},{64,448},{80,464},{96,480},{112... | collective-permute-start | bytes 1572872 | tf_op jit(solution)/shard_map/ppermute | solution.py:31
  85.4 5.4 %collective-permute-done = bf16[128,2048]{1,0:T(8,128)(2,1)S(1)} collective-permute-done((bf16[128,2048]{1,0:T(8,128)(2,1)S(1)}, bf16[128,2048]{1,0:T(8,128)(2,1)S(1)}, u32[]{:S(2)}, u32[]{:S(2)}) %collective-permute-start) | collective-permute-done | bytes 524320 | tf_op jit(solution)/shard_map/ppermute | solution.py:31
  90.8 11.9 %collective-permute-done.1 = bf16[128,2048]{1,0:T(8,128)(2,1)} collective-permute-done((bf16[128,2048]{1,0:T(8,128)(2,1)S(1)}, bf16[128,2048]{1,0:T(8,128)(2,1)}, u32[]{:S(2)}, u32[]{:S(2)}) %collective-permute-start.1) | collective-permute-done | bytes 524320 | tf_op jit(solution)/shard_map/ppermute | solution.py:31
  102.7 3.4 %add_convert_fusion = bf16[128,2048]{1,0:T(8,128)(2,1)S(1)} fusion(bf16[128,2048]{1,0:T(8,128)(2,1)} %collective-permute-done.2, bf16[128,2048]{1,0:T(8,128)(2,1)} %collective-permute-done.1, bf16[128,2048]{1,0:T(8,128)(2,1)S(1)} %collective-permute-done, bf16[1024,2048]{1,0:T(8,128)(2,1)} %param.3, bf16[1024,512]{0,1:T(8,128)(2,1)S(1)} %multiply_convert_fusion, ...), kind=kOutput, calls=%fused_computation.45 | convolution fusion | flops 538705920 | bytes 6553604 | tf_op jit(solution)/shard_map/dot_general | solution.py:87
  106.1 22.7 %all_to_all.38 = bf16[8,16,2048]{2,1,0:T(8,128)(2,1)S(1)} all-to-all(bf16[8,16,2048]{2,1,0:T(8,128)(2,1)S(1)} %bitcast.70), channel_id=1, replica_groups={{0,16,32,48,64,80,96,112},{128,144,160,176,192,208,224,240},{256,272,28..., dimensions={0} | all-to-all | bytes 1048576 | tf_op jit(solution)/shard_map/all_to_all | solution.py:22
  129.2 16.9 %all_to_all.39 = bf16[8,16,2048]{2,1,0:T(8,128)(2,1)S(1)} all-to-all(bf16[8,16,2048]{2,1,0:T(8,128)(2,1)S(1)} %broadcast_in_dim.19), channel_id=1, replica_groups={{0,16,32,48,64,80,96,112},{128,144,160,176,192,208,224,240},{256,272,28..., dimensions={0} | all-to-all | bytes 1048576 | tf_op jit(solution)/shard_map/all_to_all | solution.py:22
  146.0 4.7 %collective-permute-start.5 = (bf16[128,2048]{1,0:T(8,128)(2,1)S(1)}, bf16[128,2048]{1,0:T(8,128)(2,1)S(1)}, u32[]{:S(2)}, u32[]{:S(2)}) collective-permute-start(bf16[128,2048]{1,0:T(8,128)(2,1)S(1)} %bitcast.65), channel_id=1, source_target_pairs={{0,384},{16,400},{32,416},{48,432},{64,448},{80,464},{96,480},{112... | collective-permute-start | bytes 1572872 | tf_op jit(solution)/shard_map/ppermute | solution.py:31
  150.7 1.9 collective-permute-start.4
  152.7 3.7 %collective-permute-start.3 = (bf16[128,2048]{1,0:T(8,128)(2,1)S(1)}, bf16[128,2048]{1,0:T(8,128)(2,1)S(1)}, u32[]{:S(2)}, u32[]{:S(2)}) collective-permute-start(bf16[128,2048]{1,0:T(8,128)(2,1)S(1)} %bitcast.67), channel_id=1, source_target_pairs={{0,256},{16,272},{32,288},{48,304},{64,320},{80,336},{96,352},{112... | collective-permute-start | bytes 1572872 | tf_op jit(solution)/shard_map/ppermute | solution.py:31
  156.7 3.7 %fusion.41 = (f32[1024]{0:T(1024)S(1)}, f32[1024,128]{0,1:T(8,128)S(1)}) fusion(f32[128]{0:T(128)S(1)} %div.86, f32[1024]{0:T(1024)S(1)} %multiply_multiply_fusion, f32[1024]{0:T(1024)S(1)} %get-tuple-element.20, bf16[128,2048]{1,0:T(8,128)(2,1)S(1)} %bitcast.68, bf16[1024,2048]{1,0:T(8,128)(2,1)} %param.3), kind=kOutput, calls=%fused_computation.119 | convolution fusion | flops 537525248 | bytes 5255680 | tf_op jit(solution)/shard_map/dot_general | solution.py:107
  161.0 2.9 %collective-permute-done.4 = bf16[128,2048]{1,0:T(8,128)(2,1)S(1)} collective-permute-done((bf16[128,2048]{1,0:T(8,128)(2,1)S(1)}, bf16[128,2048]{1,0:T(8,128)(2,1)S(1)}, u32[]{:S(2)}, u32[]{:S(2)}) %collective-permute-start.4) | collective-permute-done | bytes 524320 | tf_op jit(solution)/shard_map/ppermute | solution.py:31
  164.1 9.4 %collective-permute-done.3 = bf16[128,2048]{1,0:T(8,128)(2,1)S(1)} collective-permute-done((bf16[128,2048]{1,0:T(8,128)(2,1)S(1)}, bf16[128,2048]{1,0:T(8,128)(2,1)S(1)}, u32[]{:S(2)}, u32[]{:S(2)}) %collective-permute-start.3) | collective-permute-done | bytes 524320 | tf_op jit(solution)/shard_map/ppermute | solution.py:31
  179.4 9.4 %all-to-all-start.6 = ((f32[16,1,1024]{2,1,0:T(1,128)}), f32[16,1,1024]{2,1,0:T(1,128)S(1)}, u32[]{:S(2)}, u32[]{:S(2)}) async-start(f32[16,1,1024]{2,1,0:T(1,128)} %broadcast_in_dim.20), calls=%async_computation.6 | async-start | bytes 131072 | tf_op jit(solution)/shard_map/all_to_all | solution.py:22
  191.3 5.3 %all-to-all-done.6 = f32[16,1,1024]{2,1,0:T(1,128)S(1)} async-done(((f32[16,1,1024]{2,1,0:T(1,128)}), f32[16,1,1024]{2,1,0:T(1,128)S(1)}, u32[]{:S(2)}, u32[]{:S(2)}) %all-to-all-start.6) | async-done | bytes 65568 | tf_op jit(solution)/shard_map/all_to_all | solution.py:22
  (86 shorter events, 18.9 us)
Async XLA Ops:
  0.6 2.3 %copy-start.2 = (bf16[512,2048]{1,0:T(8,128)(2,1)S(1)}, bf16[512,2048]{1,0:T(8,128)(2,1)}, u32[]{:S(2)}) copy-start(bf16[512,2048]{1,0:T(8,128)(2,1)} %param.4) | copy-start | bytes 6291460
  0.6 2.2 %copy-start.5 = (f32[1024]{0:T(1024)S(1)}, f32[1024]{0:T(1024)}, u32[]{:S(2)}) copy-start(f32[1024]{0:T(1024)} %param.5) | copy-start | bytes 12292
  56.0 12.5 %copy-start.4 = (f32[1024]{0:T(1024)}, f32[1024]{0:T(1024)S(1)}, u32[]{:S(2)}) copy-start(f32[1024]{0:T(1024)S(1)} %get-tuple-element.21) | copy-start | bytes 12292
  57.7 10.7 %all-to-all-start.3 = ((f32[16,1,1024]{2,1,0:T(1,128)}), f32[16,1,1024]{2,1,0:T(1,128)S(1)}, u32[]{:S(2)}, u32[]{:S(2)}) async-start(f32[16,1,1024]{2,1,0:T(1,128)} %broadcast_in_dim.18), calls=%async_computation.3 | async-start | bytes 131072 | tf_op jit(solution)/shard_map/all_to_all | solution.py:22
  69.2 3.5 %copy-start = (bf16[1024,2048]{1,0:T(8,128)(2,1)S(1)}, bf16[1024,2048]{1,0:T(8,128)(2,1)}, u32[]{:S(2)}) copy-start(bf16[1024,2048]{1,0:T(8,128)(2,1)} %param.3) | copy-start | bytes 12582916
  74.1 16.7 %collective-permute-start = (bf16[128,2048]{1,0:T(8,128)(2,1)S(1)}, bf16[128,2048]{1,0:T(8,128)(2,1)S(1)}, u32[]{:S(2)}, u32[]{:S(2)}) collective-permute-start(bf16[128,2048]{1,0:T(8,128)(2,1)S(1)} %convolution_convert_fusion.2), channel_id=1, source_target_pairs={{0,256},{16,272},{32,288},{48,304},{64,320},{80,336},{96,352},{112... | collective-permute-start | bytes 1572872 | tf_op jit(solution)/shard_map/ppermute | solution.py:31
  78.7 23.9 %collective-permute-start.1 = (bf16[128,2048]{1,0:T(8,128)(2,1)S(1)}, bf16[128,2048]{1,0:T(8,128)(2,1)}, u32[]{:S(2)}, u32[]{:S(2)}) collective-permute-start(bf16[128,2048]{1,0:T(8,128)(2,1)S(1)} %convolution_convert_fusion.1), channel_id=1, source_target_pairs={{0,128},{16,144},{32,160},{48,176},{64,192},{80,208},{96,224},{112... | collective-permute-start | bytes 1572872 | tf_op jit(solution)/shard_map/ppermute | solution.py:31
  81.0 21.7 %collective-permute-start.2 = (bf16[128,2048]{1,0:T(8,128)(2,1)S(1)}, bf16[128,2048]{1,0:T(8,128)(2,1)}, u32[]{:S(2)}, u32[]{:S(2)}) collective-permute-start(bf16[128,2048]{1,0:T(8,128)(2,1)S(1)} %convolution_convert_fusion), channel_id=1, source_target_pairs={{0,384},{16,400},{32,416},{48,432},{64,448},{80,464},{96,480},{112... | collective-permute-start | bytes 1572872 | tf_op jit(solution)/shard_map/ppermute | solution.py:31
  146.0 14.8 %collective-permute-start.5 = (bf16[128,2048]{1,0:T(8,128)(2,1)S(1)}, bf16[128,2048]{1,0:T(8,128)(2,1)S(1)}, u32[]{:S(2)}, u32[]{:S(2)}) collective-permute-start(bf16[128,2048]{1,0:T(8,128)(2,1)S(1)} %bitcast.65), channel_id=1, source_target_pairs={{0,384},{16,400},{32,416},{48,432},{64,448},{80,464},{96,480},{112... | collective-permute-start | bytes 1572872 | tf_op jit(solution)/shard_map/ppermute | solution.py:31
  150.7 13.2 %collective-permute-start.4 = (bf16[128,2048]{1,0:T(8,128)(2,1)S(1)}, bf16[128,2048]{1,0:T(8,128)(2,1)S(1)}, u32[]{:S(2)}, u32[]{:S(2)}) collective-permute-start(bf16[128,2048]{1,0:T(8,128)(2,1)S(1)} %bitcast.66), channel_id=1, source_target_pairs={{0,128},{16,144},{32,160},{48,176},{64,192},{80,208},{96,224},{112... | collective-permute-start | bytes 1572872 | tf_op jit(solution)/shard_map/ppermute | solution.py:31
  152.7 20.9 %collective-permute-start.3 = (bf16[128,2048]{1,0:T(8,128)(2,1)S(1)}, bf16[128,2048]{1,0:T(8,128)(2,1)S(1)}, u32[]{:S(2)}, u32[]{:S(2)}) collective-permute-start(bf16[128,2048]{1,0:T(8,128)(2,1)S(1)} %bitcast.67), channel_id=1, source_target_pairs={{0,256},{16,272},{32,288},{48,304},{64,320},{80,336},{96,352},{112... | collective-permute-start | bytes 1572872 | tf_op jit(solution)/shard_map/ppermute | solution.py:31
  160.5 13.2 %copy-start.1 = (bf16[1024,2048]{1,0:T(8,128)(2,1)S(1)}, bf16[1024,2048]{1,0:T(8,128)(2,1)}, u32[]{:S(2)}) copy-start(bf16[1024,2048]{1,0:T(8,128)(2,1)} %param.3) | copy-start | bytes 12582916
  160.8 12.9 %copy-start.3 = (bf16[512,2048]{1,0:T(8,128)(2,1)}, bf16[512,2048]{1,0:T(8,128)(2,1)S(1)}, u32[]{:S(2)}) copy-start(bf16[512,2048]{1,0:T(8,128)(2,1)S(1)} %constant_dynamic-update-slice_fusion.3) | copy-start | bytes 6291460
  179.4 17.2 %all-to-all-start.6 = ((f32[16,1,1024]{2,1,0:T(1,128)}), f32[16,1,1024]{2,1,0:T(1,128)S(1)}, u32[]{:S(2)}, u32[]{:S(2)}) async-start(f32[16,1,1024]{2,1,0:T(1,128)} %broadcast_in_dim.20), calls=%async_computation.6 | async-start | bytes 131072 | tf_op jit(solution)/shard_map/all_to_all | solution.py:22

commit v4 on v2

v4 whole, which is shorter than its diff:
```python
import math

import jax
import jax.numpy as jnp
from jax import lax
from jax.experimental import pallas as pl
from jax.experimental.pallas import tpu as pltpu
from jax.sharding import PartitionSpec as P

ITERS = 3


sharpness = 2.0
prior_weight = 1.0
epsilon = 1e-06

X, Y = 4, 8
NEAR = [[x * Y + 2 * pair + side for x in range(X) for side in range(2)] for pair in range(Y // 2)]
FAR = [[x * Y + 2 * pair + side for pair in range(Y // 2)] for x in range(X) for side in range(2)]


def exchanged(pieces, axis, groups=None):
    return lax.all_to_all(pieces, axis, 0, 0, tiled=True, axis_index_groups=groups)


def sent_to_all(value, axis, groups=None):
    devices = len(groups[0]) if groups else lax.axis_size(axis)
    return exchanged(jnp.broadcast_to(value[None], (devices, *value.shape)), axis, groups)


def summed_share(partial):
    rows, width = partial.shape
    for groups in (NEAR, FAR):
        rows //= len(groups[0])
        pieces = partial.astype(jnp.bfloat16).reshape(len(groups[0]), rows, width)
        partial = jnp.sum(exchanged(pieces, "img", groups).astype(jnp.float32), axis=0)
    return partial


def gathered_rows(share):
    for groups in (FAR, NEAR):
        share = sent_to_all(share, "img", groups).reshape(-1, share.shape[-1])
    return share


def normalize(sums):
    meansq = jnp.mean(sums * sums, axis=1)
    return (sums * lax.rsqrt(meansq + epsilon)[:, None]).astype(jnp.bfloat16)


LANES = 128
GROUP = 4


def spread(value, group):
    rows = [
        jnp.broadcast_to(value[k : k + 1], (8, LANES))
        for k in range(group * GROUP, (group + 1) * GROUP)
    ]
    return jnp.concatenate(rows, axis=1)


def folded(parts):
    rows = [part[:, k * LANES : (k + 1) * LANES] for part in parts for k in range(GROUP)]
    return jnp.concatenate(rows, axis=0)


def scan_rows(cross, norms, group, contrast, body, init, rows=8, unroll=8):
    twice = sharpness * spread(contrast, group)
    square = 0.5 * sharpness * spread(contrast * contrast, group)
    columns = slice(group * GROUP * LANES, (group + 1) * GROUP * LANES)

    def step(i, carry):
        at = pl.ds(pl.multiple_of(i * rows, rows), rows)
        for k in range(rows // 8):
            at = pl.ds(pl.multiple_of(i * rows + k * 8, 8), 8)
            terms = cross[at, columns]
            norm = jnp.concatenate([norms[at, :]] * GROUP, axis=1)
            carry = body(at, columns, twice * terms - square * norm, terms, norm, carry)
        return carry

    return lax.fori_loop(0, cross.shape[0] // rows, step, init, unroll=unroll)


def highest_of(cross, norms, group, contrast):
    low = jnp.full((8, GROUP * LANES), -jnp.inf, jnp.float32)
    high = scan_rows(
        cross, norms, group, contrast, lambda a, b, s, c, n, high: jnp.maximum(high, s), low
    )
    return jnp.max(high, axis=0, keepdims=True)


def own_refit(cross, norms, contrast, prior):
    logs, quotients = [], []
    for group in range(cross.shape[1] // (GROUP * LANES)):
        high = highest_of(cross, norms, group, contrast)
        wide = jnp.broadcast_to(high, (8, GROUP * LANES))

        def body(at, columns, scored, terms, norm, carry):
            total, along, weight = carry
            e = jnp.exp(scored - wide)
            return total + e, along + e * terms, weight + e * norm

        zero = jnp.zeros((8, GROUP * LANES), jnp.float32)
        total, along, weight = (
            jnp.sum(v, axis=0, keepdims=True)
            for v in scan_rows(cross, norms, group, contrast, body, (zero,) * 3)
        )
        first = spread(prior, group)[:1]
        lower = weight + prior_weight * total
        logs.append(high + jnp.log(lower))
        quotients.append((along + prior_weight * first * total) / lower)
    return folded(logs), folded(quotients)


def own_total(cross, norms, contrast):
    logs = []
    for group in range(cross.shape[1] // (GROUP * LANES)):
        high = highest_of(cross, norms, group, contrast)
        wide = jnp.broadcast_to(high, (8, GROUP * LANES))
        total = scan_rows(
            cross,
            norms,
            group,
            contrast,
            lambda a, b, s, c, n, total: total + jnp.exp(s - wide),
            jnp.zeros((8, GROUP * LANES), jnp.float32),
        )
        logs.append(high + jnp.log(jnp.sum(total, axis=0, keepdims=True)))
    return folded(logs)


def combined(received):
    logs, quotients = received[:, :8], received[:, 8:]
    share = jnp.exp(logs - jnp.max(logs, axis=0, keepdims=True))
    return jnp.sum(share * quotients, axis=0) / jnp.sum(share, axis=0)


def combined_log(logs):
    high = jnp.max(logs, axis=0)
    return high + jnp.log(jnp.sum(jnp.exp(logs - high[None]), axis=0))


def send_refit(out, cross, norms, contrast, prior):
    logs, quotients = own_refit(cross, norms, contrast, prior)
    out[...] = jnp.broadcast_to(jnp.concatenate([logs, quotients], axis=0)[None], out.shape)


def squares(held, norms, scale):
    rows = 32

    def step(i, _):
        at = pl.ds(pl.multiple_of(i * rows, rows), rows)
        wide = held[at, :].astype(jnp.float32)
        summed = jnp.sum(wide * wide, axis=1, keepdims=True) * scale
        norms[at, :] = jnp.broadcast_to(summed, (rows, LANES))
        return 0

    lax.fori_loop(0, held.shape[0] // rows, step, 0, unroll=2)


def products(held, images, cross, scale, before=lambda k: None):
    columns = 256
    for k in range(images.shape[0] // columns):
        at = slice(k * columns, (k + 1) * columns)
        before(k)
        product = lax.dot_general(
            held[...], images[at, :], (((1,), (1,)), ((), ())), preferred_element_type=jnp.float32
        )
        cross[:, at] = product if scale is None else product * scale


def first_kernel(images, references, prior, cross, kept, norms, out, held, semaphores):
    columns = 256
    copies = [pltpu.make_async_copy(references, held, semaphores.at[0])]
    for k in range(images.shape[0] // columns):
        at = pl.ds(k * columns, columns)
        copies.append(
            pltpu.make_async_copy(images.at[at], kept.at[at], semaphores.at[k + 1])
        )
    for copy in copies:
        copy.start()
    copies[0].wait()
    squares(held, norms, 1.0)
    products(held, kept, cross, None, lambda k: copies[k + 1].wait())
    send_refit(out, cross, norms, prior[...], prior[...])


def refit_kernel(received, cross, norms, prior, out):
    send_refit(out, cross, norms, combined(received[...]), prior[...])


def total_kernel(received, cross, norms, contrast, out):
    contrast[...] = combined(received[...])
    out[...] = jnp.broadcast_to(own_total(cross, norms, contrast[...])[None], out.shape)


def sum_kernel(received, cross, norms, contrast, images, out, weights):
    log_total = combined_log(received[...])
    for group in range(cross.shape[1] // (GROUP * LANES)):
        wide = spread(log_total, group)
        scale = spread(contrast[...], group)
        columns = slice(group * GROUP * LANES, (group + 1) * GROUP * LANES)
        twice = sharpness * scale
        square = 0.5 * sharpness * (scale * scale)

        def step(i, _):
            at = pl.ds(pl.multiple_of(i * 16, 16), 16)
            parts = []
            for k in range(2):
                part = pl.ds(pl.multiple_of(i * 16 + k * 8, 8), 8)
                norm = jnp.concatenate([norms[part, :]] * GROUP, axis=1)
                scored = twice * cross[part, columns] - square * norm
                parts.append(jnp.exp(scored - wide) * scale)
            weights[at, columns] = jnp.concatenate(parts, axis=0).astype(jnp.bfloat16)
            return 0

        lax.fori_loop(0, cross.shape[0] // 16, step, 0, unroll=4)
    width = 512
    for k in range(images.shape[1] // width):
        at = slice(k * width, (k + 1) * width)
        out[:, at] = jnp.dot(
            weights[...], images[:, at], preferred_element_type=jnp.float32
        ).astype(jnp.bfloat16)


def score_kernel(gathered, images, contrast, out, result, cross, norms, semaphore):
    copy = pltpu.make_async_copy(gathered, result, semaphore)
    copy.start()
    width = gathered.shape[1]
    squares(gathered, norms, 1.0 / width)
    products(gathered, images, cross, width**-0.5)
    out[...] = jnp.broadcast_to(own_total(cross, norms, contrast[...])[None], out.shape)
    copy.wait()


VMEM = pl.BlockSpec(memory_space=pltpu.VMEM)
HBM = pl.BlockSpec(memory_space=pltpu.HBM)


def call(kernel, outs, *args, ins=None, specs=None, scratch=(), limit=16, flops=0):
    return pl.pallas_call(
        kernel,
        out_shape=outs,
        in_specs=ins or [VMEM] * len(args),
        out_specs=specs or (VMEM,) * len(outs),
        scratch_shapes=scratch,
        compiler_params=pltpu.CompilerParams(vmem_limit_bytes=limit * 2**20),
        cost_estimate=pl.CostEstimate(
            flops=flops, bytes_accessed=2**22, transcendentals=2**19
        ),
    )(*args)


def per_device(images, references, initial_contrast):
    count, width = images.shape
    refs = references.shape[0]
    devices = lax.axis_size("ref")
    f32, bf16 = jnp.float32, jnp.bfloat16
    per_image = (count // LANES, LANES)
    prior = initial_contrast.reshape(per_image)
    two = pltpu.VMEM((devices, 2 * per_image[0], LANES), f32)
    one = pltpu.VMEM((devices, *per_image), f32)
    flops = 2 * count * refs * width

    cross, kept, norms, own = call(
        first_kernel,
        (
            pltpu.VMEM((refs, count), f32),
            pltpu.VMEM((count, width), bf16),
            pltpu.VMEM((refs, LANES), f32),
            two,
        ),
        images,
        references,
        prior,
        ins=[HBM, HBM, VMEM],
        scratch=[pltpu.VMEM((refs, width), bf16), pltpu.SemaphoreType.DMA((5,))],
        limit=56,
        flops=flops,
    )
    for _ in range(ITERS - 1):
        (own,) = call(refit_kernel, (two,), exchanged(own, "ref"), cross, norms, prior)
    contrast, own = call(
        total_kernel,
        (pltpu.VMEM(per_image, f32), one),
        exchanged(own, "ref"),
        cross,
        norms,
    )
    (img_partial,) = call(
        sum_kernel,
        (pltpu.VMEM((refs, width), bf16),),
        exchanged(own, "ref"),
        cross,
        norms,
        contrast,
        kept,
        scratch=[pltpu.VMEM((refs, count), bf16)],
        flops=flops,
    )
    gathered = gathered_rows(normalize(summed_share(img_partial)))
    own, new_references = call(
        score_kernel,
        (one, jax.ShapeDtypeStruct((refs, width), bf16)),
        gathered,
        kept,
        contrast,
        specs=(VMEM, HBM),
        scratch=[
            pltpu.VMEM((refs, count), f32),
            pltpu.VMEM((refs, LANES), f32),
            pltpu.SemaphoreType.DMA,
        ],
        flops=flops,
    )
    loglik = combined_log(exchanged(own, "ref")) - math.log(refs * devices)
    return (new_references, contrast.reshape(count), loglik.reshape(count))


def solution(mesh):
    placed = (P("img", None), P("ref", None), P("img"))
    return jax.shard_map(
        per_device,
        mesh=mesh,
        in_specs=placed,
        out_specs=(P("ref", None), P("img"), P("img")),
        check_vma=False,
    )
```

time: 185 us -> 180 us (0.973)
  Pallas kernels: 0 us -> 21.3 us
  blocking collectives: 157 us -> 138 us
  matrix products: 14.1 us -> 0 us
  other arithmetic: 10.1 us -> 1.27 us
  starting transfers between devices: 0 us -> 8.36 us
  waiting for transfers between devices: 0 us -> 7.24 us
    pallas_call x0 -> x6, Pallas kernels: none -> 21.3 us  [call(): pl.pallas_call(kernel, out_shape=outs, in_specs=ins or [VMEM] * len(args)...]
    all_to_all x9 -> x8, blocking collectives: 157 us -> 138 us  [exchanged(): lax.all_to_all(pieces, axis, 0, 0, tiled=True, axis_index_groups=groups)]
    dot_general x3 -> x0, matrix products: 14.1 us -> none  [the longest x1 4.78 us: per_device(): lax.dot_general(weights, images, (((0,), (0,)), ((), ())), preferred_elem...]
    all_to_all x0 -> x1, starting transfers between devices: none -> 8.36 us  [exchanged(): lax.all_to_all(pieces, axis, 0, 0, tiled=True, axis_index_groups=groups)]
    all_to_all x0 -> x1, waiting for transfers between devices: none -> 7.24 us  [exchanged(): lax.all_to_all(pieces, axis, 0, 0, tiled=True, axis_index_groups=groups)]
    reduce_sum x12 -> x1, other arithmetic: 6.72 us -> 0.03 us  [combined_log(): return high + jnp.log(jnp.sum(jnp.exp(logs - high[None]), axis=0))]
  transfers between devices with their start and end apart: 0 -> 1, of which waited for: 0 -> 1; matrix products, arithmetic and copies ran while one was open for 0% -> 0% of each run, Pallas kernels for 0% -> 0%
where the time goes in v4:
time: 180 us
  blocking collectives  138 us (77%)
  Pallas kernels  21.3 us (12%)
  starting transfers between devices  8.36 us (5%)
  waiting for transfers between devices  7.24 us (4%)
  local copies, waits for them, and re-layouts  3.06 us (2%)
    all_to_all x8, blocking collectives, exchanged(): lax.all_to_all(pieces, axis, 0, 0, tiled=True, axis_index_groups=groups)  138 us
    pallas_call x6, Pallas kernels, call(): pl.pallas_call(kernel, out_shape=outs, in_specs=ins or [VMEM] * len(args)...  21.3 us
    all_to_all x1, starting transfers between devices, exchanged(): lax.all_to_all(pieces, axis, 0, 0, tiled=True, axis_index_groups=groups)  8.36 us
    all_to_all x1, waiting for transfers between devices, exchanged(): lax.all_to_all(pieces, axis, 0, 0, tiled=True, axis_index_groups=groups)  7.24 us
  transfers between devices with their start and end apart: 1, of which 1 were waited for; matrix products, arithmetic and copies ran while one was open for 0% of the time, Pallas kernels for 0%

profile of v4, /device:TPU:1, one launch (start us, length us, event | category | flops | bytes accessed | tf_op | source)
XLA Modules:
  0.0 179.8 jit_solution(59583322659647926)
XLA Ops:
  0.6 0.0 copy-start.3
  0.6 9.7 %shard_map.58 = (f32[512,1024]{1,0:T(8,128)S(1)}, bf16[1024,2048]{1,0:T(8,128)(2,1)S(1)}, f32[512,128]{1,0:T(8,128)S(1)}, f32[16,16,128]{2,1,0:T(8,128)S(1)}) custom-call(bf16[1024,2048]{1,0:T(8,128)(2,1)} %images.1, bf16[512,2048]{1,0:T(8,128)(2,1)} %references.1, f32[8,128]{1,0:T(8,128)} %bitcast.11), custom_call_target="tpu_custom_call" | custom-call | flops 2147483648 | bytes 4194304 | tf_op jit(solution)/shard_map/pallas_call | solution.py:242
  10.4 20.8 %all_to_all.45.received = f32[16,16,128]{2,1,0:T(8,128)S(1)} all-to-all(f32[16,16,128]{2,1,0:T(8,128)S(1)} %get-tuple-element.11), channel_id=1, replica_groups=mesh['img'=32,'ref'=16] {'ref'}, dimensions={0} | all-to-all | bytes 262144 | tf_op jit(solution)/shard_map/all_to_all | solution.py:23
  31.2 1.3 shard_map.59
  32.5 11.6 %all_to_all.46.received = f32[16,16,128]{2,1,0:T(8,128)S(1)} all-to-all(f32[16,16,128]{2,1,0:T(8,128)S(1)} %shard_map.59), channel_id=1, replica_groups=mesh['img'=32,'ref'=16] {'ref'}, dimensions={0} | all-to-all | bytes 262144 | tf_op jit(solution)/shard_map/all_to_all | solution.py:23
  44.1 1.3 shard_map.60
  45.3 11.6 %all_to_all.47.received = f32[16,16,128]{2,1,0:T(8,128)S(1)} all-to-all(f32[16,16,128]{2,1,0:T(8,128)S(1)} %shard_map.60), channel_id=1, replica_groups=mesh['img'=32,'ref'=16] {'ref'}, dimensions={0} | all-to-all | bytes 262144 | tf_op jit(solution)/shard_map/all_to_all | solution.py:23
  56.9 1.0 shard_map.61
  57.9 10.2 %all_to_all.48.received = f32[16,8,128]{2,1,0:T(8,128)S(1)} all-to-all(f32[16,8,128]{2,1,0:T(8,128)S(1)} %get-tuple-element.14), channel_id=1, replica_groups=mesh['img'=32,'ref'=16] {'ref'}, dimensions={0} | all-to-all | bytes 131072 | tf_op jit(solution)/shard_map/all_to_all | solution.py:23
  68.2 2.2 %copy-done.1 = bf16[1024,2048]{1,0:T(8,128)(2,1)S(1)} copy-done((bf16[1024,2048]{1,0:T(8,128)(2,1)S(1)}, bf16[1024,2048]{1,0:T(8,128)(2,1)}, u32[]{:S(2)}) %copy-start.1) | copy-done | bytes 4194328
  70.4 3.0 %shard_map.62 = bf16[512,2048]{1,0:T(8,128)(2,1)S(1)} custom-call(f32[16,8,128]{2,1,0:T(8,128)S(1)} %all_to_all.48.received, f32[512,1024]{1,0:T(8,128)S(1)} %get-tuple-element.12.cross, f32[512,128]{1,0:T(8,128)S(1)} %get-tuple-element.13.norms, f32[8,128]{1,0:T(8,128)S(1)} %get-tuple-element.15.contrast, bf16[1024,2048]{1,0:T(8,128)(2,1)S(1)} %copy-done.1), custom_call_target="tpu_custom_call" | custom-call | flops 2147483648 | bytes 4194304 | tf_op jit(solution)/shard_map/pallas_call | solution.py:242
  73.4 31.4 %all_to_all.49 = bf16[8,64,2048]{2,1,0:T(8,128)(2,1)S(1)} all-to-all(bf16[8,64,2048]{2,1,0:T(8,128)(2,1)S(1)} %bitcast.9), channel_id=1, replica_groups={{0,16,128,144,256,272,384,400},{32,48,160,176,288,304,416,432},{64,80,1..., dimensions={0} | all-to-all | bytes 4194304 | tf_op jit(solution)/shard_map/all_to_all | solution.py:23
  104.8 0.4 reduce_sum.39
  105.2 13.8 %all_to_all.50 = bf16[4,16,2048]{2,1,0:T(8,128)(2,1)S(1)} all-to-all(bf16[4,16,2048]{2,1,0:T(8,128)(2,1)S(1)} %bitcast.14), channel_id=1, replica_groups={{0,32,64,96},{16,48,80,112},{128,160,192,224},{144,176,208,240},{256,28..., dimensions={0} | all-to-all | bytes 524288 | tf_op jit(solution)/shard_map/all_to_all | solution.py:23
  119.0 0.1 multiply_reduce_fusion
  119.2 0.1 multiply_convert_fusion
  119.3 12.6 %all_to_all.51 = bf16[4,16,2048]{2,1,0:T(8,128)(2,1)S(1)} all-to-all(bf16[4,16,2048]{2,1,0:T(8,128)(2,1)S(1)} %broadcast_in_dim.6), channel_id=1, replica_groups={{0,32,64,96},{16,48,80,112},{128,160,192,224},{144,176,208,240},{256,28..., dimensions={0} | all-to-all | bytes 524288 | tf_op jit(solution)/shard_map/all_to_all | solution.py:23
  131.9 0.2 broadcast_in_dim.8
  132.2 25.7 %all_to_all.52 = bf16[8,64,2048]{2,1,0:T(8,128)(2,1)S(1)} all-to-all(bf16[8,64,2048]{2,1,0:T(8,128)(2,1)S(1)} %broadcast_in_dim.8), channel_id=1, replica_groups={{0,16,128,144,256,272,384,400},{32,48,160,176,288,304,416,432},{64,80,1..., dimensions={0} | all-to-all | bytes 4194304 | tf_op jit(solution)/shard_map/all_to_all | solution.py:23
  157.9 5.0 %shard_map.63 = (f32[16,8,128]{2,1,0:T(8,128)}, bf16[512,2048]{1,0:T(8,128)(2,1)}) custom-call(bf16[512,2048]{1,0:T(8,128)(2,1)S(1)} %bitcast.10, bf16[1024,2048]{1,0:T(8,128)(2,1)S(1)} %copy-done.2, f32[8,128]{1,0:T(8,128)S(1)} %get-tuple-element.15.contrast), custom_call_target="tpu_custom_call" | custom-call | flops 2147483648 | bytes 4194304 | tf_op jit(solution)/shard_map/pallas_call | solution.py:242
  162.9 8.4 %all-to-all-start.8 = ((f32[16,8,128]{2,1,0:T(8,128)}), f32[16,8,128]{2,1,0:T(8,128)S(1)}, u32[]{:S(2)}, u32[]{:S(2)}) async-start(f32[16,8,128]{2,1,0:T(8,128)} %get-tuple-element.18), calls=%async_computation.8 | async-start | bytes 131072 | tf_op jit(solution)/shard_map/all_to_all | solution.py:23
  171.3 0.6 copy.6
  171.9 7.2 %all-to-all-done.8 = f32[16,8,128]{2,1,0:T(8,128)S(1)} async-done(((f32[16,8,128]{2,1,0:T(8,128)}), f32[16,8,128]{2,1,0:T(8,128)S(1)}, u32[]{:S(2)}, u32[]{:S(2)}) %all-to-all-start.8) | async-done | bytes 65568 | tf_op jit(solution)/shard_map/all_to_all | solution.py:23
  179.2 0.6 add_bitcast_fusion
  (11 shorter events, 0.1 us)
Async XLA Ops:
  0.6 30.6 %copy-start.3 = (f32[1024]{0:T(1024)S(1)}, f32[1024]{0:T(1024)}, u32[]{:S(2)}) copy-start(f32[1024]{0:T(1024)} %param.5) | copy-start | bytes 12292
  10.4 34.9 %copy-start = (bf16[1024,2048]{1,0:T(8,128)(2,1)}, bf16[1024,2048]{1,0:T(8,128)(2,1)S(1)}, u32[]{:S(2)}) copy-start(bf16[1024,2048]{1,0:T(8,128)(2,1)S(1)} %get-tuple-element.16.images) | copy-start | bytes 12582916
  68.2 2.2 %copy-start.1 = (bf16[1024,2048]{1,0:T(8,128)(2,1)S(1)}, bf16[1024,2048]{1,0:T(8,128)(2,1)}, u32[]{:S(2)}) copy-start(bf16[1024,2048]{1,0:T(8,128)(2,1)} %copy-done) | copy-start | bytes 12582916
  132.2 25.7 %copy-start.2 = (bf16[1024,2048]{1,0:T(8,128)(2,1)S(1)}, bf16[1024,2048]{1,0:T(8,128)(2,1)}, u32[]{:S(2)}) copy-start(bf16[1024,2048]{1,0:T(8,128)(2,1)} %copy-done) | copy-start | bytes 12582916
  162.9 16.2 %all-to-all-start.8 = ((f32[16,8,128]{2,1,0:T(8,128)}), f32[16,8,128]{2,1,0:T(8,128)S(1)}, u32[]{:S(2)}, u32[]{:S(2)}) async-start(f32[16,8,128]{2,1,0:T(8,128)} %get-tuple-element.18), calls=%async_computation.8 | async-start | bytes 131072 | tf_op jit(solution)/shard_map/all_to_all | solution.py:23

commit v5 on v4

v5 whole, which is shorter than its diff:
```python
import math

import jax
import jax.numpy as jnp
from jax import lax
from jax.experimental import pallas as pl
from jax.experimental.pallas import tpu as pltpu
from jax.sharding import PartitionSpec as P

ITERS = 3


sharpness = 2.0
prior_weight = 1.0
epsilon = 1e-06

X, Y = 4, 8
NEAR = [[x * Y + 2 * pair + side for x in range(X) for side in range(2)] for pair in range(Y // 2)]
FAR = [[x * Y + 2 * pair + side for pair in range(Y // 2)] for x in range(X) for side in range(2)]


def exchanged(pieces, axis, groups=None):
    return lax.all_to_all(pieces, axis, 0, 0, tiled=True, axis_index_groups=groups)


def sent_to_all(value, axis, groups=None):
    devices = len(groups[0]) if groups else lax.axis_size(axis)
    return exchanged(jnp.broadcast_to(value[None], (devices, *value.shape)), axis, groups)


def summed_share(partial):
    rows, width = partial.shape
    for groups in (NEAR, FAR):
        rows //= len(groups[0])
        pieces = partial.astype(jnp.bfloat16).reshape(len(groups[0]), rows, width)
        partial = jnp.sum(exchanged(pieces, "img", groups).astype(jnp.float32), axis=0)
    return partial


def gathered_rows(share):
    for groups in (FAR, NEAR):
        share = sent_to_all(share, "img", groups).reshape(-1, share.shape[-1])
    return share


def normalize(sums):
    meansq = jnp.mean(sums * sums, axis=1)
    return (sums * lax.rsqrt(meansq + epsilon)[:, None]).astype(jnp.bfloat16)


LANES = 128
BLOCK = 256
ROWS = BLOCK // LANES


def laid_out(value, k):
    return jnp.concatenate([value[k * ROWS + j : k * ROWS + j + 1] for j in range(ROWS)], axis=1)


def folded(parts):
    rows = [part[:, j * LANES : (j + 1) * LANES] for part in parts for j in range(ROWS)]
    return jnp.concatenate(rows, axis=0)


def block_at(k):
    return slice(k * BLOCK, (k + 1) * BLOCK)


def scored(terms, norms, contrast):
    wide = jnp.concatenate([norms[...]] * ROWS, axis=1)
    return sharpness * contrast * terms - 0.5 * sharpness * (contrast * contrast) * wide, wide


def own_refit(terms, norms, contrast, prior):
    scores, wide = scored(terms, norms, contrast)
    high = jnp.max(scores, axis=0, keepdims=True)
    e = jnp.exp(scores - high)
    total = jnp.sum(e, axis=0, keepdims=True)
    upper = jnp.sum(e * terms, axis=0, keepdims=True) + prior_weight * prior * total
    lower = jnp.sum(e * wide, axis=0, keepdims=True) + prior_weight * total
    return high + jnp.log(lower), upper / lower


def own_total(terms, norms, contrast):
    scores, _ = scored(terms, norms, contrast)
    high = jnp.max(scores, axis=0, keepdims=True)
    return high + jnp.log(jnp.sum(jnp.exp(scores - high), axis=0, keepdims=True))


def combined(received):
    logs, quotients = received[:, :8], received[:, 8:]
    share = jnp.exp(logs - jnp.max(logs, axis=0, keepdims=True))
    return jnp.sum(share * quotients, axis=0) / jnp.sum(share, axis=0)


def combined_log(logs):
    high = jnp.max(logs, axis=0)
    return high + jnp.log(jnp.sum(jnp.exp(logs - high[None]), axis=0))


def send(out, *parts):
    own = jnp.concatenate([folded(part) for part in parts], axis=0)
    out[...] = jnp.broadcast_to(own[None], out.shape)


def squares(held, norms, scale):
    rows = 64
    for i in range(held.shape[0] // rows):
        at = slice(i * rows, (i + 1) * rows)
        summed = jnp.zeros((rows, LANES), jnp.float32)
        for k in range(held.shape[1] // LANES):
            wide = held[at, k * LANES : (k + 1) * LANES].astype(jnp.float32)
            summed = summed + wide * wide
        norm = jnp.sum(summed, axis=1, keepdims=True) * scale
        norms[at, :] = jnp.broadcast_to(norm, (rows, LANES))


def product(held, images, k):
    return lax.dot_general(
        held[...], images[block_at(k), :], (((1,), (1,)), ((), ())), preferred_element_type=jnp.float32
    )


def first_kernel(images, references, prior, cross, kept, norms, out, held, semaphores):
    halves = 2
    size = images.shape[0] // halves
    copies = [pltpu.make_async_copy(references, held, semaphores.at[halves])]
    for h in range(halves):
        at = pl.ds(h * size, size)
        copies.append(pltpu.make_async_copy(images.at[at], kept.at[at], semaphores.at[h]))
    for copy in copies:
        copy.start()
    copies[0].wait()
    logs, quotients = [], []
    for h in range(halves):
        copies[h + 1].wait()
        if h == 0:
            squares(held, norms, 1.0)
        blocks = range(h * size // BLOCK, (h + 1) * size // BLOCK)
        for k in blocks:
            cross[:, block_at(k)] = product(held, kept, k)
        for k in blocks:
            start = laid_out(prior, k)
            log, quotient = own_refit(cross[:, block_at(k)], norms, start, start)
            logs.append(log)
            quotients.append(quotient)
    send(out, logs, quotients)


def refit_kernel(received, cross, norms, prior, images, out):
    contrast = combined(received[...])
    logs, quotients = [], []
    for k in range(cross.shape[1] // BLOCK):
        log, quotient = own_refit(
            cross[:, block_at(k)], norms, laid_out(contrast, k), laid_out(prior, k)
        )
        logs.append(log)
        quotients.append(quotient)
    send(out, logs, quotients)


def total_kernel(received, cross, norms, images, contrast, out):
    found = combined(received[...])
    contrast[...] = found
    send(
        out,
        [
            own_total(cross[:, block_at(k)], norms, laid_out(found, k))
            for k in range(cross.shape[1] // BLOCK)
        ],
    )


def sum_kernel(received, cross, norms, contrast, images, out, weights):
    log_total = combined_log(received[...])
    for k in range(cross.shape[1] // BLOCK):
        scale = laid_out(contrast, k)
        scores, _ = scored(cross[:, block_at(k)], norms, scale)
        posterior = jnp.exp(scores - laid_out(log_total, k))
        weights[:, block_at(k)] = (posterior * scale).astype(jnp.bfloat16)
    width = 512
    for k in range(images.shape[1] // width):
        at = slice(k * width, (k + 1) * width)
        out[:, at] = jnp.dot(
            weights[...], images[:, at], preferred_element_type=jnp.float32
        ).astype(jnp.bfloat16)


def score_kernel(gathered, images, contrast, out, result, norms, semaphore):
    copy = pltpu.make_async_copy(gathered, result, semaphore)
    copy.start()
    width = gathered.shape[1]
    squares(gathered, norms, 1.0 / width)
    logs = []
    for k in range(images.shape[0] // BLOCK):
        terms = product(gathered, images, k) * width**-0.5
        logs.append(own_total(terms, norms, laid_out(contrast, k)))
    send(out, logs)
    copy.wait()


VMEM = pl.BlockSpec(memory_space=pltpu.VMEM)
HBM = pl.BlockSpec(memory_space=pltpu.HBM)


def call(kernel, outs, *args, ins=None, specs=None, scratch=(), limit=16, flops=0):
    return pl.pallas_call(
        kernel,
        out_shape=outs,
        in_specs=ins or [VMEM] * len(args),
        out_specs=specs or (VMEM,) * len(outs),
        scratch_shapes=scratch,
        compiler_params=pltpu.CompilerParams(vmem_limit_bytes=limit * 2**20),
        cost_estimate=pl.CostEstimate(
            flops=flops, bytes_accessed=2**22, transcendentals=2**19
        ),
    )(*args)


def per_device(images, references, initial_contrast):
    count, width = images.shape
    refs = references.shape[0]
    devices = lax.axis_size("ref")
    f32, bf16 = jnp.float32, jnp.bfloat16
    per_image = (count // LANES, LANES)
    prior = initial_contrast.reshape(per_image)
    two = pltpu.VMEM((devices, 2 * per_image[0], LANES), f32)
    one = pltpu.VMEM((devices, *per_image), f32)
    flops = 2 * count * refs * width

    cross, kept, norms, own = call(
        first_kernel,
        (
            pltpu.VMEM((refs, count), f32),
            pltpu.VMEM((count, width), bf16),
            pltpu.VMEM((refs, LANES), f32),
            two,
        ),
        images,
        references,
        prior,
        ins=[HBM, HBM, VMEM],
        scratch=[pltpu.VMEM((refs, width), bf16), pltpu.SemaphoreType.DMA((3,))],
        limit=54,
        flops=flops,
    )
    for _ in range(ITERS - 1):
        (own,) = call(refit_kernel, (two,), exchanged(own, "ref"), cross, norms, prior, kept)
    contrast, own = call(
        total_kernel,
        (pltpu.VMEM(per_image, f32), one),
        exchanged(own, "ref"),
        cross,
        norms,
        kept,
    )
    (img_partial,) = call(
        sum_kernel,
        (pltpu.VMEM((refs, width), bf16),),
        exchanged(own, "ref"),
        cross,
        norms,
        contrast,
        kept,
        scratch=[pltpu.VMEM((refs, count), bf16)],
        flops=flops,
    )
    gathered = gathered_rows(normalize(summed_share(img_partial)))
    own, new_references = call(
        score_kernel,
        (one, jax.ShapeDtypeStruct((refs, width), bf16)),
        gathered,
        kept,
        contrast,
        specs=(VMEM, HBM),
        scratch=[
            pltpu.VMEM((refs, LANES), f32),
            pltpu.SemaphoreType.DMA,
        ],
        flops=flops,
    )
    loglik = combined_log(exchanged(own, "ref")) - math.log(refs * devices)
    return (new_references, contrast.reshape(count), loglik.reshape(count))


def solution(mesh):
    placed = (P("img", None), P("ref", None), P("img"))
    return jax.shard_map(
        per_device,
        mesh=mesh,
        in_specs=placed,
        out_specs=(P("ref", None), P("img"), P("img")),
        check_vma=False,
    )
```

time: 180 us -> 172 us (0.956)
  Pallas kernels: 21.3 us -> 15.6 us
  local copies, waits for them, and re-layouts: 3.06 us -> 0.87 us
    pallas_call x6, Pallas kernels: 21.3 us -> 15.6 us  [call(): pl.pallas_call(kernel, out_shape=outs, in_specs=ins or [VMEM] * len(args)...]
    unnamed x9 -> x7, local copies, waits for them, and re-layouts: 2.79 us -> 0.61 us
where the time goes in v5:
time: 172 us
  blocking collectives  138 us (80%)
  Pallas kernels  15.6 us (9%)
  starting transfers between devices  8.37 us (5%)
  waiting for transfers between devices  7.24 us (4%)
    all_to_all x8, blocking collectives, exchanged(): lax.all_to_all(pieces, axis, 0, 0, tiled=True, axis_index_groups=groups)  138 us
    pallas_call x6, Pallas kernels, call(): pl.pallas_call(kernel, out_shape=outs, in_specs=ins or [VMEM] * len(args)...  15.6 us
    all_to_all x1, starting transfers between devices, exchanged(): lax.all_to_all(pieces, axis, 0, 0, tiled=True, axis_index_groups=groups)  8.37 us
    all_to_all x1, waiting for transfers between devices, exchanged(): lax.all_to_all(pieces, axis, 0, 0, tiled=True, axis_index_groups=groups)  7.24 us
  transfers between devices with their start and end apart: 1, of which 1 were waited for; matrix products, arithmetic and copies ran while one was open for 0% of the time, Pallas kernels for 0%

profile of v5, /device:TPU:1, one launch (start us, length us, event | category | flops | bytes accessed | tf_op | source)
XLA Modules:
  0.0 171.9 jit_solution(14392032776731233398)
XLA Ops:
  0.6 0.0 copy-start.2
  0.6 6.6 %shard_map.58 = (f32[512,1024]{1,0:T(8,128)S(1)}, bf16[1024,2048]{1,0:T(8,128)(2,1)S(1)}, f32[512,128]{1,0:T(8,128)S(1)}, f32[16,16,128]{2,1,0:T(8,128)S(1)}) custom-call(bf16[1024,2048]{1,0:T(8,128)(2,1)} %images.1, bf16[512,2048]{1,0:T(8,128)(2,1)} %references.1, f32[8,128]{1,0:T(8,128)} %bitcast.11), custom_call_target="tpu_custom_call" | custom-call | flops 2147483648 | bytes 4194304 | tf_op jit(solution)/shard_map/pallas_call | solution.py:207
  7.2 0.0 copy-start
  7.2 20.8 %all_to_all.45.received = f32[16,16,128]{2,1,0:T(8,128)S(1)} all-to-all(f32[16,16,128]{2,1,0:T(8,128)S(1)} %get-tuple-element.11), channel_id=1, replica_groups=mesh['img'=32,'ref'=16] {'ref'}, dimensions={0} | all-to-all | bytes 262144 | tf_op jit(solution)/shard_map/all_to_all | solution.py:23
  28.0 1.1 shard_map.59
  29.1 11.6 %all_to_all.46.received = f32[16,16,128]{2,1,0:T(8,128)S(1)} all-to-all(f32[16,16,128]{2,1,0:T(8,128)S(1)} %shard_map.59), channel_id=1, replica_groups=mesh['img'=32,'ref'=16] {'ref'}, dimensions={0} | all-to-all | bytes 262144 | tf_op jit(solution)/shard_map/all_to_all | solution.py:23
  40.7 1.1 shard_map.60
  41.8 11.6 %all_to_all.47.received = f32[16,16,128]{2,1,0:T(8,128)S(1)} all-to-all(f32[16,16,128]{2,1,0:T(8,128)S(1)} %shard_map.60), channel_id=1, replica_groups=mesh['img'=32,'ref'=16] {'ref'}, dimensions={0} | all-to-all | bytes 262144 | tf_op jit(solution)/shard_map/all_to_all | solution.py:23
  53.4 0.8 shard_map.61
  54.2 10.2 %all_to_all.48.received = f32[16,8,128]{2,1,0:T(8,128)S(1)} all-to-all(f32[16,8,128]{2,1,0:T(8,128)S(1)} %get-tuple-element.15), channel_id=1, replica_groups=mesh['img'=32,'ref'=16] {'ref'}, dimensions={0} | all-to-all | bytes 131072 | tf_op jit(solution)/shard_map/all_to_all | solution.py:23
  64.4 2.4 %shard_map.62 = bf16[512,2048]{1,0:T(8,128)(2,1)S(1)} custom-call(f32[16,8,128]{2,1,0:T(8,128)S(1)} %all_to_all.48.received, f32[512,1024]{1,0:T(8,128)S(1)} %get-tuple-element.12.cross, f32[512,128]{1,0:T(8,128)S(1)} %get-tuple-element.13.norms, f32[8,128]{1,0:T(8,128)S(1)} %get-tuple-element.16.contrast, bf16[1024,2048]{1,0:T(8,128)(2,1)S(1)} %get-tuple-element.14.images), custom_call_target="tpu_custom_call" | custom-call | flops 2147483648 | bytes 4194304 | tf_op jit(solution)/shard_map/pallas_call | solution.py:207
  66.8 31.4 %all_to_all.49 = bf16[8,64,2048]{2,1,0:T(8,128)(2,1)S(1)} all-to-all(bf16[8,64,2048]{2,1,0:T(8,128)(2,1)S(1)} %bitcast.9), channel_id=1, replica_groups={{0,16,128,144,256,272,384,400},{32,48,160,176,288,304,416,432},{64,80,1..., dimensions={0} | all-to-all | bytes 4194304 | tf_op jit(solution)/shard_map/all_to_all | solution.py:23
  98.3 0.4 reduce_sum.39
  98.6 13.8 %all_to_all.50 = bf16[4,16,2048]{2,1,0:T(8,128)(2,1)S(1)} all-to-all(bf16[4,16,2048]{2,1,0:T(8,128)(2,1)S(1)} %bitcast.14), channel_id=1, replica_groups={{0,32,64,96},{16,48,80,112},{128,160,192,224},{144,176,208,240},{256,28..., dimensions={0} | all-to-all | bytes 524288 | tf_op jit(solution)/shard_map/all_to_all | solution.py:23
  112.5 0.1 multiply_reduce_fusion
  112.6 0.1 multiply_convert_fusion
  112.7 12.6 %all_to_all.51 = bf16[4,16,2048]{2,1,0:T(8,128)(2,1)S(1)} all-to-all(bf16[4,16,2048]{2,1,0:T(8,128)(2,1)S(1)} %broadcast_in_dim.6), channel_id=1, replica_groups={{0,32,64,96},{16,48,80,112},{128,160,192,224},{144,176,208,240},{256,28..., dimensions={0} | all-to-all | bytes 524288 | tf_op jit(solution)/shard_map/all_to_all | solution.py:23
  125.4 0.2 broadcast_in_dim.8
  125.6 25.7 %all_to_all.52 = bf16[8,64,2048]{2,1,0:T(8,128)(2,1)S(1)} all-to-all(bf16[8,64,2048]{2,1,0:T(8,128)(2,1)S(1)} %broadcast_in_dim.8), channel_id=1, replica_groups={{0,16,128,144,256,272,384,400},{32,48,160,176,288,304,416,432},{64,80,1..., dimensions={0} | all-to-all | bytes 4194304 | tf_op jit(solution)/shard_map/all_to_all | solution.py:23
  151.3 3.7 %shard_map.63 = (f32[16,8,128]{2,1,0:T(8,128)}, bf16[512,2048]{1,0:T(8,128)(2,1)}) custom-call(bf16[512,2048]{1,0:T(8,128)(2,1)S(1)} %bitcast.10, bf16[1024,2048]{1,0:T(8,128)(2,1)S(1)} %copy-done.1, f32[8,128]{1,0:T(8,128)S(1)} %get-tuple-element.16.contrast), custom_call_target="tpu_custom_call" | custom-call | flops 2147483648 | bytes 4194304 | tf_op jit(solution)/shard_map/pallas_call | solution.py:207
  155.0 8.4 %all-to-all-start.8 = ((f32[16,8,128]{2,1,0:T(8,128)}), f32[16,8,128]{2,1,0:T(8,128)S(1)}, u32[]{:S(2)}, u32[]{:S(2)}) async-start(f32[16,8,128]{2,1,0:T(8,128)} %get-tuple-element.18), calls=%async_computation.8 | async-start | bytes 131072 | tf_op jit(solution)/shard_map/all_to_all | solution.py:23
  163.4 0.6 copy.6
  164.0 7.2 %all-to-all-done.8 = f32[16,8,128]{2,1,0:T(8,128)S(1)} async-done(((f32[16,8,128]{2,1,0:T(8,128)}), f32[16,8,128]{2,1,0:T(8,128)S(1)}, u32[]{:S(2)}, u32[]{:S(2)}) %all-to-all-start.8) | async-done | bytes 65568 | tf_op jit(solution)/shard_map/all_to_all | solution.py:23
  171.3 0.6 add_bitcast_fusion
  (9 shorter events, 0.1 us)
Async XLA Ops:
  0.6 27.4 %copy-start.2 = (f32[1024]{0:T(1024)S(1)}, f32[1024]{0:T(1024)}, u32[]{:S(2)}) copy-start(f32[1024]{0:T(1024)} %param.5) | copy-start | bytes 12292
  7.2 57.2 %copy-start = (bf16[1024,2048]{1,0:T(8,128)(2,1)}, bf16[1024,2048]{1,0:T(8,128)(2,1)S(1)}, u32[]{:S(2)}) copy-start(bf16[1024,2048]{1,0:T(8,128)(2,1)S(1)} %get-tuple-element.14.images) | copy-start | bytes 12582916
  125.6 25.7 %copy-start.1 = (bf16[1024,2048]{1,0:T(8,128)(2,1)S(1)}, bf16[1024,2048]{1,0:T(8,128)(2,1)}, u32[]{:S(2)}) copy-start(bf16[1024,2048]{1,0:T(8,128)(2,1)} %copy-done) | copy-start | bytes 12582916
  155.0 16.2 %all-to-all-start.8 = ((f32[16,8,128]{2,1,0:T(8,128)}), f32[16,8,128]{2,1,0:T(8,128)S(1)}, u32[]{:S(2)}, u32[]{:S(2)}) async-start(f32[16,8,128]{2,1,0:T(8,128)} %get-tuple-element.18), calls=%async_computation.8 | async-start | bytes 131072 | tf_op jit(solution)/shard_map/all_to_all | solution.py:23

commit v6 on v5

--- a/solution.py
+++ b/solution.py
@@ -14,32 +14,49 @@
 prior_weight = 1.0
 epsilon = 1e-06
 
-X, Y = 4, 8
-NEAR = [[x * Y + 2 * pair + side for x in range(X) for side in range(2)] for pair in range(Y // 2)]
-FAR = [[x * Y + 2 * pair + side for pair in range(Y // 2)] for x in range(X) for side in range(2)]
+X, Y, Z, CORES = 4, 8, 8, 2
+PLANE = ("img", "ref")
+
+
+def device(x, y, ref):
+    return ((x % X) * Y + y % Y) * Z * CORES + ref
+
+
+SIDES = [(a, b) for a in range(2) for b in range(2)]
+PLACES = [(2 * i, 2 * j) for i in range(X // 2) for j in range(Y // 2)]
+CORNERS = [(ref, ref % CORES) for ref in range(Z * CORES)]
+BLOCKS = [
+    [device(x + a + core, y + b + core, ref) for a, b in SIDES]
+    for ref, core in CORNERS
+    for x, y in PLACES
+]
+SPREAD = [
+    [device(x + a + core, y + b + core, ref) for x, y in PLACES]
+    for ref, core in CORNERS
+    for a, b in SIDES
+]
 
 
 def exchanged(pieces, axis, groups=None):
     return lax.all_to_all(pieces, axis, 0, 0, tiled=True, axis_index_groups=groups)
 
 
-def sent_to_all(value, axis, groups=None):
-    devices = len(groups[0]) if groups else lax.axis_size(axis)
-    return exchanged(jnp.broadcast_to(value[None], (devices, *value.shape)), axis, groups)
+def sent_to_all(value, axis, groups):
+    return exchanged(jnp.broadcast_to(value[None], (len(groups[0]), *value.shape)), axis, groups)
 
 
 def summed_share(partial):
     rows, width = partial.shape
-    for groups in (NEAR, FAR):
+    for groups in (BLOCKS, SPREAD):
         rows //= len(groups[0])
         pieces = partial.astype(jnp.bfloat16).reshape(len(groups[0]), rows, width)
-        partial = jnp.sum(exchanged(pieces, "img", groups).astype(jnp.float32), axis=0)
+        partial = jnp.sum(exchanged(pieces, PLANE, groups).astype(jnp.float32), axis=0)
     return partial
 
 
 def gathered_rows(share):
-    for groups in (FAR, NEAR):
-        share = sent_to_all(share, "img", groups).reshape(-1, share.shape[-1])
+    for groups in (SPREAD, BLOCKS):
+        share = sent_to_all(share, PLANE, groups).reshape(-1, share.shape[-1])
     return share
 
 

time: 172 us -> 171 us (level)
  no operation moved by 1% of the time
where the time goes in v6:
time: 171 us
  blocking collectives  138 us (81%)
  Pallas kernels  15.6 us (9%)
  waiting for transfers between devices  7.24 us (4%)
  starting transfers between devices  7.14 us (4%)
    all_to_all x8, blocking collectives, exchanged(): lax.all_to_all(pieces, axis, 0, 0, tiled=True, axis_index_groups=groups)  138 us
    pallas_call x6, Pallas kernels, call(): pl.pallas_call(kernel, out_shape=outs, in_specs=ins or [VMEM] * len(args)...  15.6 us
    all_to_all x1, waiting for transfers between devices, exchanged(): lax.all_to_all(pieces, axis, 0, 0, tiled=True, axis_index_groups=groups)  7.24 us
    all_to_all x1, starting transfers between devices, exchanged(): lax.all_to_all(pieces, axis, 0, 0, tiled=True, axis_index_groups=groups)  7.14 us
  transfers between devices with their start and end apart: 1, of which 1 were waited for; matrix products, arithmetic and copies ran while one was open for 0% of the time, Pallas kernels for 0%

profile of v6, /device:TPU:1, one launch (start us, length us, event | category | flops | bytes accessed | tf_op | source)
XLA Modules:
  0.0 170.6 jit_solution(16710107098311449572)
XLA Ops:
  0.6 6.6 %shard_map.58 = (f32[512,1024]{1,0:T(8,128)S(1)}, bf16[1024,2048]{1,0:T(8,128)(2,1)S(1)}, f32[512,128]{1,0:T(8,128)S(1)}, f32[16,16,128]{2,1,0:T(8,128)S(1)}) custom-call(bf16[1024,2048]{1,0:T(8,128)(2,1)} %images.1, bf16[512,2048]{1,0:T(8,128)(2,1)} %references.1, f32[8,128]{1,0:T(8,128)} %bitcast.11), custom_call_target="tpu_custom_call" | custom-call | flops 2147483648 | bytes 4194304 | tf_op jit(solution)/shard_map/pallas_call | solution.py:224
  7.2 20.8 %all_to_all.45.received = f32[16,16,128]{2,1,0:T(8,128)S(1)} all-to-all(f32[16,16,128]{2,1,0:T(8,128)S(1)} %get-tuple-element.11), channel_id=1, replica_groups=mesh['img'=32,'ref'=16] {'ref'}, dimensions={0} | all-to-all | bytes 262144 | tf_op jit(solution)/shard_map/all_to_all | solution.py:41
  28.0 1.1 shard_map.59
  29.1 11.6 %all_to_all.46.received = f32[16,16,128]{2,1,0:T(8,128)S(1)} all-to-all(f32[16,16,128]{2,1,0:T(8,128)S(1)} %shard_map.59), channel_id=1, replica_groups=mesh['img'=32,'ref'=16] {'ref'}, dimensions={0} | all-to-all | bytes 262144 | tf_op jit(solution)/shard_map/all_to_all | solution.py:41
  40.7 1.1 shard_map.60
  41.8 11.6 %all_to_all.47.received = f32[16,16,128]{2,1,0:T(8,128)S(1)} all-to-all(f32[16,16,128]{2,1,0:T(8,128)S(1)} %shard_map.60), channel_id=1, replica_groups=mesh['img'=32,'ref'=16] {'ref'}, dimensions={0} | all-to-all | bytes 262144 | tf_op jit(solution)/shard_map/all_to_all | solution.py:41
  53.4 0.8 shard_map.61
  54.2 10.2 %all_to_all.48.received = f32[16,8,128]{2,1,0:T(8,128)S(1)} all-to-all(f32[16,8,128]{2,1,0:T(8,128)S(1)} %get-tuple-element.15), channel_id=1, replica_groups=mesh['img'=32,'ref'=16] {'ref'}, dimensions={0} | all-to-all | bytes 131072 | tf_op jit(solution)/shard_map/all_to_all | solution.py:41
  64.4 2.4 %shard_map.62 = bf16[512,2048]{1,0:T(8,128)(2,1)S(1)} custom-call(f32[16,8,128]{2,1,0:T(8,128)S(1)} %all_to_all.48.received, f32[512,1024]{1,0:T(8,128)S(1)} %get-tuple-element.12.cross, f32[512,128]{1,0:T(8,128)S(1)} %get-tuple-element.13.norms, f32[8,128]{1,0:T(8,128)S(1)} %get-tuple-element.16.contrast, bf16[1024,2048]{1,0:T(8,128)(2,1)S(1)} %get-tuple-element.14.images), custom_call_target="tpu_custom_call" | custom-call | flops 2147483648 | bytes 4194304 | tf_op jit(solution)/shard_map/pallas_call | solution.py:224
  66.8 20.5 %all_to_all.49 = bf16[4,128,2048]{2,1,0:T(8,128)(2,1)S(1)} all-to-all(bf16[4,128,2048]{2,1,0:T(8,128)(2,1)S(1)} %bitcast.9), channel_id=1, replica_groups={{0,16,128,144},{32,48,160,176},{64,80,192,208},{96,112,224,240},{256,27..., dimensions={0} | all-to-all | bytes 4194304 | tf_op jit(solution)/shard_map/all_to_all | solution.py:41
  87.3 0.4 reduce_sum.39
  87.8 23.1 %all_to_all.50 = bf16[8,16,2048]{2,1,0:T(8,128)(2,1)S(1)} all-to-all(bf16[8,16,2048]{2,1,0:T(8,128)(2,1)S(1)} %bitcast.15), channel_id=1, replica_groups={{0,32,64,96,256,288,320,352},{16,48,80,112,272,304,336,368},{128,160,19..., dimensions={0} | all-to-all | bytes 1048576 | tf_op jit(solution)/shard_map/all_to_all | solution.py:41
  110.9 0.1 convert_reduce_fusion
  110.9 0.1 multiply_reduce_fusion
  111.1 0.1 multiply_convert_fusion
  111.2 0.1 broadcast_in_dim.6
  111.2 18.3 %all_to_all.51 = bf16[8,16,2048]{2,1,0:T(8,128)(2,1)S(1)} all-to-all(bf16[8,16,2048]{2,1,0:T(8,128)(2,1)S(1)} %broadcast_in_dim.6), channel_id=1, replica_groups={{0,32,64,96,256,288,320,352},{16,48,80,112,272,304,336,368},{128,160,19..., dimensions={0} | all-to-all | bytes 1048576 | tf_op jit(solution)/shard_map/all_to_all | solution.py:41
  129.6 0.2 broadcast_in_dim.8
  129.8 21.4 %all_to_all.52 = bf16[4,128,2048]{2,1,0:T(8,128)(2,1)S(1)} all-to-all(bf16[4,128,2048]{2,1,0:T(8,128)(2,1)S(1)} %broadcast_in_dim.8), channel_id=1, replica_groups={{0,16,128,144},{32,48,160,176},{64,80,192,208},{96,112,224,240},{256,27..., dimensions={0} | all-to-all | bytes 4194304 | tf_op jit(solution)/shard_map/all_to_all | solution.py:41
  151.3 3.7 %shard_map.63 = (f32[16,8,128]{2,1,0:T(8,128)}, bf16[512,2048]{1,0:T(8,128)(2,1)}) custom-call(bf16[512,2048]{1,0:T(8,128)(2,1)S(1)} %bitcast.10, bf16[1024,2048]{1,0:T(8,128)(2,1)S(1)} %copy-done.1, f32[8,128]{1,0:T(8,128)S(1)} %get-tuple-element.16.contrast), custom_call_target="tpu_custom_call" | custom-call | flops 2147483648 | bytes 4194304 | tf_op jit(solution)/shard_map/pallas_call | solution.py:224
  155.0 7.1 %all-to-all-start.8 = ((f32[16,8,128]{2,1,0:T(8,128)}), f32[16,8,128]{2,1,0:T(8,128)S(1)}, u32[]{:S(2)}, u32[]{:S(2)}) async-start(f32[16,8,128]{2,1,0:T(8,128)} %get-tuple-element.18), calls=%async_computation.8 | async-start | bytes 131072 | tf_op jit(solution)/shard_map/all_to_all | solution.py:41
  162.1 0.6 copy.6
  162.7 7.2 %all-to-all-done.8 = f32[16,8,128]{2,1,0:T(8,128)S(1)} async-done(((f32[16,8,128]{2,1,0:T(8,128)}), f32[16,8,128]{2,1,0:T(8,128)S(1)}, u32[]{:S(2)}, u32[]{:S(2)}) %all-to-all-start.8) | async-done | bytes 65568 | tf_op jit(solution)/shard_map/all_to_all | solution.py:41
  170.0 0.6 add_bitcast_fusion
  (9 shorter events, 0.1 us)
Async XLA Ops:
  0.6 27.4 %copy-start.2 = (f32[1024]{0:T(1024)S(1)}, f32[1024]{0:T(1024)}, u32[]{:S(2)}) copy-start(f32[1024]{0:T(1024)} %param.5) | copy-start | bytes 12292
  7.2 57.2 %copy-start = (bf16[1024,2048]{1,0:T(8,128)(2,1)}, bf16[1024,2048]{1,0:T(8,128)(2,1)S(1)}, u32[]{:S(2)}) copy-start(bf16[1024,2048]{1,0:T(8,128)(2,1)S(1)} %get-tuple-element.14.images) | copy-start | bytes 12582916
  129.8 21.4 %copy-start.1 = (bf16[1024,2048]{1,0:T(8,128)(2,1)S(1)}, bf16[1024,2048]{1,0:T(8,128)(2,1)}, u32[]{:S(2)}) copy-start(bf16[1024,2048]{1,0:T(8,128)(2,1)} %copy-done) | copy-start | bytes 12582916
  155.0 15.0 %all-to-all-start.8 = ((f32[16,8,128]{2,1,0:T(8,128)}), f32[16,8,128]{2,1,0:T(8,128)S(1)}, u32[]{:S(2)}, u32[]{:S(2)}) async-start(f32[16,8,128]{2,1,0:T(8,128)} %get-tuple-element.18), calls=%async_computation.8 | async-start | bytes 131072 | tf_op jit(solution)/shard_map/all_to_all | solution.py:41

commit v7 on v6

--- a/solution.py
+++ b/solution.py
@@ -23,17 +23,36 @@
 
 
 SIDES = [(a, b) for a in range(2) for b in range(2)]
-PLACES = [(2 * i, 2 * j) for i in range(X // 2) for j in range(Y // 2)]
+ALONG_X = [2 * i for i in range(X // 2)]
+ALONG_Y = [2 * j for j in range(Y // 2)]
 CORNERS = [(ref, ref % CORES) for ref in range(Z * CORES)]
+
+
+def at(ref, core, side, x, y):
+    return device(x + side[0] + core, y + side[1] + core, ref)
+
+
 BLOCKS = [
-    [device(x + a + core, y + b + core, ref) for a, b in SIDES]
-    for ref, core in CORNERS
-    for x, y in PLACES
+    [at(*corner, side, x, y) for side in SIDES]
+    for corner in CORNERS
+    for x in ALONG_X
+    for y in ALONG_Y
 ]
 SPREAD = [
-    [device(x + a + core, y + b + core, ref) for x, y in PLACES]
-    for ref, core in CORNERS
-    for a, b in SIDES
+    [at(*corner, side, x, y) for x in ALONG_X for y in ALONG_Y]
+    for corner in CORNERS
+    for side in SIDES
+]
+FAR = [
+    [at(*corner, side, x, y) for y in ALONG_Y]
+    for corner in CORNERS
+    for side in SIDES
+    for x in ALONG_X
+]
+NEAR = [
+    [at(*corner, side, x, y) for side in SIDES for x in ALONG_X]
+    for corner in CORNERS
+    for y in ALONG_Y
 ]
 
 
@@ -55,7 +74,7 @@
 
 
 def gathered_rows(share):
-    for groups in (SPREAD, BLOCKS):
+    for groups in (FAR, NEAR):
         share = sent_to_all(share, PLANE, groups).reshape(-1, share.shape[-1])
     return share
 

time: 171 us -> 172 us (level)
  blocking collectives: 138 us -> 141 us
  starting transfers between devices: 7.14 us -> 4.99 us
    all_to_all x8, blocking collectives: 138 us -> 141 us  [exchanged(): lax.all_to_all(pieces, axis, 0, 0, tiled=True, axis_index_groups=groups)]
    all_to_all x1, starting transfers between devices: 7.14 us -> 4.99 us  [exchanged(): lax.all_to_all(pieces, axis, 0, 0, tiled=True, axis_index_groups=groups)]
where the time goes in v7:
time: 172 us; the launch traced here: 171 us
  blocking collectives  141 us (82%)
  Pallas kernels  15.6 us (9%)
  waiting for transfers between devices  7.21 us (4%)
  starting transfers between devices  4.99 us (3%)
    all_to_all x8, blocking collectives, exchanged(): lax.all_to_all(pieces, axis, 0, 0, tiled=True, axis_index_groups=groups)  141 us
    pallas_call x6, Pallas kernels, call(): pl.pallas_call(kernel, out_shape=outs, in_specs=ins or [VMEM] * len(args)...  15.6 us
    all_to_all x1, waiting for transfers between devices, exchanged(): lax.all_to_all(pieces, axis, 0, 0, tiled=True, axis_index_groups=groups)  7.21 us
    all_to_all x1, starting transfers between devices, exchanged(): lax.all_to_all(pieces, axis, 0, 0, tiled=True, axis_index_groups=groups)  4.99 us
  transfers between devices with their start and end apart: 1, of which 1 were waited for; matrix products, arithmetic and copies ran while one was open for 0% of the time, Pallas kernels for 0%

profile of v7, /device:TPU:1, one launch (start us, length us, event | category | flops | bytes accessed | tf_op | source)
XLA Modules:
  0.0 171.5 jit_solution(16480935615135694852)
XLA Ops:
  0.6 6.6 %shard_map.58 = (f32[512,1024]{1,0:T(8,128)S(1)}, bf16[1024,2048]{1,0:T(8,128)(2,1)S(1)}, f32[512,128]{1,0:T(8,128)S(1)}, f32[16,16,128]{2,1,0:T(8,128)S(1)}) custom-call(bf16[1024,2048]{1,0:T(8,128)(2,1)} %images.1, bf16[512,2048]{1,0:T(8,128)(2,1)} %references.1, f32[8,128]{1,0:T(8,128)} %bitcast.11), custom_call_target="tpu_custom_call" | custom-call | flops 2147483648 | bytes 4194304 | tf_op jit(solution)/shard_map/pallas_call | solution.py:243
  7.2 0.0 copy-start
  7.2 20.8 %all_to_all.45.received = f32[16,16,128]{2,1,0:T(8,128)S(1)} all-to-all(f32[16,16,128]{2,1,0:T(8,128)S(1)} %get-tuple-element.11), channel_id=1, replica_groups=mesh['img'=32,'ref'=16] {'ref'}, dimensions={0} | all-to-all | bytes 262144 | tf_op jit(solution)/shard_map/all_to_all | solution.py:60
  28.0 1.1 shard_map.59
  29.1 11.6 %all_to_all.46.received = f32[16,16,128]{2,1,0:T(8,128)S(1)} all-to-all(f32[16,16,128]{2,1,0:T(8,128)S(1)} %shard_map.59), channel_id=1, replica_groups=mesh['img'=32,'ref'=16] {'ref'}, dimensions={0} | all-to-all | bytes 262144 | tf_op jit(solution)/shard_map/all_to_all | solution.py:60
  40.7 1.1 shard_map.60
  41.8 11.6 %all_to_all.47.received = f32[16,16,128]{2,1,0:T(8,128)S(1)} all-to-all(f32[16,16,128]{2,1,0:T(8,128)S(1)} %shard_map.60), channel_id=1, replica_groups=mesh['img'=32,'ref'=16] {'ref'}, dimensions={0} | all-to-all | bytes 262144 | tf_op jit(solution)/shard_map/all_to_all | solution.py:60
  53.4 0.8 shard_map.61
  54.2 10.2 %all_to_all.48.received = f32[16,8,128]{2,1,0:T(8,128)S(1)} all-to-all(f32[16,8,128]{2,1,0:T(8,128)S(1)} %get-tuple-element.15), channel_id=1, replica_groups=mesh['img'=32,'ref'=16] {'ref'}, dimensions={0} | all-to-all | bytes 131072 | tf_op jit(solution)/shard_map/all_to_all | solution.py:60
  64.4 2.4 %shard_map.62 = bf16[512,2048]{1,0:T(8,128)(2,1)S(1)} custom-call(f32[16,8,128]{2,1,0:T(8,128)S(1)} %all_to_all.48.received, f32[512,1024]{1,0:T(8,128)S(1)} %get-tuple-element.12.cross, f32[512,128]{1,0:T(8,128)S(1)} %get-tuple-element.13.norms, f32[8,128]{1,0:T(8,128)S(1)} %get-tuple-element.16.contrast, bf16[1024,2048]{1,0:T(8,128)(2,1)S(1)} %get-tuple-element.14.images), custom_call_target="tpu_custom_call" | custom-call | flops 2147483648 | bytes 4194304 | tf_op jit(solution)/shard_map/pallas_call | solution.py:243
  66.8 20.5 %all_to_all.49 = bf16[4,128,2048]{2,1,0:T(8,128)(2,1)S(1)} all-to-all(bf16[4,128,2048]{2,1,0:T(8,128)(2,1)S(1)} %bitcast.9), channel_id=1, replica_groups={{0,16,128,144},{32,48,160,176},{64,80,192,208},{96,112,224,240},{256,27..., dimensions={0} | all-to-all | bytes 4194304 | tf_op jit(solution)/shard_map/all_to_all | solution.py:60
  87.3 0.4 reduce_sum.39
  87.8 23.1 %all_to_all.50 = bf16[8,16,2048]{2,1,0:T(8,128)(2,1)S(1)} all-to-all(bf16[8,16,2048]{2,1,0:T(8,128)(2,1)S(1)} %bitcast.14), channel_id=1, replica_groups={{0,32,64,96,256,288,320,352},{16,48,80,112,272,304,336,368},{128,160,19..., dimensions={0} | all-to-all | bytes 1048576 | tf_op jit(solution)/shard_map/all_to_all | solution.py:60
  110.9 0.1 convert_reduce_fusion
  110.9 0.1 multiply_reduce_fusion
  111.1 0.1 multiply_convert_fusion
  111.2 10.7 %all_to_all.51 = bf16[4,16,2048]{2,1,0:T(8,128)(2,1)S(1)} all-to-all(bf16[4,16,2048]{2,1,0:T(8,128)(2,1)S(1)} %broadcast_in_dim.6), channel_id=1, replica_groups={{0,32,64,96},{256,288,320,352},{16,48,80,112},{272,304,336,368},{128,16..., dimensions={0} | all-to-all | bytes 524288 | tf_op jit(solution)/shard_map/all_to_all | solution.py:60
  121.9 0.2 broadcast_in_dim.8
  122.2 32.2 %all_to_all.52 = bf16[8,64,2048]{2,1,0:T(8,128)(2,1)S(1)} all-to-all(bf16[8,64,2048]{2,1,0:T(8,128)(2,1)S(1)} %broadcast_in_dim.8), channel_id=1, replica_groups={{0,256,16,272,128,384,144,400},{32,288,48,304,160,416,176,432},{64,320,..., dimensions={0} | all-to-all | bytes 4194304 | tf_op jit(solution)/shard_map/all_to_all | solution.py:60
  154.3 3.7 %shard_map.63 = (f32[16,8,128]{2,1,0:T(8,128)}, bf16[512,2048]{1,0:T(8,128)(2,1)}) custom-call(bf16[512,2048]{1,0:T(8,128)(2,1)S(1)} %bitcast.10, bf16[1024,2048]{1,0:T(8,128)(2,1)S(1)} %copy-done.1, f32[8,128]{1,0:T(8,128)S(1)} %get-tuple-element.16.contrast), custom_call_target="tpu_custom_call" | custom-call | flops 2147483648 | bytes 4194304 | tf_op jit(solution)/shard_map/pallas_call | solution.py:243
  158.0 5.0 %all-to-all-start.8 = ((f32[16,8,128]{2,1,0:T(8,128)}), f32[16,8,128]{2,1,0:T(8,128)S(1)}, u32[]{:S(2)}, u32[]{:S(2)}) async-start(f32[16,8,128]{2,1,0:T(8,128)} %get-tuple-element.18), calls=%async_computation.8 | async-start | bytes 131072 | tf_op jit(solution)/shard_map/all_to_all | solution.py:60
  163.0 0.6 copy.6
  163.6 7.2 %all-to-all-done.8 = f32[16,8,128]{2,1,0:T(8,128)S(1)} async-done(((f32[16,8,128]{2,1,0:T(8,128)}), f32[16,8,128]{2,1,0:T(8,128)S(1)}, u32[]{:S(2)}, u32[]{:S(2)}) %all-to-all-start.8) | async-done | bytes 65568 | tf_op jit(solution)/shard_map/all_to_all | solution.py:60
  170.9 0.6 add_bitcast_fusion
  (9 shorter events, 0.1 us)
Async XLA Ops:
  0.6 27.4 %copy-start.2 = (f32[1024]{0:T(1024)S(1)}, f32[1024]{0:T(1024)}, u32[]{:S(2)}) copy-start(f32[1024]{0:T(1024)} %param.5) | copy-start | bytes 12292
  7.2 57.2 %copy-start = (bf16[1024,2048]{1,0:T(8,128)(2,1)}, bf16[1024,2048]{1,0:T(8,128)(2,1)S(1)}, u32[]{:S(2)}) copy-start(bf16[1024,2048]{1,0:T(8,128)(2,1)S(1)} %get-tuple-element.14.images) | copy-start | bytes 12582916
  122.1 32.2 %copy-start.1 = (bf16[1024,2048]{1,0:T(8,128)(2,1)S(1)}, bf16[1024,2048]{1,0:T(8,128)(2,1)}, u32[]{:S(2)}) copy-start(bf16[1024,2048]{1,0:T(8,128)(2,1)} %copy-done) | copy-start | bytes 12582916
  158.0 12.8 %all-to-all-start.8 = ((f32[16,8,128]{2,1,0:T(8,128)}), f32[16,8,128]{2,1,0:T(8,128)S(1)}, u32[]{:S(2)}, u32[]{:S(2)}) async-start(f32[16,8,128]{2,1,0:T(8,128)} %get-tuple-element.18), calls=%async_computation.8 | async-start | bytes 131072 | tf_op jit(solution)/shard_map/all_to_all | solution.py:60

commit v8 on v6

--- a/solution.py
+++ b/solution.py
@@ -23,18 +23,15 @@
 
 
 SIDES = [(a, b) for a in range(2) for b in range(2)]
-PLACES = [(2 * i, 2 * j) for i in range(X // 2) for j in range(Y // 2)]
-CORNERS = [(ref, ref % CORES) for ref in range(Z * CORES)]
+REFS = range(Z * CORES)
 BLOCKS = [
-    [device(x + a + core, y + b + core, ref) for a, b in SIDES]
-    for ref, core in CORNERS
-    for x, y in PLACES
+    [device(2 * i + a + ref % CORES, 2 * j + b + ref % CORES, ref) for a, b in SIDES]
+    for ref in REFS
+    for i in range(X // 2)
+    for j in range(Y // 2)
 ]
-SPREAD = [
-    [device(x + a + core, y + b + core, ref) for x, y in PLACES]
-    for ref, core in CORNERS
-    for a, b in SIDES
-]
+ORDER = [(k % 2, (k // 2 + k % 2 * 2) % 4) for k in range(X * Y // 4)]
+SPREAD = [[device(2 * i + a, 2 * j + b, ref) for i, j in ORDER] for ref in REFS for a, b in SIDES]
 
 
 def exchanged(pieces, axis, groups=None):

time: 171 us -> 168 us (0.982)
  starting transfers between devices: 7.14 us -> 3.4 us
    all_to_all x1, starting transfers between devices: 7.14 us -> 3.4 us  [exchanged(): lax.all_to_all(pieces, axis, 0, 0, tiled=True, axis_index_groups=groups)]
where the time goes in v8:
time: 168 us; the launch traced here: 167 us
  blocking collectives  138 us (82%)
  Pallas kernels  15.6 us (9%)
  waiting for transfers between devices  7.08 us (4%)
  starting transfers between devices  3.4 us (2%)
    all_to_all x8, blocking collectives, exchanged(): lax.all_to_all(pieces, axis, 0, 0, tiled=True, axis_index_groups=groups)  138 us
    pallas_call x6, Pallas kernels, call(): pl.pallas_call(kernel, out_shape=outs, in_specs=ins or [VMEM] * len(args)...  15.6 us
    all_to_all x1, waiting for transfers between devices, exchanged(): lax.all_to_all(pieces, axis, 0, 0, tiled=True, axis_index_groups=groups)  7.08 us
    all_to_all x1, starting transfers between devices, exchanged(): lax.all_to_all(pieces, axis, 0, 0, tiled=True, axis_index_groups=groups)  3.4 us
  transfers between devices with their start and end apart: 1, of which 1 were waited for; matrix products, arithmetic and copies ran while one was open for 0% of the time, Pallas kernels for 0%

profile of v8, /device:TPU:1, one launch (start us, length us, event | category | flops | bytes accessed | tf_op | source)
XLA Modules:
  0.0 167.1 jit_solution(11218828989867860197)
XLA Ops:
  0.6 6.6 %shard_map.58 = (f32[512,1024]{1,0:T(8,128)S(1)}, bf16[1024,2048]{1,0:T(8,128)(2,1)S(1)}, f32[512,128]{1,0:T(8,128)S(1)}, f32[16,16,128]{2,1,0:T(8,128)S(1)}) custom-call(bf16[1024,2048]{1,0:T(8,128)(2,1)} %images.1, bf16[512,2048]{1,0:T(8,128)(2,1)} %references.1, f32[8,128]{1,0:T(8,128)} %bitcast.11), custom_call_target="tpu_custom_call" | custom-call | flops 2147483648 | bytes 4194304 | tf_op jit(solution)/shard_map/pallas_call | solution.py:221
  7.2 20.8 %all_to_all.45.received = f32[16,16,128]{2,1,0:T(8,128)S(1)} all-to-all(f32[16,16,128]{2,1,0:T(8,128)S(1)} %get-tuple-element.11), channel_id=1, replica_groups=mesh['img'=32,'ref'=16] {'ref'}, dimensions={0} | all-to-all | bytes 262144 | tf_op jit(solution)/shard_map/all_to_all | solution.py:38
  28.0 1.1 shard_map.59
  29.1 11.6 %all_to_all.46.received = f32[16,16,128]{2,1,0:T(8,128)S(1)} all-to-all(f32[16,16,128]{2,1,0:T(8,128)S(1)} %shard_map.59), channel_id=1, replica_groups=mesh['img'=32,'ref'=16] {'ref'}, dimensions={0} | all-to-all | bytes 262144 | tf_op jit(solution)/shard_map/all_to_all | solution.py:38
  40.7 1.1 shard_map.60
  41.8 11.6 %all_to_all.47.received = f32[16,16,128]{2,1,0:T(8,128)S(1)} all-to-all(f32[16,16,128]{2,1,0:T(8,128)S(1)} %shard_map.60), channel_id=1, replica_groups=mesh['img'=32,'ref'=16] {'ref'}, dimensions={0} | all-to-all | bytes 262144 | tf_op jit(solution)/shard_map/all_to_all | solution.py:38
  53.4 0.8 shard_map.61
  54.2 10.2 %all_to_all.48.received = f32[16,8,128]{2,1,0:T(8,128)S(1)} all-to-all(f32[16,8,128]{2,1,0:T(8,128)S(1)} %get-tuple-element.15), channel_id=1, replica_groups=mesh['img'=32,'ref'=16] {'ref'}, dimensions={0} | all-to-all | bytes 131072 | tf_op jit(solution)/shard_map/all_to_all | solution.py:38
  64.4 2.4 %shard_map.62 = bf16[512,2048]{1,0:T(8,128)(2,1)S(1)} custom-call(f32[16,8,128]{2,1,0:T(8,128)S(1)} %all_to_all.48.received, f32[512,1024]{1,0:T(8,128)S(1)} %get-tuple-element.12.cross, f32[512,128]{1,0:T(8,128)S(1)} %get-tuple-element.13.norms, f32[8,128]{1,0:T(8,128)S(1)} %get-tuple-element.16.contrast, bf16[1024,2048]{1,0:T(8,128)(2,1)S(1)} %get-tuple-element.14.images), custom_call_target="tpu_custom_call" | custom-call | flops 2147483648 | bytes 4194304 | tf_op jit(solution)/shard_map/pallas_call | solution.py:221
  66.8 20.5 %all_to_all.49 = bf16[4,128,2048]{2,1,0:T(8,128)(2,1)S(1)} all-to-all(bf16[4,128,2048]{2,1,0:T(8,128)(2,1)S(1)} %bitcast.9), channel_id=1, replica_groups={{0,16,128,144},{32,48,160,176},{64,80,192,208},{96,112,224,240},{256,27..., dimensions={0} | all-to-all | bytes 4194304 | tf_op jit(solution)/shard_map/all_to_all | solution.py:38
  87.3 0.4 reduce_sum.39
  87.8 22.9 %all_to_all.50 = bf16[8,16,2048]{2,1,0:T(8,128)(2,1)S(1)} all-to-all(bf16[8,16,2048]{2,1,0:T(8,128)(2,1)S(1)} %bitcast.15), channel_id=1, replica_groups={{0,320,32,352,64,256,96,288},{16,336,48,368,80,272,112,304},{128,448,16..., dimensions={0} | all-to-all | bytes 1048576 | tf_op jit(solution)/shard_map/all_to_all | solution.py:38
  110.6 0.1 convert_reduce_fusion
  110.7 0.1 multiply_reduce_fusion
  110.8 0.1 multiply_convert_fusion
  110.9 0.1 broadcast_in_dim.6
  111.0 17.6 %all_to_all.51 = bf16[8,16,2048]{2,1,0:T(8,128)(2,1)S(1)} all-to-all(bf16[8,16,2048]{2,1,0:T(8,128)(2,1)S(1)} %broadcast_in_dim.6), channel_id=1, replica_groups={{0,320,32,352,64,256,96,288},{16,336,48,368,80,272,112,304},{128,448,16..., dimensions={0} | all-to-all | bytes 1048576 | tf_op jit(solution)/shard_map/all_to_all | solution.py:38
  128.6 0.2 broadcast_in_dim.8
  128.9 22.8 %all_to_all.52 = bf16[4,128,2048]{2,1,0:T(8,128)(2,1)S(1)} all-to-all(bf16[4,128,2048]{2,1,0:T(8,128)(2,1)S(1)} %broadcast_in_dim.8), channel_id=1, replica_groups={{0,16,128,144},{32,48,160,176},{64,80,192,208},{96,112,224,240},{256,27..., dimensions={0} | all-to-all | bytes 4194304 | tf_op jit(solution)/shard_map/all_to_all | solution.py:38
  151.7 3.7 %shard_map.63 = (f32[16,8,128]{2,1,0:T(8,128)}, bf16[512,2048]{1,0:T(8,128)(2,1)}) custom-call(bf16[512,2048]{1,0:T(8,128)(2,1)S(1)} %bitcast.10, bf16[1024,2048]{1,0:T(8,128)(2,1)S(1)} %copy-done.1, f32[8,128]{1,0:T(8,128)S(1)} %get-tuple-element.16.contrast), custom_call_target="tpu_custom_call" | custom-call | flops 2147483648 | bytes 4194304 | tf_op jit(solution)/shard_map/pallas_call | solution.py:221
  155.4 3.4 %all-to-all-start.8 = ((f32[16,8,128]{2,1,0:T(8,128)}), f32[16,8,128]{2,1,0:T(8,128)S(1)}, u32[]{:S(2)}, u32[]{:S(2)}) async-start(f32[16,8,128]{2,1,0:T(8,128)} %get-tuple-element.18), calls=%async_computation.8 | async-start | bytes 131072 | tf_op jit(solution)/shard_map/all_to_all | solution.py:38
  158.8 0.6 copy.6
  159.4 7.1 %all-to-all-done.8 = f32[16,8,128]{2,1,0:T(8,128)S(1)} async-done(((f32[16,8,128]{2,1,0:T(8,128)}), f32[16,8,128]{2,1,0:T(8,128)S(1)}, u32[]{:S(2)}, u32[]{:S(2)}) %all-to-all-start.8) | async-done | bytes 65568 | tf_op jit(solution)/shard_map/all_to_all | solution.py:38
  166.5 0.6 add_bitcast_fusion
  (9 shorter events, 0.1 us)
Async XLA Ops:
  0.6 27.4 %copy-start.2 = (f32[1024]{0:T(1024)S(1)}, f32[1024]{0:T(1024)}, u32[]{:S(2)}) copy-start(f32[1024]{0:T(1024)} %param.5) | copy-start | bytes 12292
  7.2 57.2 %copy-start = (bf16[1024,2048]{1,0:T(8,128)(2,1)}, bf16[1024,2048]{1,0:T(8,128)(2,1)S(1)}, u32[]{:S(2)}) copy-start(bf16[1024,2048]{1,0:T(8,128)(2,1)S(1)} %get-tuple-element.14.images) | copy-start | bytes 12582916
  128.9 22.8 %copy-start.1 = (bf16[1024,2048]{1,0:T(8,128)(2,1)S(1)}, bf16[1024,2048]{1,0:T(8,128)(2,1)}, u32[]{:S(2)}) copy-start(bf16[1024,2048]{1,0:T(8,128)(2,1)} %copy-done) | copy-start | bytes 12582916
  155.4 11.1 %all-to-all-start.8 = ((f32[16,8,128]{2,1,0:T(8,128)}), f32[16,8,128]{2,1,0:T(8,128)S(1)}, u32[]{:S(2)}, u32[]{:S(2)}) async-start(f32[16,8,128]{2,1,0:T(8,128)} %get-tuple-element.18), calls=%async_computation.8 | async-start | bytes 131072 | tf_op jit(solution)/shard_map/all_to_all | solution.py:38

commit v9 on v8

--- a/solution.py
+++ b/solution.py
@@ -30,7 +30,7 @@
     for i in range(X // 2)
     for j in range(Y // 2)
 ]
-ORDER = [(k % 2, (k // 2 + k % 2 * 2) % 4) for k in range(X * Y // 4)]
+ORDER = [(k % 2, j) for k, j in enumerate((0, 1, 1, 3, 2, 2, 3, 0))]
 SPREAD = [[device(2 * i + a, 2 * j + b, ref) for i, j in ORDER] for ref in REFS for a, b in SIDES]
 
 

time: 168 us -> 168 us (level)
  no operation moved by 1% of the time
where the time goes in v9:
time: 168 us
  blocking collectives  137 us (82%)
  Pallas kernels  15.6 us (9%)
  waiting for transfers between devices  7.24 us (4%)
  starting transfers between devices  4.39 us (3%)
    all_to_all x8, blocking collectives, exchanged(): lax.all_to_all(pieces, axis, 0, 0, tiled=True, axis_index_groups=groups)  137 us
    pallas_call x6, Pallas kernels, call(): pl.pallas_call(kernel, out_shape=outs, in_specs=ins or [VMEM] * len(args)...  15.6 us
    all_to_all x1, waiting for transfers between devices, exchanged(): lax.all_to_all(pieces, axis, 0, 0, tiled=True, axis_index_groups=groups)  7.24 us
    all_to_all x1, starting transfers between devices, exchanged(): lax.all_to_all(pieces, axis, 0, 0, tiled=True, axis_index_groups=groups)  4.39 us
  transfers between devices with their start and end apart: 1, of which 1 were waited for; matrix products, arithmetic and copies ran while one was open for 0% of the time, Pallas kernels for 0%

profile of v9, /device:TPU:1, one launch (start us, length us, event | category | flops | bytes accessed | tf_op | source)
XLA Modules:
  0.0 167.6 jit_solution(18408233883748306517)
XLA Ops:
  0.6 6.6 %shard_map.58 = (f32[512,1024]{1,0:T(8,128)S(1)}, bf16[1024,2048]{1,0:T(8,128)(2,1)S(1)}, f32[512,128]{1,0:T(8,128)S(1)}, f32[16,16,128]{2,1,0:T(8,128)S(1)}) custom-call(bf16[1024,2048]{1,0:T(8,128)(2,1)} %images.1, bf16[512,2048]{1,0:T(8,128)(2,1)} %references.1, f32[8,128]{1,0:T(8,128)} %bitcast.11), custom_call_target="tpu_custom_call" | custom-call | flops 2147483648 | bytes 4194304 | tf_op jit(solution)/shard_map/pallas_call | solution.py:221
  7.2 20.8 %all_to_all.45.received = f32[16,16,128]{2,1,0:T(8,128)S(1)} all-to-all(f32[16,16,128]{2,1,0:T(8,128)S(1)} %get-tuple-element.11), channel_id=1, replica_groups=mesh['img'=32,'ref'=16] {'ref'}, dimensions={0} | all-to-all | bytes 262144 | tf_op jit(solution)/shard_map/all_to_all | solution.py:38
  28.0 1.1 shard_map.59
  29.1 11.6 %all_to_all.46.received = f32[16,16,128]{2,1,0:T(8,128)S(1)} all-to-all(f32[16,16,128]{2,1,0:T(8,128)S(1)} %shard_map.59), channel_id=1, replica_groups=mesh['img'=32,'ref'=16] {'ref'}, dimensions={0} | all-to-all | bytes 262144 | tf_op jit(solution)/shard_map/all_to_all | solution.py:38
  40.7 1.1 shard_map.60
  41.8 11.6 %all_to_all.47.received = f32[16,16,128]{2,1,0:T(8,128)S(1)} all-to-all(f32[16,16,128]{2,1,0:T(8,128)S(1)} %shard_map.60), channel_id=1, replica_groups=mesh['img'=32,'ref'=16] {'ref'}, dimensions={0} | all-to-all | bytes 262144 | tf_op jit(solution)/shard_map/all_to_all | solution.py:38
  53.4 0.8 shard_map.61
  54.2 10.2 %all_to_all.48.received = f32[16,8,128]{2,1,0:T(8,128)S(1)} all-to-all(f32[16,8,128]{2,1,0:T(8,128)S(1)} %get-tuple-element.15), channel_id=1, replica_groups=mesh['img'=32,'ref'=16] {'ref'}, dimensions={0} | all-to-all | bytes 131072 | tf_op jit(solution)/shard_map/all_to_all | solution.py:38
  64.4 2.4 %shard_map.62 = bf16[512,2048]{1,0:T(8,128)(2,1)S(1)} custom-call(f32[16,8,128]{2,1,0:T(8,128)S(1)} %all_to_all.48.received, f32[512,1024]{1,0:T(8,128)S(1)} %get-tuple-element.12.cross, f32[512,128]{1,0:T(8,128)S(1)} %get-tuple-element.13.norms, f32[8,128]{1,0:T(8,128)S(1)} %get-tuple-element.16.contrast, bf16[1024,2048]{1,0:T(8,128)(2,1)S(1)} %get-tuple-element.14.images), custom_call_target="tpu_custom_call" | custom-call | flops 2147483648 | bytes 4194304 | tf_op jit(solution)/shard_map/pallas_call | solution.py:221
  66.8 20.5 %all_to_all.49 = bf16[4,128,2048]{2,1,0:T(8,128)(2,1)S(1)} all-to-all(bf16[4,128,2048]{2,1,0:T(8,128)(2,1)S(1)} %bitcast.9), channel_id=1, replica_groups={{0,16,128,144},{32,48,160,176},{64,80,192,208},{96,112,224,240},{256,27..., dimensions={0} | all-to-all | bytes 4194304 | tf_op jit(solution)/shard_map/all_to_all | solution.py:38
  87.3 0.4 reduce_sum.39
  87.8 22.0 %all_to_all.50 = bf16[8,16,2048]{2,1,0:T(8,128)(2,1)S(1)} all-to-all(bf16[8,16,2048]{2,1,0:T(8,128)(2,1)S(1)} %bitcast.15), channel_id=1, replica_groups={{0,288,32,352,64,320,96,256},{16,304,48,368,80,336,112,272},{128,416,16..., dimensions={0} | all-to-all | bytes 1048576 | tf_op jit(solution)/shard_map/all_to_all | solution.py:38
  109.8 0.1 convert_reduce_fusion
  109.8 0.1 multiply_reduce_fusion
  110.0 0.1 multiply_convert_fusion
  110.0 0.1 broadcast_in_dim.6
  110.1 18.1 %all_to_all.51 = bf16[8,16,2048]{2,1,0:T(8,128)(2,1)S(1)} all-to-all(bf16[8,16,2048]{2,1,0:T(8,128)(2,1)S(1)} %broadcast_in_dim.6), channel_id=1, replica_groups={{0,288,32,352,64,320,96,256},{16,304,48,368,80,336,112,272},{128,416,16..., dimensions={0} | all-to-all | bytes 1048576 | tf_op jit(solution)/shard_map/all_to_all | solution.py:38
  128.2 0.2 broadcast_in_dim.8
  128.5 22.5 %all_to_all.52 = bf16[4,128,2048]{2,1,0:T(8,128)(2,1)S(1)} all-to-all(bf16[4,128,2048]{2,1,0:T(8,128)(2,1)S(1)} %broadcast_in_dim.8), channel_id=1, replica_groups={{0,16,128,144},{32,48,160,176},{64,80,192,208},{96,112,224,240},{256,27..., dimensions={0} | all-to-all | bytes 4194304 | tf_op jit(solution)/shard_map/all_to_all | solution.py:38
  151.1 3.7 %shard_map.63 = (f32[16,8,128]{2,1,0:T(8,128)}, bf16[512,2048]{1,0:T(8,128)(2,1)}) custom-call(bf16[512,2048]{1,0:T(8,128)(2,1)S(1)} %bitcast.10, bf16[1024,2048]{1,0:T(8,128)(2,1)S(1)} %copy-done.1, f32[8,128]{1,0:T(8,128)S(1)} %get-tuple-element.16.contrast), custom_call_target="tpu_custom_call" | custom-call | flops 2147483648 | bytes 4194304 | tf_op jit(solution)/shard_map/pallas_call | solution.py:221
  154.8 4.4 %all-to-all-start.8 = ((f32[16,8,128]{2,1,0:T(8,128)}), f32[16,8,128]{2,1,0:T(8,128)S(1)}, u32[]{:S(2)}, u32[]{:S(2)}) async-start(f32[16,8,128]{2,1,0:T(8,128)} %get-tuple-element.18), calls=%async_computation.8 | async-start | bytes 131072 | tf_op jit(solution)/shard_map/all_to_all | solution.py:38
  159.1 0.6 copy.6
  159.7 7.2 %all-to-all-done.8 = f32[16,8,128]{2,1,0:T(8,128)S(1)} async-done(((f32[16,8,128]{2,1,0:T(8,128)}), f32[16,8,128]{2,1,0:T(8,128)S(1)}, u32[]{:S(2)}, u32[]{:S(2)}) %all-to-all-start.8) | async-done | bytes 65568 | tf_op jit(solution)/shard_map/all_to_all | solution.py:38
  167.0 0.6 add_bitcast_fusion
  (9 shorter events, 0.1 us)
Async XLA Ops:
  0.6 27.4 %copy-start.2 = (f32[1024]{0:T(1024)S(1)}, f32[1024]{0:T(1024)}, u32[]{:S(2)}) copy-start(f32[1024]{0:T(1024)} %param.5) | copy-start | bytes 12292
  7.2 57.2 %copy-start = (bf16[1024,2048]{1,0:T(8,128)(2,1)}, bf16[1024,2048]{1,0:T(8,128)(2,1)S(1)}, u32[]{:S(2)}) copy-start(bf16[1024,2048]{1,0:T(8,128)(2,1)S(1)} %get-tuple-element.14.images) | copy-start | bytes 12582916
  128.5 22.5 %copy-start.1 = (bf16[1024,2048]{1,0:T(8,128)(2,1)S(1)}, bf16[1024,2048]{1,0:T(8,128)(2,1)}, u32[]{:S(2)}) copy-start(bf16[1024,2048]{1,0:T(8,128)(2,1)} %copy-done) | copy-start | bytes 12582916
  154.8 12.2 %all-to-all-start.8 = ((f32[16,8,128]{2,1,0:T(8,128)}), f32[16,8,128]{2,1,0:T(8,128)S(1)}, u32[]{:S(2)}, u32[]{:S(2)}) async-start(f32[16,8,128]{2,1,0:T(8,128)} %get-tuple-element.18), calls=%async_computation.8 | async-start | bytes 131072 | tf_op jit(solution)/shard_map/all_to_all | solution.py:38

commit v10 on v8

--- a/solution.py
+++ b/solution.py
@@ -51,10 +51,18 @@
     return partial
 
 
-def gathered_rows(share):
-    for groups in (SPREAD, BLOCKS):
-        share = sent_to_all(share, PLANE, groups).reshape(-1, share.shape[-1])
-    return share
+WAYS = ((1, 0), (0, 1), (1, 1))
+
+
+def toward(along_x, along_y):
+    pairs = []
+    for ref in REFS:
+        for x in range(X):
+            for y in range(Y):
+                a, b = (x + ref) % 2, (y + ref) % 2
+                to = device(x + along_x * (1 - 2 * a), y + along_y * (1 - 2 * b), ref)
+                pairs.append((device(x, y, ref), to))
+    return pairs
 
 
 def normalize(sums):
@@ -200,17 +208,48 @@
         ).astype(jnp.bfloat16)
 
 
-def score_kernel(gathered, images, contrast, out, result, norms, semaphore):
-    copy = pltpu.make_async_copy(gathered, result, semaphore)
-    copy.start()
-    width = gathered.shape[1]
-    squares(gathered, norms, 1.0 / width)
+def scored_rows(piece, images, contrast, norms):
+    width = piece.shape[1]
+    squares(piece, norms, 1.0 / width)
     logs = []
     for k in range(images.shape[0] // BLOCK):
-        terms = product(gathered, images, k) * width**-0.5
+        terms = product(piece, images, k) * width**-0.5
         logs.append(own_total(terms, norms, laid_out(contrast, k)))
-    send(out, logs)
-    copy.wait()
+    return folded(logs)
+
+
+def score_kernel(piece, images, contrast, out, norms):
+    out[...] = scored_rows(piece, images, contrast, norms)
+
+
+def pair_kernel(first, second, images, contrast, before, out, norms):
+    logs = [before[...]]
+    logs += [scored_rows(piece, images, contrast, norms) for piece in (first, second)]
+    out[...] = combined_log(jnp.stack(logs))
+
+
+def last_kernel(own, first, second, last, images, contrast, before, out, result, norms, semaphores):
+    image, ref = lax.axis_index("img"), lax.axis_index("ref")
+    a = lax.rem(lax.div(image, Y) + ref, 2)
+    b = lax.rem(lax.rem(image, Y) + ref, 2)
+    rows = own.shape[0]
+    copies = []
+    for k, (piece, side) in enumerate(
+        (
+            (own, a * 2 + b),
+            (first, (1 - a) * 2 + b),
+            (second, a * 2 + 1 - b),
+            (last, (1 - a) * 2 + 1 - b),
+        )
+    ):
+        place = pl.ds(pl.multiple_of(side * rows, rows), rows)
+        copies.append(pltpu.make_async_copy(piece, result.at[place], semaphores.at[k]))
+    for copy in copies:
+        copy.start()
+    logs = scored_rows(last, images, contrast, norms)
+    out[...] = jnp.broadcast_to(combined_log(jnp.stack([before[...], logs]))[None], out.shape)
+    for copy in copies:
+        copy.wait()
 
 
 VMEM = pl.BlockSpec(memory_space=pltpu.VMEM)
@@ -279,19 +318,28 @@
         scratch=[pltpu.VMEM((refs, count), bf16)],
         flops=flops,
     )
-    gathered = gathered_rows(normalize(summed_share(img_partial)))
+    share = normalize(summed_share(img_partial))
+    rows = sent_to_all(share, PLANE, SPREAD).reshape(-1, width)
+    first, second, last = (lax.ppermute(rows, PLANE, toward(*way)) for way in WAYS)
+    norm = [pltpu.VMEM((rows.shape[0], LANES), f32)]
+    log = (pltpu.VMEM(per_image, f32),)
+    (before,) = call(score_kernel, log, rows, kept, contrast, scratch=norm, flops=flops // 4)
+    (before,) = call(
+        pair_kernel, log, first, second, kept, contrast, before, scratch=norm, flops=flops // 2
+    )
     own, new_references = call(
-        score_kernel,
+        last_kernel,
         (one, jax.ShapeDtypeStruct((refs, width), bf16)),
-        gathered,
+        rows,
+        first,
+        second,
+        last,
         kept,
         contrast,
+        before,
         specs=(VMEM, HBM),
-        scratch=[
-            pltpu.VMEM((refs, LANES), f32),
-            pltpu.SemaphoreType.DMA,
-        ],
-        flops=flops,
+        scratch=[*norm, pltpu.SemaphoreType.DMA((4,))],
+        flops=flops // 4,
     )
     loglik = combined_log(exchanged(own, "ref")) - math.log(refs * devices)
     return (new_references, contrast.reshape(count), loglik.reshape(count))

time: 168 us -> 169 us (level)
  blocking collectives: 138 us -> 115 us
  starting transfers between devices: 3.4 us -> 18.1 us
  Pallas kernels: 15.6 us -> 19.9 us
  waiting for transfers between devices: 7.08 us -> 9.59 us
  local copies, waits for them, and re-layouts: 0.91 us -> 2.84 us
    all_to_all x8 -> x7, blocking collectives: 138 us -> 115 us  [exchanged(): lax.all_to_all(pieces, axis, 0, 0, tiled=True, axis_index_groups=groups)]
    ppermute x0 -> x3, starting transfers between devices: none -> 14.7 us  [per_device(): lax.ppermute(rows, PLANE, toward(*way))]
    pallas_call x6 -> x8, Pallas kernels: 15.6 us -> 19.9 us  [call(): pl.pallas_call(kernel, out_shape=outs, in_specs=ins or [VMEM] * len(args)...]
    ppermute x0 -> x3, waiting for transfers between devices: none -> 3.21 us  [per_device(): lax.ppermute(rows, PLANE, toward(*way))]
    unnamed x7, local copies, waits for them, and re-layouts: 0.61 us -> 2.78 us
  transfers between devices with their start and end apart: 1 -> 4, of which waited for: 1 -> 3; matrix products, arithmetic and copies ran while one was open for 0% -> 0% of each run, Pallas kernels for 0% -> 3%
where the time goes in v10:
time: 169 us; the launch traced here: 168 us
  blocking collectives  115 us (68%)
  Pallas kernels  19.9 us (12%)
  starting transfers between devices  18.1 us (11%)
  waiting for transfers between devices  9.59 us (6%)
  local copies, waits for them, and re-layouts  2.84 us (2%)
    all_to_all x7, blocking collectives, exchanged(): lax.all_to_all(pieces, axis, 0, 0, tiled=True, axis_index_groups=groups)  115 us
    pallas_call x8, Pallas kernels, call(): pl.pallas_call(kernel, out_shape=outs, in_specs=ins or [VMEM] * len(args)...  19.9 us
    ppermute x3, starting transfers between devices, per_device(): lax.ppermute(rows, PLANE, toward(*way))  14.7 us
    all_to_all x1, waiting for transfers between devices, exchanged(): lax.all_to_all(pieces, axis, 0, 0, tiled=True, axis_index_groups=groups)  6.38 us
    all_to_all x1, starting transfers between devices, exchanged(): lax.all_to_all(pieces, axis, 0, 0, tiled=True, axis_index_groups=groups)  3.4 us
  transfers between devices with their start and end apart: 4, of which 3 were waited for; matrix products, arithmetic and copies ran while one was open for 0% of the time, Pallas kernels for 3%

profile of v10, /device:TPU:1, one launch (start us, length us, event | category | flops | bytes accessed | tf_op | source)
XLA Modules:
  0.0 167.8 jit_solution(228675125543355923)
XLA Ops:
  0.6 6.6 %shard_map.58 = (f32[512,1024]{1,0:T(8,128)S(1)}, bf16[1024,2048]{1,0:T(8,128)(2,1)S(1)}, f32[512,128]{1,0:T(8,128)S(1)}, f32[16,16,128]{2,1,0:T(8,128)S(1)}) custom-call(bf16[1024,2048]{1,0:T(8,128)(2,1)} %images.1, bf16[512,2048]{1,0:T(8,128)(2,1)} %references.1, f32[8,128]{1,0:T(8,128)} %bitcast.14), custom_call_target="tpu_custom_call" | custom-call | flops 2147483648 | bytes 4194304 | tf_op jit(solution)/shard_map/pallas_call | solution.py:260
  7.2 20.8 %all_to_all.40.received = f32[16,16,128]{2,1,0:T(8,128)S(1)} all-to-all(f32[16,16,128]{2,1,0:T(8,128)S(1)} %get-tuple-element.11), channel_id=1, replica_groups=mesh['img'=32,'ref'=16] {'ref'}, dimensions={0} | all-to-all | bytes 262144 | tf_op jit(solution)/shard_map/all_to_all | solution.py:38
  28.0 1.1 shard_map.59
  29.1 11.6 %all_to_all.41.received = f32[16,16,128]{2,1,0:T(8,128)S(1)} all-to-all(f32[16,16,128]{2,1,0:T(8,128)S(1)} %shard_map.59), channel_id=1, replica_groups=mesh['img'=32,'ref'=16] {'ref'}, dimensions={0} | all-to-all | bytes 262144 | tf_op jit(solution)/shard_map/all_to_all | solution.py:38
  40.7 1.1 shard_map.60
  41.8 11.6 %all_to_all.42.received = f32[16,16,128]{2,1,0:T(8,128)S(1)} all-to-all(f32[16,16,128]{2,1,0:T(8,128)S(1)} %shard_map.60), channel_id=1, replica_groups=mesh['img'=32,'ref'=16] {'ref'}, dimensions={0} | all-to-all | bytes 262144 | tf_op jit(solution)/shard_map/all_to_all | solution.py:38
  53.4 0.8 shard_map.61
  54.2 10.2 %all_to_all.43.received = f32[16,8,128]{2,1,0:T(8,128)S(1)} all-to-all(f32[16,8,128]{2,1,0:T(8,128)S(1)} %get-tuple-element.15), channel_id=1, replica_groups=mesh['img'=32,'ref'=16] {'ref'}, dimensions={0} | all-to-all | bytes 131072 | tf_op jit(solution)/shard_map/all_to_all | solution.py:38
  64.4 2.4 %shard_map.62 = bf16[512,2048]{1,0:T(8,128)(2,1)S(1)} custom-call(f32[16,8,128]{2,1,0:T(8,128)S(1)} %all_to_all.43.received, f32[512,1024]{1,0:T(8,128)S(1)} %get-tuple-element.12.cross, f32[512,128]{1,0:T(8,128)S(1)} %get-tuple-element.13.norms, f32[8,128]{1,0:T(8,128)S(1)} %get-tuple-element.16.contrast, bf16[1024,2048]{1,0:T(8,128)(2,1)S(1)} %get-tuple-element.14.images), custom_call_target="tpu_custom_call" | custom-call | flops 2147483648 | bytes 4194304 | tf_op jit(solution)/shard_map/pallas_call | solution.py:260
  66.8 20.5 %all_to_all.44 = bf16[4,128,2048]{2,1,0:T(8,128)(2,1)S(1)} all-to-all(bf16[4,128,2048]{2,1,0:T(8,128)(2,1)S(1)} %bitcast.8), channel_id=1, replica_groups={{0,16,128,144},{32,48,160,176},{64,80,192,208},{96,112,224,240},{256,27..., dimensions={0} | all-to-all | bytes 4194304 | tf_op jit(solution)/shard_map/all_to_all | solution.py:38
  87.8 22.9 %all_to_all.45 = bf16[8,16,2048]{2,1,0:T(8,128)(2,1)S(1)} all-to-all(bf16[8,16,2048]{2,1,0:T(8,128)(2,1)S(1)} %bitcast.17), channel_id=1, replica_groups={{0,320,32,352,64,256,96,288},{16,336,48,368,80,272,112,304},{128,448,16..., dimensions={0} | all-to-all | bytes 1048576 | tf_op jit(solution)/shard_map/all_to_all | solution.py:38
  111.0 17.6 %all_to_all.46 = bf16[8,16,2048]{2,1,0:T(8,128)(2,1)S(1)} all-to-all(bf16[8,16,2048]{2,1,0:T(8,128)(2,1)S(1)} %broadcast_in_dim.2), channel_id=1, replica_groups={{0,320,32,352,64,256,96,288},{16,336,48,368,80,272,112,304},{128,448,16..., dimensions={0} | all-to-all | bytes 1048576 | tf_op jit(solution)/shard_map/all_to_all | solution.py:38
  128.6 8.3 %collective-permute-start = (bf16[128,2048]{1,0:T(8,128)(2,1)S(1)}, bf16[128,2048]{1,0:T(8,128)(2,1)S(1)}, u32[]{:S(2)}, u32[]{:S(2)}) collective-permute-start(bf16[128,2048]{1,0:T(8,128)(2,1)S(1)} %bitcast.9), channel_id=1, source_target_pairs={{0,128},{16,144},{32,160},{48,176},{64,192},{80,208},{96,224},{112... | collective-permute-start | bytes 1572872 | tf_op jit(solution)/shard_map/ppermute | solution.py:323
  136.9 1.9 %collective-permute-start.1 = (bf16[128,2048]{1,0:T(8,128)(2,1)S(1)}, bf16[128,2048]{1,0:T(8,128)(2,1)S(1)}, u32[]{:S(2)}, u32[]{:S(2)}) collective-permute-start(bf16[128,2048]{1,0:T(8,128)(2,1)S(1)} %bitcast.10), channel_id=1, source_target_pairs={{0,16},{16,0},{32,48},{48,32},{64,80},{80,64},{96,112},{112,96},{1... | collective-permute-start | bytes 1572872 | tf_op jit(solution)/shard_map/ppermute | solution.py:323
  138.8 4.5 %collective-permute-start.2 = (bf16[128,2048]{1,0:T(8,128)(2,1)S(1)}, bf16[128,2048]{1,0:T(8,128)(2,1)S(1)}, u32[]{:S(2)}, u32[]{:S(2)}) collective-permute-start(bf16[128,2048]{1,0:T(8,128)(2,1)S(1)} %bitcast.11), channel_id=1, source_target_pairs={{0,144},{16,128},{32,176},{48,160},{64,208},{80,192},{96,240},{112... | collective-permute-start | bytes 1572872 | tf_op jit(solution)/shard_map/ppermute | solution.py:323
  143.3 2.2 %copy-done.1 = bf16[1024,2048]{1,0:T(8,128)(2,1)S(1)} copy-done((bf16[1024,2048]{1,0:T(8,128)(2,1)S(1)}, bf16[1024,2048]{1,0:T(8,128)(2,1)}, u32[]{:S(2)}) %copy-start.1) | copy-done | bytes 4194328
  145.5 1.6 shard_map.63.before
  147.1 1.1 collective-permute-done.1.second
  148.2 3.0 %shard_map.64.before = f32[8,128]{1,0:T(8,128)S(1)} custom-call(bf16[128,2048]{1,0:T(8,128)(2,1)S(1)} %collective-permute-done.first, bf16[128,2048]{1,0:T(8,128)(2,1)S(1)} %collective-permute-done.1.second, bf16[1024,2048]{1,0:T(8,128)(2,1)S(1)} %copy-done.1, f32[8,128]{1,0:T(8,128)S(1)} %get-tuple-element.16.contrast, f32[8,128]{1,0:T(8,128)S(1)} %shard_map.63.before), custom_call_target="tpu_custom_call" | custom-call | flops 1073741824 | bytes 4194304 | tf_op jit(solution)/shard_map/pallas_call | solution.py:260
  151.2 2.2 %collective-permute-done.2.last = bf16[128,2048]{1,0:T(8,128)(2,1)S(1)} collective-permute-done((bf16[128,2048]{1,0:T(8,128)(2,1)S(1)}, bf16[128,2048]{1,0:T(8,128)(2,1)S(1)}, u32[]{:S(2)}, u32[]{:S(2)}) %collective-permute-start.2) | collective-permute-done | bytes 524320 | tf_op jit(solution)/shard_map/ppermute | solution.py:323
  153.4 3.3 %shard_map.65 = (f32[16,8,128]{2,1,0:T(8,128)}, bf16[512,2048]{1,0:T(8,128)(2,1)}) custom-call(bf16[128,2048]{1,0:T(8,128)(2,1)S(1)} %bitcast.13, bf16[128,2048]{1,0:T(8,128)(2,1)S(1)} %collective-permute-done.first, bf16[128,2048]{1,0:T(8,128)(2,1)S(1)} %collective-permute-done.1.second, bf16[128,2048]{1,0:T(8,128)(2,1)S(1)} %collective-permute-done.2.last, ...), custom_call_target="tpu_custom_call" | custom-call | flops 536870912 | bytes 4194304 | tf_op jit(solution)/shard_map/pallas_call | solution.py:260
  156.7 3.4 %all-to-all-start.7 = ((f32[16,8,128]{2,1,0:T(8,128)}), f32[16,8,128]{2,1,0:T(8,128)S(1)}, u32[]{:S(2)}, u32[]{:S(2)}) async-start(f32[16,8,128]{2,1,0:T(8,128)} %get-tuple-element.18), calls=%async_computation.7 | async-start | bytes 131072 | tf_op jit(solution)/shard_map/all_to_all | solution.py:38
  160.7 6.4 %all-to-all-done.7 = f32[16,8,128]{2,1,0:T(8,128)S(1)} async-done(((f32[16,8,128]{2,1,0:T(8,128)}), f32[16,8,128]{2,1,0:T(8,128)S(1)}, u32[]{:S(2)}, u32[]{:S(2)}) %all-to-all-start.7) | async-done | bytes 65568 | tf_op jit(solution)/shard_map/all_to_all | solution.py:38
  167.2 0.6 add_bitcast_fusion
  (15 shorter events, 1.4 us)
Async XLA Ops:
  0.6 27.4 %copy-start.2 = (f32[1024]{0:T(1024)S(1)}, f32[1024]{0:T(1024)}, u32[]{:S(2)}) copy-start(f32[1024]{0:T(1024)} %param.5) | copy-start | bytes 12292
  7.2 57.2 %copy-start = (bf16[1024,2048]{1,0:T(8,128)(2,1)}, bf16[1024,2048]{1,0:T(8,128)(2,1)S(1)}, u32[]{:S(2)}) copy-start(bf16[1024,2048]{1,0:T(8,128)(2,1)S(1)} %get-tuple-element.14.images) | copy-start | bytes 12582916
  128.6 18.5 %collective-permute-start = (bf16[128,2048]{1,0:T(8,128)(2,1)S(1)}, bf16[128,2048]{1,0:T(8,128)(2,1)S(1)}, u32[]{:S(2)}, u32[]{:S(2)}) collective-permute-start(bf16[128,2048]{1,0:T(8,128)(2,1)S(1)} %bitcast.9), channel_id=1, source_target_pairs={{0,128},{16,144},{32,160},{48,176},{64,192},{80,208},{96,224},{112... | collective-permute-start | bytes 1572872 | tf_op jit(solution)/shard_map/ppermute | solution.py:323
  136.9 11.3 %collective-permute-start.1 = (bf16[128,2048]{1,0:T(8,128)(2,1)S(1)}, bf16[128,2048]{1,0:T(8,128)(2,1)S(1)}, u32[]{:S(2)}, u32[]{:S(2)}) collective-permute-start(bf16[128,2048]{1,0:T(8,128)(2,1)S(1)} %bitcast.10), channel_id=1, source_target_pairs={{0,16},{16,0},{32,48},{48,32},{64,80},{80,64},{96,112},{112,96},{1... | collective-permute-start | bytes 1572872 | tf_op jit(solution)/shard_map/ppermute | solution.py:323
  138.8 14.6 %collective-permute-start.2 = (bf16[128,2048]{1,0:T(8,128)(2,1)S(1)}, bf16[128,2048]{1,0:T(8,128)(2,1)S(1)}, u32[]{:S(2)}, u32[]{:S(2)}) collective-permute-start(bf16[128,2048]{1,0:T(8,128)(2,1)S(1)} %bitcast.11), channel_id=1, source_target_pairs={{0,144},{16,128},{32,176},{48,160},{64,208},{80,192},{96,240},{112... | collective-permute-start | bytes 1572872 | tf_op jit(solution)/shard_map/ppermute | solution.py:323
  143.3 2.2 %copy-start.1 = (bf16[1024,2048]{1,0:T(8,128)(2,1)S(1)}, bf16[1024,2048]{1,0:T(8,128)(2,1)}, u32[]{:S(2)}) copy-start(bf16[1024,2048]{1,0:T(8,128)(2,1)} %copy-done) | copy-start | bytes 12582916
  156.7 10.4 %all-to-all-start.7 = ((f32[16,8,128]{2,1,0:T(8,128)}), f32[16,8,128]{2,1,0:T(8,128)S(1)}, u32[]{:S(2)}, u32[]{:S(2)}) async-start(f32[16,8,128]{2,1,0:T(8,128)} %get-tuple-element.18), calls=%async_computation.7 | async-start | bytes 131072 | tf_op jit(solution)/shard_map/all_to_all | solution.py:38

commit v11 on v10

--- a/solution.py
+++ b/solution.py
@@ -222,47 +222,50 @@
     out[...] = scored_rows(piece, images, contrast, norms)
 
 
-def pair_kernel(first, second, images, contrast, before, out, norms):
+def writes(pieces, result, semaphores):
+    image, ref = lax.axis_index("img"), lax.axis_index("ref")
+    a = lax.rem(lax.div(image, Y) + ref, 2)
+    b = lax.rem(lax.rem(image, Y) + ref, 2)
+    copies = []
+    for k, (piece, (along_x, along_y)) in enumerate(pieces):
+        side = (1 - a if along_x else a) * 2 + (1 - b if along_y else b)
+        rows = piece.shape[0]
+        place = pl.ds(pl.multiple_of(side * rows, rows), rows)
+        copies.append(pltpu.make_async_copy(piece, result.at[place], semaphores.at[k]))
+    return copies
+
+
+def pair_kernel(own, first, second, images, contrast, before, out, result, norms, semaphores):
+    copies = writes(((own, (0, 0)), (first, WAYS[0]), (second, WAYS[1])), result, semaphores)
+    for copy in copies:
+        copy.start()
     logs = [before[...]]
     logs += [scored_rows(piece, images, contrast, norms) for piece in (first, second)]
     out[...] = combined_log(jnp.stack(logs))
-
-
-def last_kernel(own, first, second, last, images, contrast, before, out, result, norms, semaphores):
-    image, ref = lax.axis_index("img"), lax.axis_index("ref")
-    a = lax.rem(lax.div(image, Y) + ref, 2)
-    b = lax.rem(lax.rem(image, Y) + ref, 2)
-    rows = own.shape[0]
-    copies = []
-    for k, (piece, side) in enumerate(
-        (
-            (own, a * 2 + b),
-            (first, (1 - a) * 2 + b),
-            (second, a * 2 + 1 - b),
-            (last, (1 - a) * 2 + 1 - b),
-        )
-    ):
-        place = pl.ds(pl.multiple_of(side * rows, rows), rows)
-        copies.append(pltpu.make_async_copy(piece, result.at[place], semaphores.at[k]))
     for copy in copies:
-        copy.start()
+        copy.wait()
+
+
+def last_kernel(last, images, contrast, before, begun, out, result, norms, semaphores):
+    (copy,) = writes(((last, WAYS[2]),), result, semaphores)
+    copy.start()
     logs = scored_rows(last, images, contrast, norms)
     out[...] = jnp.broadcast_to(combined_log(jnp.stack([before[...], logs]))[None], out.shape)
-    for copy in copies:
-        copy.wait()
+    copy.wait()
 
 
 VMEM = pl.BlockSpec(memory_space=pltpu.VMEM)
 HBM = pl.BlockSpec(memory_space=pltpu.HBM)
 
 
-def call(kernel, outs, *args, ins=None, specs=None, scratch=(), limit=16, flops=0):
+def call(kernel, outs, *args, ins=None, specs=None, scratch=(), limit=16, flops=0, aliases=None):
     return pl.pallas_call(
         kernel,
         out_shape=outs,
         in_specs=ins or [VMEM] * len(args),
         out_specs=specs or (VMEM,) * len(outs),
         scratch_shapes=scratch,
+        input_output_aliases=aliases or {},
         compiler_params=pltpu.CompilerParams(vmem_limit_bytes=limit * 2**20),
         cost_estimate=pl.CostEstimate(
             flops=flops, bytes_accessed=2**22, transcendentals=2**19
@@ -324,21 +327,31 @@
     norm = [pltpu.VMEM((rows.shape[0], LANES), f32)]
     log = (pltpu.VMEM(per_image, f32),)
     (before,) = call(score_kernel, log, rows, kept, contrast, scratch=norm, flops=flops // 4)
-    (before,) = call(
-        pair_kernel, log, first, second, kept, contrast, before, scratch=norm, flops=flops // 2
-    )
-    own, new_references = call(
-        last_kernel,
-        (one, jax.ShapeDtypeStruct((refs, width), bf16)),
+    before, begun = call(
+        pair_kernel,
+        (*log, pltpu.HBM((refs, width), bf16)),
         rows,
         first,
         second,
+        kept,
+        contrast,
+        before,
+        specs=(VMEM, HBM),
+        scratch=[*norm, pltpu.SemaphoreType.DMA((3,))],
+        flops=flops // 2,
+    )
+    own, new_references = call(
+        last_kernel,
+        (one, pltpu.HBM((refs, width), bf16)),
         last,
         kept,
         contrast,
         before,
+        begun,
+        ins=[VMEM] * 4 + [HBM],
         specs=(VMEM, HBM),
-        scratch=[*norm, pltpu.SemaphoreType.DMA((4,))],
+        scratch=[*norm, pltpu.SemaphoreType.DMA((1,))],
+        aliases={4: 1},
         flops=flops // 4,
     )
     loglik = combined_log(exchanged(own, "ref")) - math.log(refs * devices)

time: 169 us -> 168 us (level)
  no operation moved by 1% of the time
where the time goes in v11:
time: 168 us; the launch traced here: 167 us
  blocking collectives  115 us (68%)
  Pallas kernels  20.3 us (12%)
  starting transfers between devices  18.1 us (11%)
  waiting for transfers between devices  8.69 us (5%)
  local copies, waits for them, and re-layouts  2.84 us (2%)
    all_to_all x7, blocking collectives, exchanged(): lax.all_to_all(pieces, axis, 0, 0, tiled=True, axis_index_groups=groups)  115 us
    pallas_call x8, Pallas kernels, call(): pl.pallas_call(kernel, out_shape=outs, in_specs=ins or [VMEM] * len(args)...  20.3 us
    ppermute x3, starting transfers between devices, per_device(): lax.ppermute(rows, PLANE, toward(*way))  14.7 us
    all_to_all x1, waiting for transfers between devices, exchanged(): lax.all_to_all(pieces, axis, 0, 0, tiled=True, axis_index_groups=groups)  6.38 us
    all_to_all x1, starting transfers between devices, exchanged(): lax.all_to_all(pieces, axis, 0, 0, tiled=True, axis_index_groups=groups)  3.4 us
  transfers between devices with their start and end apart: 4, of which 3 were waited for; matrix products, arithmetic and copies ran while one was open for 0% of the time, Pallas kernels for 3%

profile of v11, /device:TPU:1, one launch (start us, length us, event | category | flops | bytes accessed | tf_op | source)
XLA Modules:
  0.0 167.2 jit_solution(5411283147738661662)
XLA Ops:
  0.6 6.6 %shard_map.58 = (f32[512,1024]{1,0:T(8,128)S(1)}, bf16[1024,2048]{1,0:T(8,128)(2,1)S(1)}, f32[512,128]{1,0:T(8,128)S(1)}, f32[16,16,128]{2,1,0:T(8,128)S(1)}) custom-call(bf16[1024,2048]{1,0:T(8,128)(2,1)} %images.1, bf16[512,2048]{1,0:T(8,128)(2,1)} %references.1, f32[8,128]{1,0:T(8,128)} %bitcast.14), custom_call_target="tpu_custom_call" | custom-call | flops 2147483648 | bytes 4194304 | tf_op jit(solution)/shard_map/pallas_call | solution.py:262
  7.2 20.8 %all_to_all.40.received = f32[16,16,128]{2,1,0:T(8,128)S(1)} all-to-all(f32[16,16,128]{2,1,0:T(8,128)S(1)} %get-tuple-element.13), channel_id=1, replica_groups=mesh['img'=32,'ref'=16] {'ref'}, dimensions={0} | all-to-all | bytes 262144 | tf_op jit(solution)/shard_map/all_to_all | solution.py:38
  28.0 1.1 shard_map.59
  29.1 11.6 %all_to_all.41.received = f32[16,16,128]{2,1,0:T(8,128)S(1)} all-to-all(f32[16,16,128]{2,1,0:T(8,128)S(1)} %shard_map.59), channel_id=1, replica_groups=mesh['img'=32,'ref'=16] {'ref'}, dimensions={0} | all-to-all | bytes 262144 | tf_op jit(solution)/shard_map/all_to_all | solution.py:38
  40.7 1.1 shard_map.60
  41.8 11.6 %all_to_all.42.received = f32[16,16,128]{2,1,0:T(8,128)S(1)} all-to-all(f32[16,16,128]{2,1,0:T(8,128)S(1)} %shard_map.60), channel_id=1, replica_groups=mesh['img'=32,'ref'=16] {'ref'}, dimensions={0} | all-to-all | bytes 262144 | tf_op jit(solution)/shard_map/all_to_all | solution.py:38
  53.4 0.8 shard_map.61
  54.2 10.2 %all_to_all.43.received = f32[16,8,128]{2,1,0:T(8,128)S(1)} all-to-all(f32[16,8,128]{2,1,0:T(8,128)S(1)} %get-tuple-element.17), channel_id=1, replica_groups=mesh['img'=32,'ref'=16] {'ref'}, dimensions={0} | all-to-all | bytes 131072 | tf_op jit(solution)/shard_map/all_to_all | solution.py:38
  64.4 2.4 %shard_map.62 = bf16[512,2048]{1,0:T(8,128)(2,1)S(1)} custom-call(f32[16,8,128]{2,1,0:T(8,128)S(1)} %all_to_all.43.received, f32[512,1024]{1,0:T(8,128)S(1)} %get-tuple-element.14.cross, f32[512,128]{1,0:T(8,128)S(1)} %get-tuple-element.15.norms, f32[8,128]{1,0:T(8,128)S(1)} %get-tuple-element.18.contrast, bf16[1024,2048]{1,0:T(8,128)(2,1)S(1)} %get-tuple-element.16.images), custom_call_target="tpu_custom_call" | custom-call | flops 2147483648 | bytes 4194304 | tf_op jit(solution)/shard_map/pallas_call | solution.py:262
  66.8 20.5 %all_to_all.44 = bf16[4,128,2048]{2,1,0:T(8,128)(2,1)S(1)} all-to-all(bf16[4,128,2048]{2,1,0:T(8,128)(2,1)S(1)} %bitcast.8), channel_id=1, replica_groups={{0,16,128,144},{32,48,160,176},{64,80,192,208},{96,112,224,240},{256,27..., dimensions={0} | all-to-all | bytes 4194304 | tf_op jit(solution)/shard_map/all_to_all | solution.py:38
  87.8 22.9 %all_to_all.45 = bf16[8,16,2048]{2,1,0:T(8,128)(2,1)S(1)} all-to-all(bf16[8,16,2048]{2,1,0:T(8,128)(2,1)S(1)} %bitcast.17), channel_id=1, replica_groups={{0,320,32,352,64,256,96,288},{16,336,48,368,80,272,112,304},{128,448,16..., dimensions={0} | all-to-all | bytes 1048576 | tf_op jit(solution)/shard_map/all_to_all | solution.py:38
  111.0 17.6 %all_to_all.46 = bf16[8,16,2048]{2,1,0:T(8,128)(2,1)S(1)} all-to-all(bf16[8,16,2048]{2,1,0:T(8,128)(2,1)S(1)} %broadcast_in_dim.2), channel_id=1, replica_groups={{0,320,32,352,64,256,96,288},{16,336,48,368,80,272,112,304},{128,448,16..., dimensions={0} | all-to-all | bytes 1048576 | tf_op jit(solution)/shard_map/all_to_all | solution.py:38
  128.6 8.3 %collective-permute-start.1 = (bf16[128,2048]{1,0:T(8,128)(2,1)S(1)}, bf16[128,2048]{1,0:T(8,128)(2,1)S(1)}, u32[]{:S(2)}, u32[]{:S(2)}) collective-permute-start(bf16[128,2048]{1,0:T(8,128)(2,1)S(1)} %bitcast.9), channel_id=1, source_target_pairs={{0,128},{16,144},{32,160},{48,176},{64,192},{80,208},{96,224},{112... | collective-permute-start | bytes 1572872 | tf_op jit(solution)/shard_map/ppermute | solution.py:326
  136.9 1.9 %collective-permute-start.2 = (bf16[128,2048]{1,0:T(8,128)(2,1)S(1)}, bf16[128,2048]{1,0:T(8,128)(2,1)S(1)}, u32[]{:S(2)}, u32[]{:S(2)}) collective-permute-start(bf16[128,2048]{1,0:T(8,128)(2,1)S(1)} %bitcast.10), channel_id=1, source_target_pairs={{0,16},{16,0},{32,48},{48,32},{64,80},{80,64},{96,112},{112,96},{1... | collective-permute-start | bytes 1572872 | tf_op jit(solution)/shard_map/ppermute | solution.py:326
  138.8 4.5 %collective-permute-start = (bf16[128,2048]{1,0:T(8,128)(2,1)S(1)}, bf16[128,2048]{1,0:T(8,128)(2,1)S(1)}, u32[]{:S(2)}, u32[]{:S(2)}) collective-permute-start(bf16[128,2048]{1,0:T(8,128)(2,1)S(1)} %bitcast.11), channel_id=1, source_target_pairs={{0,144},{16,128},{32,176},{48,160},{64,208},{80,192},{96,240},{112... | collective-permute-start | bytes 1572872 | tf_op jit(solution)/shard_map/ppermute | solution.py:326
  143.3 2.2 %copy-done.1 = bf16[1024,2048]{1,0:T(8,128)(2,1)S(1)} copy-done((bf16[1024,2048]{1,0:T(8,128)(2,1)S(1)}, bf16[1024,2048]{1,0:T(8,128)(2,1)}, u32[]{:S(2)}) %copy-start.1) | copy-done | bytes 4194328
  145.5 1.6 shard_map.63.before
  147.1 1.1 collective-permute-done.2.second
  148.2 4.0 %shard_map.64 = (f32[8,128]{1,0:T(8,128)S(1)}, bf16[512,2048]{1,0:T(8,128)(2,1)}) custom-call(bf16[128,2048]{1,0:T(8,128)(2,1)S(1)} %bitcast.13, bf16[128,2048]{1,0:T(8,128)(2,1)S(1)} %collective-permute-done.1.first, bf16[128,2048]{1,0:T(8,128)(2,1)S(1)} %collective-permute-done.2.second, bf16[1024,2048]{1,0:T(8,128)(2,1)S(1)} %copy-done.1, ...), custom_call_target="tpu_custom_call" | custom-call | flops 1073741824 | bytes 4194304 | tf_op jit(solution)/shard_map/pallas_call | solution.py:262
  152.1 1.2 collective-permute-done.last
  153.4 2.8 %shard_map.65 = (f32[16,8,128]{2,1,0:T(8,128)}, bf16[512,2048]{1,0:T(8,128)(2,1)}) custom-call(bf16[128,2048]{1,0:T(8,128)(2,1)S(1)} %collective-permute-done.last, bf16[1024,2048]{1,0:T(8,128)(2,1)S(1)} %copy-done.1, f32[8,128]{1,0:T(8,128)S(1)} %get-tuple-element.18.contrast, ...), custom_call_target="tpu_custom_call", output_to_operand_aliasing={{1}: (4, {})} | custom-call | flops 536870912 | bytes 4194304 | tf_op jit(solution)/shard_map/pallas_call | solution.py:262
  156.2 3.4 %all-to-all-start.7 = ((f32[16,8,128]{2,1,0:T(8,128)}), f32[16,8,128]{2,1,0:T(8,128)S(1)}, u32[]{:S(2)}, u32[]{:S(2)}) async-start(f32[16,8,128]{2,1,0:T(8,128)} %get-tuple-element.22), calls=%async_computation.7 | async-start | bytes 131072 | tf_op jit(solution)/shard_map/all_to_all | solution.py:38
  160.2 6.4 %all-to-all-done.7 = f32[16,8,128]{2,1,0:T(8,128)S(1)} async-done(((f32[16,8,128]{2,1,0:T(8,128)}), f32[16,8,128]{2,1,0:T(8,128)S(1)}, u32[]{:S(2)}, u32[]{:S(2)}) %all-to-all-start.7) | async-done | bytes 65568 | tf_op jit(solution)/shard_map/all_to_all | solution.py:38
  166.6 0.6 add_bitcast_fusion
  (15 shorter events, 1.4 us)
Async XLA Ops:
  0.6 27.4 %copy-start.2 = (f32[1024]{0:T(1024)S(1)}, f32[1024]{0:T(1024)}, u32[]{:S(2)}) copy-start(f32[1024]{0:T(1024)} %param.5) | copy-start | bytes 12292
  7.2 57.2 %copy-start = (bf16[1024,2048]{1,0:T(8,128)(2,1)}, bf16[1024,2048]{1,0:T(8,128)(2,1)S(1)}, u32[]{:S(2)}) copy-start(bf16[1024,2048]{1,0:T(8,128)(2,1)S(1)} %get-tuple-element.16.images) | copy-start | bytes 12582916
  128.6 18.5 %collective-permute-start.1 = (bf16[128,2048]{1,0:T(8,128)(2,1)S(1)}, bf16[128,2048]{1,0:T(8,128)(2,1)S(1)}, u32[]{:S(2)}, u32[]{:S(2)}) collective-permute-start(bf16[128,2048]{1,0:T(8,128)(2,1)S(1)} %bitcast.9), channel_id=1, source_target_pairs={{0,128},{16,144},{32,160},{48,176},{64,192},{80,208},{96,224},{112... | collective-permute-start | bytes 1572872 | tf_op jit(solution)/shard_map/ppermute | solution.py:326
  136.9 11.3 %collective-permute-start.2 = (bf16[128,2048]{1,0:T(8,128)(2,1)S(1)}, bf16[128,2048]{1,0:T(8,128)(2,1)S(1)}, u32[]{:S(2)}, u32[]{:S(2)}) collective-permute-start(bf16[128,2048]{1,0:T(8,128)(2,1)S(1)} %bitcast.10), channel_id=1, source_target_pairs={{0,16},{16,0},{32,48},{48,32},{64,80},{80,64},{96,112},{112,96},{1... | collective-permute-start | bytes 1572872 | tf_op jit(solution)/shard_map/ppermute | solution.py:326
  138.8 14.6 %collective-permute-start = (bf16[128,2048]{1,0:T(8,128)(2,1)S(1)}, bf16[128,2048]{1,0:T(8,128)(2,1)S(1)}, u32[]{:S(2)}, u32[]{:S(2)}) collective-permute-start(bf16[128,2048]{1,0:T(8,128)(2,1)S(1)} %bitcast.11), channel_id=1, source_target_pairs={{0,144},{16,128},{32,176},{48,160},{64,208},{80,192},{96,240},{112... | collective-permute-start | bytes 1572872 | tf_op jit(solution)/shard_map/ppermute | solution.py:326
  143.3 2.2 %copy-start.1 = (bf16[1024,2048]{1,0:T(8,128)(2,1)S(1)}, bf16[1024,2048]{1,0:T(8,128)(2,1)}, u32[]{:S(2)}) copy-start(bf16[1024,2048]{1,0:T(8,128)(2,1)} %copy-done) | copy-start | bytes 12582916
  156.2 10.4 %all-to-all-start.7 = ((f32[16,8,128]{2,1,0:T(8,128)}), f32[16,8,128]{2,1,0:T(8,128)S(1)}, u32[]{:S(2)}, u32[]{:S(2)}) async-start(f32[16,8,128]{2,1,0:T(8,128)} %get-tuple-element.22), calls=%async_computation.7 | async-start | bytes 131072 | tf_op jit(solution)/shard_map/all_to_all | solution.py:38

commit v12 on v11

--- a/solution.py
+++ b/solution.py
@@ -181,9 +181,11 @@
     send(out, logs, quotients)
 
 
-def total_kernel(received, cross, norms, images, contrast, out):
+def total_kernel(received, cross, norms, images, contrast, out, result, semaphore):
     found = combined(received[...])
     contrast[...] = found
+    copy = pltpu.make_async_copy(contrast, result, semaphore)
+    copy.start()
     send(
         out,
         [
@@ -191,6 +193,7 @@
             for k in range(cross.shape[1] // BLOCK)
         ],
     )
+    copy.wait()
 
 
 def sum_kernel(received, cross, norms, contrast, images, out, weights):
@@ -302,13 +305,15 @@
     )
     for _ in range(ITERS - 1):
         (own,) = call(refit_kernel, (two,), exchanged(own, "ref"), cross, norms, prior, kept)
-    contrast, own = call(
+    contrast, own, fitted = call(
         total_kernel,
-        (pltpu.VMEM(per_image, f32), one),
+        (pltpu.VMEM(per_image, f32), one, pltpu.HBM(per_image, f32)),
         exchanged(own, "ref"),
         cross,
         norms,
         kept,
+        specs=(VMEM, VMEM, HBM),
+        scratch=[pltpu.SemaphoreType.DMA],
     )
     (img_partial,) = call(
         sum_kernel,
@@ -355,7 +360,7 @@
         flops=flops // 4,
     )
     loglik = combined_log(exchanged(own, "ref")) - math.log(refs * devices)
-    return (new_references, contrast.reshape(count), loglik.reshape(count))
+    return (new_references, fitted.reshape(count), loglik.reshape(count))
 
 
 def solution(mesh):

time: 168 us -> 171 us (1.018)
  blocking collectives: 115 us -> 128 us
  waiting for transfers between devices: 8.69 us -> 3.44 us
  starting transfers between devices: 18.1 us -> 14.6 us
    all_to_all x7 -> x8, blocking collectives: 115 us -> 128 us  [exchanged(): lax.all_to_all(pieces, axis, 0, 0, tiled=True, axis_index_groups=groups)]
    all_to_all x1 -> x0, waiting for transfers between devices: 6.38 us -> none  [exchanged(): lax.all_to_all(pieces, axis, 0, 0, tiled=True, axis_index_groups=groups)]
    all_to_all x1 -> x0, starting transfers between devices: 3.4 us -> none  [exchanged(): lax.all_to_all(pieces, axis, 0, 0, tiled=True, axis_index_groups=groups)]
  transfers between devices with their start and end apart: 4 -> 3, of which waited for: 3 -> 1; matrix products, arithmetic and copies ran while one was open for 0% -> 0% of each run, Pallas kernels for 3% -> 3%
where the time goes in v12:
time: 171 us; the launch traced here: 170 us
  blocking collectives  128 us (75%)
  Pallas kernels  19.7 us (12%)
  starting transfers between devices  14.6 us (9%)
  waiting for transfers between devices  3.44 us (2%)
  local copies, waits for them, and re-layouts  2.24 us (1%)
    all_to_all x8, blocking collectives, exchanged(): lax.all_to_all(pieces, axis, 0, 0, tiled=True, axis_index_groups=groups)  128 us
    pallas_call x8, Pallas kernels, call(): pl.pallas_call(kernel, out_shape=outs, in_specs=ins or [VMEM] * len(args)...  19.7 us
    ppermute x3, starting transfers between devices, per_device(): lax.ppermute(rows, PLANE, toward(*way))  14.6 us
    ppermute x3, waiting for transfers between devices, per_device(): lax.ppermute(rows, PLANE, toward(*way))  3.44 us
  transfers between devices with their start and end apart: 3, of which 1 were waited for; matrix products, arithmetic and copies ran while one was open for 0% of the time, Pallas kernels for 3%

profile of v12, /device:TPU:1, one launch (start us, length us, event | category | flops | bytes accessed | tf_op | source)
XLA Modules:
  0.0 170.1 jit_solution(2553614734972465646)
XLA Ops:
  0.6 6.6 %shard_map.58 = (f32[512,1024]{1,0:T(8,128)S(1)}, bf16[1024,2048]{1,0:T(8,128)(2,1)S(1)}, f32[512,128]{1,0:T(8,128)S(1)}, f32[16,16,128]{2,1,0:T(8,128)S(1)}) custom-call(bf16[1024,2048]{1,0:T(8,128)(2,1)} %images.1, bf16[512,2048]{1,0:T(8,128)(2,1)} %references.1, f32[8,128]{1,0:T(8,128)} %bitcast.13), custom_call_target="tpu_custom_call" | custom-call | flops 2147483648 | bytes 4194304 | tf_op jit(solution)/shard_map/pallas_call | solution.py:265
  7.2 20.8 %all_to_all.40.received = f32[16,16,128]{2,1,0:T(8,128)S(1)} all-to-all(f32[16,16,128]{2,1,0:T(8,128)S(1)} %get-tuple-element.14), channel_id=1, replica_groups=mesh['img'=32,'ref'=16] {'ref'}, dimensions={0} | all-to-all | bytes 262144 | tf_op jit(solution)/shard_map/all_to_all | solution.py:38
  28.0 1.1 shard_map.59
  29.1 11.6 %all_to_all.41.received = f32[16,16,128]{2,1,0:T(8,128)S(1)} all-to-all(f32[16,16,128]{2,1,0:T(8,128)S(1)} %shard_map.59), channel_id=1, replica_groups=mesh['img'=32,'ref'=16] {'ref'}, dimensions={0} | all-to-all | bytes 262144 | tf_op jit(solution)/shard_map/all_to_all | solution.py:38
  40.7 1.1 shard_map.60
  41.8 11.6 %all_to_all.42.received = f32[16,16,128]{2,1,0:T(8,128)S(1)} all-to-all(f32[16,16,128]{2,1,0:T(8,128)S(1)} %shard_map.60), channel_id=1, replica_groups=mesh['img'=32,'ref'=16] {'ref'}, dimensions={0} | all-to-all | bytes 262144 | tf_op jit(solution)/shard_map/all_to_all | solution.py:38
  53.4 0.8 shard_map.61
  54.2 10.2 %all_to_all.43.received = f32[16,8,128]{2,1,0:T(8,128)S(1)} all-to-all(f32[16,8,128]{2,1,0:T(8,128)S(1)} %get-tuple-element.18), channel_id=1, replica_groups=mesh['img'=32,'ref'=16] {'ref'}, dimensions={0} | all-to-all | bytes 131072 | tf_op jit(solution)/shard_map/all_to_all | solution.py:38
  64.4 2.4 %shard_map.62 = bf16[512,2048]{1,0:T(8,128)(2,1)S(1)} custom-call(f32[16,8,128]{2,1,0:T(8,128)S(1)} %all_to_all.43.received, f32[512,1024]{1,0:T(8,128)S(1)} %get-tuple-element.15.cross, f32[512,128]{1,0:T(8,128)S(1)} %get-tuple-element.16.norms, f32[8,128]{1,0:T(8,128)S(1)} %get-tuple-element.19.contrast, bf16[1024,2048]{1,0:T(8,128)(2,1)S(1)} %get-tuple-element.17.images), custom_call_target="tpu_custom_call" | custom-call | flops 2147483648 | bytes 4194304 | tf_op jit(solution)/shard_map/pallas_call | solution.py:265
  66.8 20.5 %all_to_all.44 = bf16[4,128,2048]{2,1,0:T(8,128)(2,1)S(1)} all-to-all(bf16[4,128,2048]{2,1,0:T(8,128)(2,1)S(1)} %bitcast.7), channel_id=1, replica_groups={{0,16,128,144},{32,48,160,176},{64,80,192,208},{96,112,224,240},{256,27..., dimensions={0} | all-to-all | bytes 4194304 | tf_op jit(solution)/shard_map/all_to_all | solution.py:38
  87.3 0.4 reduce_sum.39
  87.8 22.9 %all_to_all.45 = bf16[8,16,2048]{2,1,0:T(8,128)(2,1)S(1)} all-to-all(bf16[8,16,2048]{2,1,0:T(8,128)(2,1)S(1)} %bitcast.16), channel_id=1, replica_groups={{0,320,32,352,64,256,96,288},{16,336,48,368,80,272,112,304},{128,448,16..., dimensions={0} | all-to-all | bytes 1048576 | tf_op jit(solution)/shard_map/all_to_all | solution.py:38
  110.7 0.1 multiply_reduce_fusion
  111.0 17.6 %all_to_all.46 = bf16[8,16,2048]{2,1,0:T(8,128)(2,1)S(1)} all-to-all(bf16[8,16,2048]{2,1,0:T(8,128)(2,1)S(1)} %broadcast_in_dim.2), channel_id=1, replica_groups={{0,320,32,352,64,256,96,288},{16,336,48,368,80,272,112,304},{128,448,16..., dimensions={0} | all-to-all | bytes 1048576 | tf_op jit(solution)/shard_map/all_to_all | solution.py:38
  128.7 1.9 %collective-permute-start.2 = (bf16[128,2048]{1,0:T(8,128)(2,1)S(1)}, bf16[128,2048]{1,0:T(8,128)(2,1)S(1)}, u32[]{:S(2)}, u32[]{:S(2)}) collective-permute-start(bf16[128,2048]{1,0:T(8,128)(2,1)S(1)} %bitcast.8), channel_id=1, source_target_pairs={{0,16},{16,0},{32,48},{48,32},{64,80},{80,64},{96,112},{112,96},{1... | collective-permute-start | bytes 1572872 | tf_op jit(solution)/shard_map/ppermute | solution.py:331
  130.6 8.2 %collective-permute-start.1 = (bf16[128,2048]{1,0:T(8,128)(2,1)S(1)}, bf16[128,2048]{1,0:T(8,128)(2,1)S(1)}, u32[]{:S(2)}, u32[]{:S(2)}) collective-permute-start(bf16[128,2048]{1,0:T(8,128)(2,1)S(1)} %bitcast.9), channel_id=1, source_target_pairs={{0,128},{16,144},{32,160},{48,176},{64,192},{80,208},{96,224},{112... | collective-permute-start | bytes 1572872 | tf_op jit(solution)/shard_map/ppermute | solution.py:331
  138.8 4.5 %collective-permute-start = (bf16[128,2048]{1,0:T(8,128)(2,1)S(1)}, bf16[128,2048]{1,0:T(8,128)(2,1)S(1)}, u32[]{:S(2)}, u32[]{:S(2)}) collective-permute-start(bf16[128,2048]{1,0:T(8,128)(2,1)S(1)} %bitcast.10), channel_id=1, source_target_pairs={{0,144},{16,128},{32,176},{48,160},{64,208},{80,192},{96,240},{112... | collective-permute-start | bytes 1572872 | tf_op jit(solution)/shard_map/ppermute | solution.py:331
  143.3 2.2 %copy-done.1 = bf16[1024,2048]{1,0:T(8,128)(2,1)S(1)} copy-done((bf16[1024,2048]{1,0:T(8,128)(2,1)S(1)}, bf16[1024,2048]{1,0:T(8,128)(2,1)}, u32[]{:S(2)}) %copy-start.1) | copy-done | bytes 4194328
  145.5 1.6 shard_map.63.before
  147.1 3.4 %collective-permute-done.1.first = bf16[128,2048]{1,0:T(8,128)(2,1)S(1)} collective-permute-done((bf16[128,2048]{1,0:T(8,128)(2,1)S(1)}, bf16[128,2048]{1,0:T(8,128)(2,1)S(1)}, u32[]{:S(2)}, u32[]{:S(2)}) %collective-permute-start.1) | collective-permute-done | bytes 524320 | tf_op jit(solution)/shard_map/ppermute | solution.py:331
  150.5 4.0 %shard_map.64 = (f32[8,128]{1,0:T(8,128)S(1)}, bf16[512,2048]{1,0:T(8,128)(2,1)}) custom-call(bf16[128,2048]{1,0:T(8,128)(2,1)S(1)} %bitcast.12, bf16[128,2048]{1,0:T(8,128)(2,1)S(1)} %collective-permute-done.1.first, bf16[128,2048]{1,0:T(8,128)(2,1)S(1)} %collective-permute-done.2.second, bf16[1024,2048]{1,0:T(8,128)(2,1)S(1)} %copy-done.1, ...), custom_call_target="tpu_custom_call" | custom-call | flops 1073741824 | bytes 4194304 | tf_op jit(solution)/shard_map/pallas_call | solution.py:265
  154.5 2.2 %shard_map.65 = (f32[16,8,128]{2,1,0:T(8,128)S(1)}, bf16[512,2048]{1,0:T(8,128)(2,1)}) custom-call(bf16[128,2048]{1,0:T(8,128)(2,1)S(1)} %collective-permute-done.last, bf16[1024,2048]{1,0:T(8,128)(2,1)S(1)} %copy-done.1, f32[8,128]{1,0:T(8,128)S(1)} %get-tuple-element.19.contrast, ...), custom_call_target="tpu_custom_call", output_to_operand_aliasing={{1}: (4, {})} | custom-call | flops 536870912 | bytes 4194304 | tf_op jit(solution)/shard_map/pallas_call | solution.py:265
  156.7 12.8 %all_to_all.47 = f32[16,8,128]{2,1,0:T(8,128)S(1)} all-to-all(f32[16,8,128]{2,1,0:T(8,128)S(1)} %get-tuple-element.24), channel_id=1, replica_groups=mesh['img'=32,'ref'=16] {'ref'}, dimensions={0} | all-to-all | bytes 131072 | tf_op jit(solution)/shard_map/all_to_all | solution.py:38
  169.5 0.6 add_bitcast_fusion
  (13 shorter events, 0.3 us)
Async XLA Ops:
  0.6 27.4 %copy-start.2 = (f32[1024]{0:T(1024)S(1)}, f32[1024]{0:T(1024)}, u32[]{:S(2)}) copy-start(f32[1024]{0:T(1024)} %param.5) | copy-start | bytes 12292
  7.2 57.2 %copy-start = (bf16[1024,2048]{1,0:T(8,128)(2,1)}, bf16[1024,2048]{1,0:T(8,128)(2,1)S(1)}, u32[]{:S(2)}) copy-start(bf16[1024,2048]{1,0:T(8,128)(2,1)S(1)} %get-tuple-element.17.images) | copy-start | bytes 12582916
  128.7 18.5 %collective-permute-start.2 = (bf16[128,2048]{1,0:T(8,128)(2,1)S(1)}, bf16[128,2048]{1,0:T(8,128)(2,1)S(1)}, u32[]{:S(2)}, u32[]{:S(2)}) collective-permute-start(bf16[128,2048]{1,0:T(8,128)(2,1)S(1)} %bitcast.8), channel_id=1, source_target_pairs={{0,16},{16,0},{32,48},{48,32},{64,80},{80,64},{96,112},{112,96},{1... | collective-permute-start | bytes 1572872 | tf_op jit(solution)/shard_map/ppermute | solution.py:331
  130.6 20.0 %collective-permute-start.1 = (bf16[128,2048]{1,0:T(8,128)(2,1)S(1)}, bf16[128,2048]{1,0:T(8,128)(2,1)S(1)}, u32[]{:S(2)}, u32[]{:S(2)}) collective-permute-start(bf16[128,2048]{1,0:T(8,128)(2,1)S(1)} %bitcast.9), channel_id=1, source_target_pairs={{0,128},{16,144},{32,160},{48,176},{64,192},{80,208},{96,224},{112... | collective-permute-start | bytes 1572872 | tf_op jit(solution)/shard_map/ppermute | solution.py:331
  138.8 15.7 %collective-permute-start = (bf16[128,2048]{1,0:T(8,128)(2,1)S(1)}, bf16[128,2048]{1,0:T(8,128)(2,1)S(1)}, u32[]{:S(2)}, u32[]{:S(2)}) collective-permute-start(bf16[128,2048]{1,0:T(8,128)(2,1)S(1)} %bitcast.10), channel_id=1, source_target_pairs={{0,144},{16,128},{32,176},{48,160},{64,208},{80,192},{96,240},{112... | collective-permute-start | bytes 1572872 | tf_op jit(solution)/shard_map/ppermute | solution.py:331
  143.3 2.2 %copy-start.1 = (bf16[1024,2048]{1,0:T(8,128)(2,1)S(1)}, bf16[1024,2048]{1,0:T(8,128)(2,1)}, u32[]{:S(2)}) copy-start(bf16[1024,2048]{1,0:T(8,128)(2,1)} %copy-done) | copy-start | bytes 12582916

commit v13 on v12

--- a/solution.py
+++ b/solution.py
@@ -51,7 +51,7 @@
     return partial
 
 
-WAYS = ((1, 0), (0, 1), (1, 1))
+WAYS = ((0, 1), (1, 0), (1, 1))
 
 
 def toward(along_x, along_y):

time: 171 us -> 167 us (0.977)
  blocking collectives: 128 us -> 126 us
    all_to_all x8, blocking collectives: 128 us -> 126 us  [exchanged(): lax.all_to_all(pieces, axis, 0, 0, tiled=True, axis_index_groups=groups)]
  transfers between devices with their start and end apart: 3 -> 3, of which waited for: 1 -> 2; matrix products, arithmetic and copies ran while one was open for 0% -> 0% of each run, Pallas kernels for 3% -> 3%
where the time goes in v13:
time: 167 us
  blocking collectives  126 us (75%)
  Pallas kernels  19.7 us (12%)
  starting transfers between devices  14.6 us (9%)
  waiting for transfers between devices  2.3 us (1%)
  local copies, waits for them, and re-layouts  2.24 us (1%)
    all_to_all x8, blocking collectives, exchanged(): lax.all_to_all(pieces, axis, 0, 0, tiled=True, axis_index_groups=groups)  126 us
    pallas_call x8, Pallas kernels, call(): pl.pallas_call(kernel, out_shape=outs, in_specs=ins or [VMEM] * len(args)...  19.7 us
    ppermute x3, starting transfers between devices, per_device(): lax.ppermute(rows, PLANE, toward(*way))  14.6 us
  transfers between devices with their start and end apart: 3, of which 2 were waited for; matrix products, arithmetic and copies ran while one was open for 0% of the time, Pallas kernels for 3%

profile of v13, /device:TPU:1, one launch (start us, length us, event | category | flops | bytes accessed | tf_op | source)
XLA Modules:
  0.0 166.5 jit_solution(5411294623751326215)
XLA Ops:
  0.6 6.6 %shard_map.58 = (f32[512,1024]{1,0:T(8,128)S(1)}, bf16[1024,2048]{1,0:T(8,128)(2,1)S(1)}, f32[512,128]{1,0:T(8,128)S(1)}, f32[16,16,128]{2,1,0:T(8,128)S(1)}) custom-call(bf16[1024,2048]{1,0:T(8,128)(2,1)} %images.1, bf16[512,2048]{1,0:T(8,128)(2,1)} %references.1, f32[8,128]{1,0:T(8,128)} %bitcast.13), custom_call_target="tpu_custom_call" | custom-call | flops 2147483648 | bytes 4194304 | tf_op jit(solution)/shard_map/pallas_call | solution.py:265
  7.2 20.8 %all_to_all.40.received = f32[16,16,128]{2,1,0:T(8,128)S(1)} all-to-all(f32[16,16,128]{2,1,0:T(8,128)S(1)} %get-tuple-element.14), channel_id=1, replica_groups=mesh['img'=32,'ref'=16] {'ref'}, dimensions={0} | all-to-all | bytes 262144 | tf_op jit(solution)/shard_map/all_to_all | solution.py:38
  28.0 1.1 shard_map.59
  29.1 11.6 %all_to_all.41.received = f32[16,16,128]{2,1,0:T(8,128)S(1)} all-to-all(f32[16,16,128]{2,1,0:T(8,128)S(1)} %shard_map.59), channel_id=1, replica_groups=mesh['img'=32,'ref'=16] {'ref'}, dimensions={0} | all-to-all | bytes 262144 | tf_op jit(solution)/shard_map/all_to_all | solution.py:38
  40.7 1.1 shard_map.60
  41.8 11.6 %all_to_all.42.received = f32[16,16,128]{2,1,0:T(8,128)S(1)} all-to-all(f32[16,16,128]{2,1,0:T(8,128)S(1)} %shard_map.60), channel_id=1, replica_groups=mesh['img'=32,'ref'=16] {'ref'}, dimensions={0} | all-to-all | bytes 262144 | tf_op jit(solution)/shard_map/all_to_all | solution.py:38
  53.4 0.8 shard_map.61
  54.2 10.2 %all_to_all.43.received = f32[16,8,128]{2,1,0:T(8,128)S(1)} all-to-all(f32[16,8,128]{2,1,0:T(8,128)S(1)} %get-tuple-element.18), channel_id=1, replica_groups=mesh['img'=32,'ref'=16] {'ref'}, dimensions={0} | all-to-all | bytes 131072 | tf_op jit(solution)/shard_map/all_to_all | solution.py:38
  64.4 2.4 %shard_map.62 = bf16[512,2048]{1,0:T(8,128)(2,1)S(1)} custom-call(f32[16,8,128]{2,1,0:T(8,128)S(1)} %all_to_all.43.received, f32[512,1024]{1,0:T(8,128)S(1)} %get-tuple-element.15.cross, f32[512,128]{1,0:T(8,128)S(1)} %get-tuple-element.16.norms, f32[8,128]{1,0:T(8,128)S(1)} %get-tuple-element.19.contrast, bf16[1024,2048]{1,0:T(8,128)(2,1)S(1)} %get-tuple-element.17.images), custom_call_target="tpu_custom_call" | custom-call | flops 2147483648 | bytes 4194304 | tf_op jit(solution)/shard_map/pallas_call | solution.py:265
  66.8 20.5 %all_to_all.44 = bf16[4,128,2048]{2,1,0:T(8,128)(2,1)S(1)} all-to-all(bf16[4,128,2048]{2,1,0:T(8,128)(2,1)S(1)} %bitcast.7), channel_id=1, replica_groups={{0,16,128,144},{32,48,160,176},{64,80,192,208},{96,112,224,240},{256,27..., dimensions={0} | all-to-all | bytes 4194304 | tf_op jit(solution)/shard_map/all_to_all | solution.py:38
  87.3 0.4 reduce_sum.39
  87.8 22.9 %all_to_all.45 = bf16[8,16,2048]{2,1,0:T(8,128)(2,1)S(1)} all-to-all(bf16[8,16,2048]{2,1,0:T(8,128)(2,1)S(1)} %bitcast.16), channel_id=1, replica_groups={{0,320,32,352,64,256,96,288},{16,336,48,368,80,272,112,304},{128,448,16..., dimensions={0} | all-to-all | bytes 1048576 | tf_op jit(solution)/shard_map/all_to_all | solution.py:38
  111.0 17.6 %all_to_all.46 = bf16[8,16,2048]{2,1,0:T(8,128)(2,1)S(1)} all-to-all(bf16[8,16,2048]{2,1,0:T(8,128)(2,1)S(1)} %broadcast_in_dim.2), channel_id=1, replica_groups={{0,320,32,352,64,256,96,288},{16,336,48,368,80,272,112,304},{128,448,16..., dimensions={0} | all-to-all | bytes 1048576 | tf_op jit(solution)/shard_map/all_to_all | solution.py:38
  128.7 8.2 %collective-permute-start.2 = (bf16[128,2048]{1,0:T(8,128)(2,1)S(1)}, bf16[128,2048]{1,0:T(8,128)(2,1)S(1)}, u32[]{:S(2)}, u32[]{:S(2)}) collective-permute-start(bf16[128,2048]{1,0:T(8,128)(2,1)S(1)} %bitcast.8), channel_id=1, source_target_pairs={{0,128},{16,144},{32,160},{48,176},{64,192},{80,208},{96,224},{112... | collective-permute-start | bytes 1572872 | tf_op jit(solution)/shard_map/ppermute | solution.py:331
  136.9 1.9 %collective-permute-start.1 = (bf16[128,2048]{1,0:T(8,128)(2,1)S(1)}, bf16[128,2048]{1,0:T(8,128)(2,1)S(1)}, u32[]{:S(2)}, u32[]{:S(2)}) collective-permute-start(bf16[128,2048]{1,0:T(8,128)(2,1)S(1)} %bitcast.9), channel_id=1, source_target_pairs={{0,16},{16,0},{32,48},{48,32},{64,80},{80,64},{96,112},{112,96},{1... | collective-permute-start | bytes 1572872 | tf_op jit(solution)/shard_map/ppermute | solution.py:331
  138.8 4.5 %collective-permute-start = (bf16[128,2048]{1,0:T(8,128)(2,1)S(1)}, bf16[128,2048]{1,0:T(8,128)(2,1)S(1)}, u32[]{:S(2)}, u32[]{:S(2)}) collective-permute-start(bf16[128,2048]{1,0:T(8,128)(2,1)S(1)} %bitcast.10), channel_id=1, source_target_pairs={{0,144},{16,128},{32,176},{48,160},{64,208},{80,192},{96,240},{112... | collective-permute-start | bytes 1572872 | tf_op jit(solution)/shard_map/ppermute | solution.py:331
  143.3 2.2 %copy-done.1 = bf16[1024,2048]{1,0:T(8,128)(2,1)S(1)} copy-done((bf16[1024,2048]{1,0:T(8,128)(2,1)S(1)}, bf16[1024,2048]{1,0:T(8,128)(2,1)}, u32[]{:S(2)}) %copy-start.1) | copy-done | bytes 4194328
  145.5 1.6 shard_map.63.before
  147.1 1.1 collective-permute-done.1.first
  148.2 4.0 %shard_map.64 = (f32[8,128]{1,0:T(8,128)S(1)}, bf16[512,2048]{1,0:T(8,128)(2,1)}) custom-call(bf16[128,2048]{1,0:T(8,128)(2,1)S(1)} %bitcast.12, bf16[128,2048]{1,0:T(8,128)(2,1)S(1)} %collective-permute-done.1.first, bf16[128,2048]{1,0:T(8,128)(2,1)S(1)} %collective-permute-done.2.second, bf16[1024,2048]{1,0:T(8,128)(2,1)S(1)} %copy-done.1, ...), custom_call_target="tpu_custom_call" | custom-call | flops 1073741824 | bytes 4194304 | tf_op jit(solution)/shard_map/pallas_call | solution.py:265
  152.1 1.2 collective-permute-done.last
  153.4 2.2 %shard_map.65 = (f32[16,8,128]{2,1,0:T(8,128)S(1)}, bf16[512,2048]{1,0:T(8,128)(2,1)}) custom-call(bf16[128,2048]{1,0:T(8,128)(2,1)S(1)} %collective-permute-done.last, bf16[1024,2048]{1,0:T(8,128)(2,1)S(1)} %copy-done.1, f32[8,128]{1,0:T(8,128)S(1)} %get-tuple-element.19.contrast, ...), custom_call_target="tpu_custom_call", output_to_operand_aliasing={{1}: (4, {})} | custom-call | flops 536870912 | bytes 4194304 | tf_op jit(solution)/shard_map/pallas_call | solution.py:265
  155.5 10.3 %all_to_all.47 = f32[16,8,128]{2,1,0:T(8,128)S(1)} all-to-all(f32[16,8,128]{2,1,0:T(8,128)S(1)} %get-tuple-element.24), channel_id=1, replica_groups=mesh['img'=32,'ref'=16] {'ref'}, dimensions={0} | all-to-all | bytes 131072 | tf_op jit(solution)/shard_map/all_to_all | solution.py:38
  165.9 0.6 add_bitcast_fusion
  (13 shorter events, 0.4 us)
Async XLA Ops:
  0.6 27.4 %copy-start.2 = (f32[1024]{0:T(1024)S(1)}, f32[1024]{0:T(1024)}, u32[]{:S(2)}) copy-start(f32[1024]{0:T(1024)} %param.5) | copy-start | bytes 12292
  7.2 57.2 %copy-start = (bf16[1024,2048]{1,0:T(8,128)(2,1)}, bf16[1024,2048]{1,0:T(8,128)(2,1)S(1)}, u32[]{:S(2)}) copy-start(bf16[1024,2048]{1,0:T(8,128)(2,1)S(1)} %get-tuple-element.17.images) | copy-start | bytes 12582916
  128.7 18.5 %collective-permute-start.2 = (bf16[128,2048]{1,0:T(8,128)(2,1)S(1)}, bf16[128,2048]{1,0:T(8,128)(2,1)S(1)}, u32[]{:S(2)}, u32[]{:S(2)}) collective-permute-start(bf16[128,2048]{1,0:T(8,128)(2,1)S(1)} %bitcast.8), channel_id=1, source_target_pairs={{0,128},{16,144},{32,160},{48,176},{64,192},{80,208},{96,224},{112... | collective-permute-start | bytes 1572872 | tf_op jit(solution)/shard_map/ppermute | solution.py:331
  136.9 11.3 %collective-permute-start.1 = (bf16[128,2048]{1,0:T(8,128)(2,1)S(1)}, bf16[128,2048]{1,0:T(8,128)(2,1)S(1)}, u32[]{:S(2)}, u32[]{:S(2)}) collective-permute-start(bf16[128,2048]{1,0:T(8,128)(2,1)S(1)} %bitcast.9), channel_id=1, source_target_pairs={{0,16},{16,0},{32,48},{48,32},{64,80},{80,64},{96,112},{112,96},{1... | collective-permute-start | bytes 1572872 | tf_op jit(solution)/shard_map/ppermute | solution.py:331
  138.8 14.6 %collective-permute-start = (bf16[128,2048]{1,0:T(8,128)(2,1)S(1)}, bf16[128,2048]{1,0:T(8,128)(2,1)S(1)}, u32[]{:S(2)}, u32[]{:S(2)}) collective-permute-start(bf16[128,2048]{1,0:T(8,128)(2,1)S(1)} %bitcast.10), channel_id=1, source_target_pairs={{0,144},{16,128},{32,176},{48,160},{64,208},{80,192},{96,240},{112... | collective-permute-start | bytes 1572872 | tf_op jit(solution)/shard_map/ppermute | solution.py:331
  143.3 2.2 %copy-start.1 = (bf16[1024,2048]{1,0:T(8,128)(2,1)S(1)}, bf16[1024,2048]{1,0:T(8,128)(2,1)}, u32[]{:S(2)}) copy-start(bf16[1024,2048]{1,0:T(8,128)(2,1)} %copy-done) | copy-start | bytes 12582916
